TPU v7x, 256 devices: a whole 4x4x8 slice. The times are simulated.
256 devices in a mesh: outer: 8 (over z_hi, x), inner: 32 (over z_lo, y, core).
Axes of the slice: x: 4, y: 4, z: 8 (z_hi: 2, z_lo: 4; z = z_hi * 4 + z_lo), core: 2. Of those that a mesh axis runs over, the one named last changes fastest.
Arguments:
- points: bfloat16 [16, 1048576], P(None, ('outer', 'inner')), may hold values from -3 to 3
- charges: bfloat16 [64, 1048576], P(None, ('outer', 'inner')), may hold values from -6 to 6
- near_leaves: int32 [4096, 16], P(('outer', 'inner')), may hold values from 0 to 4095, as said below
- skel_device: int32 [256, 512], P(('outer', 'inner')), may hold values from 0 to 4095, as said below
- skel_tree: int32 [256, 7, 512], P(('outer', 'inner')), may hold values from 0 to 1023, as said below
Outputs:
- potential: float32 [64, 1048576], P(None, ('outer', 'inner'))
Inputs may be any that keep to these rules, and one draw needn't show every extreme that they name: `near_leaves`: row b holds 16 different leaf numbers, b among them, each a leaf of b's level-0 node or of the level-0 nodes just before and just after it. `skel_device`: row c holds 512 different offsets among the 4096 points of level-0 node c. skel_tree[c, k] holds 512 different positions among the 1024 skeleton points of the children of the level-(k+1) node that contains level-0 node c; all level-0 nodes inside one level-(k+1) node have equal rows k.
All inputs are finite; a program needn't handle non-finite values.
Results may differ from a plain program's by a relative error of at most 0.0035.
Values may be sent and summed in bfloat16 or wider, within the bound.
No kernel may reach another device: no remote copies, remote signals or barrier semaphores. Data moves between devices by JAX's collectives and lax.ppermute only.
A program may use at most 64 MiB of HBM per device.

v0:
```python
import jax
import jax.numpy as jnp
from jax import lax
from jax.sharding import PartitionSpec as P

DIM = 16
NRHS = 64


GAMMA = 0.125


def partner(block, axis, stride):
    count = lax.axis_size(axis)
    route = []
    for low in range(count):
        high = low | 1 << stride
        if high != low and high < count:
            route += [(low, high), (high, low)]
    return lax.ppermute(block, axis, route)


def extended_2(array, sides, width):
    for axis, dim in sides:
        peers, length = (lax.axis_size(axis), array.shape[dim])
        up = [(i, (i + 1) % peers) for i in range(peers - 1)]
        down = [(j, i) for i, j in up]
        last = lax.slice_in_dim(array, length - width, length, axis=dim)
        leading = lax.slice_in_dim(array, 0, width, axis=dim)
        before = lax.ppermute(last, axis, up)
        after = lax.ppermute(leading, axis, down)
        array = jnp.concatenate([before, array, after], axis=dim)
    return array


def kernel_block(left, right):
    left32 = left.astype(jnp.float32)
    right32 = right.astype(jnp.float32)
    products = jnp.einsum("dm,dn->mn", left, right, preferred_element_type=jnp.float32)
    distance = (
        jnp.sum(left32 * left32, 0)[:, None]
        + jnp.sum(right32 * right32, 0)[None, :]
        - 2.0 * products
    )
    return jnp.exp(-GAMMA * distance).astype(jnp.bfloat16)


def spread_weights(weights, block):
    totals = jnp.sum(block.astype(jnp.float32), 1)
    return (weights.astype(jnp.float32) / totals[None, :]).astype(jnp.bfloat16)


def carry_values(values, block):
    totals = jnp.sum(block.astype(jnp.float32), 0)
    return jnp.dot(values, block, preferred_element_type=jnp.float32) / totals[None, :]


def parent_node(joined, chosen):
    joined_x = joined[:DIM]
    parent_x = jnp.take(joined_x, chosen, axis=1)
    block = kernel_block(joined_x, parent_x)
    parent_up = jnp.dot(
        spread_weights(joined[DIM:], block), block, preferred_element_type=jnp.float32
    ).astype(jnp.bfloat16)
    return jnp.concatenate([parent_x, parent_up], 0)


def downward_top(sibling, own_x):
    return jnp.dot(
        sibling[DIM:], kernel_block(sibling[:DIM], own_x), preferred_element_type=jnp.float32
    ).astype(jnp.bfloat16)


def downward_node(sibling, parent_x, parent_down, own_x):
    beside = jnp.dot(
        sibling[DIM:], kernel_block(sibling[:DIM], own_x), preferred_element_type=jnp.float32
    )
    above = carry_values(parent_down, kernel_block(parent_x, own_x))
    return (beside + above).astype(jnp.bfloat16)


def near_block(leaves, targets_x, leaf_ids):
    target32 = targets_x.astype(jnp.float32)
    target_norm = jnp.sum(target32 * target32, 1)

    def one_turn(turn, summed):
        source = jnp.take(leaves, leaf_ids[:, turn], axis=0)
        source_x = source[:, :DIM]
        source32 = source_x.astype(jnp.float32)
        products = jnp.einsum(
            "bdt,bds->bts", targets_x, source_x, preferred_element_type=jnp.float32
        )
        distance = (
            target_norm[:, :, None] + jnp.sum(source32 * source32, 1)[:, None, :] - 2.0 * products
        )
        weights = jnp.exp(-GAMMA * distance).astype(jnp.bfloat16)
        return summed + jnp.einsum(
            "bts,brs->rbt", weights, source[:, DIM:], preferred_element_type=jnp.float32
        )

    start = jnp.zeros((NRHS, targets_x.shape[0], targets_x.shape[2]), jnp.float32)
    return lax.fori_loop(0, leaf_ids.shape[1], one_turn, start)


def swap_inner(node_data, bit_index):
    return partner(node_data, "inner", bit_index)


def swap_outer(node_data, bit_index):
    return partner(node_data, "outer", bit_index)


def climb_swap(node_data, skel_rows, records, parents, first, number, exchange, position, levels):
    for offset in range(number):
        height = first + offset
        sibling = exchange(node_data, offset)
        records.append((node_data[:DIM], sibling))
        if height < levels - 1:
            is_right = position >> offset & 1 == 1
            joined = jnp.where(
                is_right,
                jnp.concatenate([sibling, node_data], 1),
                jnp.concatenate([node_data, sibling], 1),
            )
            node_data = parent_node(joined, skel_rows[height])
            parents.append(node_data[:DIM])
    return node_data


def body(points, charges, near_leaves, skel_device, skel_tree):
    inner_levels = lax.axis_size("inner").bit_length() - 1
    outer_levels = lax.axis_size("outer").bit_length() - 1
    levels = inner_levels + outer_levels
    position = lax.axis_index(("outer", "inner"))
    dev_points = points.shape[1]
    leaf_dev = near_leaves.shape[0]
    leaf_size = dev_points // leaf_dev
    stacked = jnp.concatenate([points, charges], 0)
    extended = extended_2(stacked, ((("outer", "inner"), 1),), dev_points)
    base_x = jnp.take(points, skel_device[0], axis=1)
    base_block = kernel_block(points, base_x)
    base_up = jnp.dot(
        spread_weights(charges, base_block), base_block, preferred_element_type=jnp.float32
    ).astype(jnp.bfloat16)
    node_data = jnp.concatenate([base_x, base_up], 0)
    skel_rows = skel_tree[0]
    records = []
    parents = []
    node_data = climb_swap(
        node_data,
        skel_rows,
        records,
        parents,
        0,
        inner_levels,
        swap_inner,
        lax.axis_index("inner"),
        levels,
    )
    node_data = climb_swap(
        node_data,
        skel_rows,
        records,
        parents,
        inner_levels,
        outer_levels,
        swap_outer,
        lax.axis_index("outer"),
        levels,
    )
    downward = None
    for height in range(levels - 1, -1, -1):
        own_x, sibling = records[height]
        if height == levels - 1:
            downward = downward_top(sibling, own_x)
        else:
            downward = downward_node(sibling, parents[height], downward, own_x)
    far_part = carry_values(downward, kernel_block(base_x, points))
    leaves = extended.reshape(DIM + NRHS, 3 * leaf_dev, leaf_size).transpose(1, 0, 2)
    targets_x = points.reshape(DIM, leaf_dev, leaf_size).transpose(1, 0, 2)
    leaf_ids = near_leaves - (position - 1) * leaf_dev
    near_part = near_block(leaves, targets_x, leaf_ids)
    return near_part.reshape(NRHS, dev_points) + far_part


def solution(mesh):
    return jax.shard_map(
        body,
        mesh=mesh,
        in_specs=(
            P(None, ("outer", "inner")),
            P(None, ("outer", "inner")),
            P(("outer", "inner"), None),
            P(("outer", "inner"), None),
            P(("outer", "inner"), None, None),
        ),
        out_specs=P(None, ("outer", "inner")),
        check_vma=False,
    )
```

profile of v0, /device:TPU:2, one launch (start us, length us, event | category | flops | bytes accessed | tf_op | source)
XLA Modules:
  0.0 195.0 jit_solution(1449796217870734448)
XLA Ops:
  2.1 8.4 %collective-permute-start.1 = (bf16[80,4096]{1,0:T(8,128)(2,1)S(1)}, bf16[80,4096]{1,0:T(8,128)(2,1)S(1)}, u32[]{:S(2)}, u32[]{:S(2)}) collective-permute-start(bf16[80,4096]{1,0:T(8,128)(2,1)S(1)} %constant_dynamic-update-slice_fusion), channel_id=1, source_target_pairs={{1,0},{2,1},{3,2},{4,3},{5,4},{6,5},{7,6},{8,7},{9,8},{10,9},{11,1... | collective-permute-start | bytes 1966088 | tf_op jit(solution)/shard_map/ppermute | solution.py:31
  15.4 4.6 %convert_reduce_fusion.1 = (f32[4096]{0:T(1024)S(1)}, bf16[4096,512]{0,1:T(8,128)(2,1)S(1)}, f32[512,4096]{1,0:T(8,128)}) fusion(f32[512]{0:T(512)S(1)} %get-tuple-element.175, f32[4096]{0:T(1024)S(1)} %multiply_reduce_fusion.1, bf16[16,4096]{1,0:T(8,128)(2,1)S(1)} %copy-done, bf16[512,16]{0,1:T(8,128)(2,1)S(1)} %copy.29, ...), kind=kOutput, calls=%fused_computation.31 | convolution fusion | flops 81793024 | bytes 12765696 | tf_op jit(solution)/shard_map/dm,dn->mn/dot_general | solution.py:39
  21.9 5.9 %convert_reduce_fusion = (f32[4096]{0:T(1024)S(1)}, bf16[512,4096]{1,0:T(8,128)(2,1)}) fusion(f32[512,4096]{1,0:T(8,128)} %get-tuple-element.184, f32[4096]{0:T(1024)S(1)} %multiply_reduce_fusion.1, f32[512]{0:T(512)S(1)} %get-tuple-element.175), kind=kLoop, calls=%fused_computation.29 | loop fusion | flops 14675968 | bytes 12617728 | tf_op jit(solution)/shard_map/reduce_sum | solution.py:54
  32.7 4.8 %collective-permute-done.3 = bf16[80,512]{1,0:T(8,128)(2,1)S(1)} collective-permute-done((bf16[80,512]{1,0:T(8,128)(2,1)S(1)}, bf16[80,512]{1,0:T(8,128)(2,1)S(1)}, u32[]{:S(2)}, u32[]{:S(2)}) %collective-permute-start.3) | collective-permute-done | bytes 81952 | tf_op jit(solution)/shard_map/ppermute | solution.py:20
  42.6 5.9 %collective-permute-done.4 = bf16[80,512]{1,0:T(8,128)(2,1)S(1)} collective-permute-done((bf16[80,512]{1,0:T(8,128)(2,1)S(1)}, bf16[80,512]{1,0:T(8,128)(2,1)S(1)}, u32[]{:S(2)}, u32[]{:S(2)}) %collective-permute-start.4) | collective-permute-done | bytes 81952 | tf_op jit(solution)/shard_map/ppermute | solution.py:20
  53.4 4.4 %collective-permute-done.5 = bf16[80,512]{1,0:T(8,128)(2,1)S(1)} collective-permute-done((bf16[80,512]{1,0:T(8,128)(2,1)S(1)}, bf16[80,512]{1,0:T(8,128)(2,1)S(1)}, u32[]{:S(2)}, u32[]{:S(2)}) %collective-permute-start.5) | collective-permute-done | bytes 81952 | tf_op jit(solution)/shard_map/ppermute | solution.py:20
  64.5 4.4 %collective-permute-done.6 = bf16[80,512]{1,0:T(8,128)(2,1)S(1)} collective-permute-done((bf16[80,512]{1,0:T(8,128)(2,1)S(1)}, bf16[80,512]{1,0:T(8,128)(2,1)S(1)}, u32[]{:S(2)}, u32[]{:S(2)}) %collective-permute-start.6) | collective-permute-done | bytes 81952 | tf_op jit(solution)/shard_map/ppermute | solution.py:20
  73.7 4.4 %collective-permute-done.7 = bf16[80,512]{1,0:T(8,128)(2,1)S(1)} collective-permute-done((bf16[80,512]{1,0:T(8,128)(2,1)S(1)}, bf16[80,512]{1,0:T(8,128)(2,1)S(1)}, u32[]{:S(2)}, u32[]{:S(2)}) %collective-permute-start.7) | collective-permute-done | bytes 81952 | tf_op jit(solution)/shard_map/ppermute | solution.py:20
  92.5 4.8 %collective-permute-start.9 = (bf16[80,512]{1,0:T(8,128)(2,1)S(1)}, bf16[80,512]{1,0:T(8,128)(2,1)S(1)}, u32[]{:S(2)}, u32[]{:S(2)}) collective-permute-start(bf16[80,512]{1,0:T(8,128)(2,1)S(1)} %pad_maximum_fusion.8), channel_id=1, source_target_pairs={{0,128},{128,0},{32,160},{160,32},{64,192},{192,64},{96,224},{224,... | collective-permute-start | bytes 245768 | tf_op jit(solution)/shard_map/ppermute | solution.py:20
  115.9 73.7 %while.14 = (s32[]{:T(128)}, f32[64,16,256]{2,0,1:T(8,128)}, s32[16,16]{0,1:T(8,128)S(1)}, bf16[48,80,256]{2,1,0:T(8,128)(2,1)S(1)}, f32[16,256]{1,0:T(8,128)S(1...) while((s32[]{:T(128)}, f32[64,16,256]{2,0,1:T(8,128)}, s32[16,16]{0,1:T(8,128)S(1)}, ...), condition=%wide.region_3.4_spmd.clone, body=%wide.region_1.3_spmd.clone.sunk | while | flops 174060640 | bytes 5689739 | solution.py:102
  120.2 3.9 %fusion.273 = f32[64,16,256]{2,0,1:T(8,128)} fusion(bf16[16,16,256]{2,1,0:T(8,128)(2,1)S(1)} %get-tuple-element.283, f32[16,256]{1,0:T(8,128)S(1)} %multiply_reduce_fusion.27, f32[16,256]{1,0:T(8,128)S(1)} %get-tuple-element.282, f32[64,16,256]{2,0,1:T(8,128)} %get-tuple-element.271, bf16[16,80,256]{2,1,0:T(8,128)(2,1)S(1)} %broadcast_select_fusion.7, ...), kind=kOutput, calls=%fused_computation.15.clone.1 | convolution fusion | flops 173539328 | bytes 2916353 | tf_op jit(solution)/shard_map/while/body/eval_jaxpr/bts,brs->rbt/dot_general | solution.py:97
  124.9 3.9 %fusion.273 = f32[64,16,256]{2,0,1:T(8,128)} fusion(bf16[16,16,256]{2,1,0:T(8,128)(2,1)S(1)} %get-tuple-element.283, f32[16,256]{1,0:T(8,128)S(1)} %multiply_reduce_fusion.27, f32[16,256]{1,0:T(8,128)S(1)} %get-tuple-element.282, f32[64,16,256]{2,0,1:T(8,128)} %get-tuple-element.271, bf16[16,80,256]{2,1,0:T(8,128)(2,1)S(1)} %broadcast_select_fusion.7, ...), kind=kOutput, calls=%fused_computation.15.clone.1 | convolution fusion | flops 173539328 | bytes 2916353 | tf_op jit(solution)/shard_map/while/body/eval_jaxpr/bts,brs->rbt/dot_general | solution.py:97
  129.6 3.9 %fusion.273 = f32[64,16,256]{2,0,1:T(8,128)} fusion(bf16[16,16,256]{2,1,0:T(8,128)(2,1)S(1)} %get-tuple-element.283, f32[16,256]{1,0:T(8,128)S(1)} %multiply_reduce_fusion.27, f32[16,256]{1,0:T(8,128)S(1)} %get-tuple-element.282, f32[64,16,256]{2,0,1:T(8,128)} %get-tuple-element.271, bf16[16,80,256]{2,1,0:T(8,128)(2,1)S(1)} %broadcast_select_fusion.7, ...), kind=kOutput, calls=%fused_computation.15.clone.1 | convolution fusion | flops 173539328 | bytes 2916353 | tf_op jit(solution)/shard_map/while/body/eval_jaxpr/bts,brs->rbt/dot_general | solution.py:97
  134.2 3.9 %fusion.273 = f32[64,16,256]{2,0,1:T(8,128)} fusion(bf16[16,16,256]{2,1,0:T(8,128)(2,1)S(1)} %get-tuple-element.283, f32[16,256]{1,0:T(8,128)S(1)} %multiply_reduce_fusion.27, f32[16,256]{1,0:T(8,128)S(1)} %get-tuple-element.282, f32[64,16,256]{2,0,1:T(8,128)} %get-tuple-element.271, bf16[16,80,256]{2,1,0:T(8,128)(2,1)S(1)} %broadcast_select_fusion.7, ...), kind=kOutput, calls=%fused_computation.15.clone.1 | convolution fusion | flops 173539328 | bytes 2916353 | tf_op jit(solution)/shard_map/while/body/eval_jaxpr/bts,brs->rbt/dot_general | solution.py:97
  138.9 3.9 %fusion.273 = f32[64,16,256]{2,0,1:T(8,128)} fusion(bf16[16,16,256]{2,1,0:T(8,128)(2,1)S(1)} %get-tuple-element.283, f32[16,256]{1,0:T(8,128)S(1)} %multiply_reduce_fusion.27, f32[16,256]{1,0:T(8,128)S(1)} %get-tuple-element.282, f32[64,16,256]{2,0,1:T(8,128)} %get-tuple-element.271, bf16[16,80,256]{2,1,0:T(8,128)(2,1)S(1)} %broadcast_select_fusion.7, ...), kind=kOutput, calls=%fused_computation.15.clone.1 | convolution fusion | flops 173539328 | bytes 2916353 | tf_op jit(solution)/shard_map/while/body/eval_jaxpr/bts,brs->rbt/dot_general | solution.py:97
  143.6 3.9 %fusion.273 = f32[64,16,256]{2,0,1:T(8,128)} fusion(bf16[16,16,256]{2,1,0:T(8,128)(2,1)S(1)} %get-tuple-element.283, f32[16,256]{1,0:T(8,128)S(1)} %multiply_reduce_fusion.27, f32[16,256]{1,0:T(8,128)S(1)} %get-tuple-element.282, f32[64,16,256]{2,0,1:T(8,128)} %get-tuple-element.271, bf16[16,80,256]{2,1,0:T(8,128)(2,1)S(1)} %broadcast_select_fusion.7, ...), kind=kOutput, calls=%fused_computation.15.clone.1 | convolution fusion | flops 173539328 | bytes 2916353 | tf_op jit(solution)/shard_map/while/body/eval_jaxpr/bts,brs->rbt/dot_general | solution.py:97
  148.3 3.9 %fusion.273 = f32[64,16,256]{2,0,1:T(8,128)} fusion(bf16[16,16,256]{2,1,0:T(8,128)(2,1)S(1)} %get-tuple-element.283, f32[16,256]{1,0:T(8,128)S(1)} %multiply_reduce_fusion.27, f32[16,256]{1,0:T(8,128)S(1)} %get-tuple-element.282, f32[64,16,256]{2,0,1:T(8,128)} %get-tuple-element.271, bf16[16,80,256]{2,1,0:T(8,128)(2,1)S(1)} %broadcast_select_fusion.7, ...), kind=kOutput, calls=%fused_computation.15.clone.1 | convolution fusion | flops 173539328 | bytes 2916353 | tf_op jit(solution)/shard_map/while/body/eval_jaxpr/bts,brs->rbt/dot_general | solution.py:97
  153.0 3.9 %fusion.273 = f32[64,16,256]{2,0,1:T(8,128)} fusion(bf16[16,16,256]{2,1,0:T(8,128)(2,1)S(1)} %get-tuple-element.283, f32[16,256]{1,0:T(8,128)S(1)} %multiply_reduce_fusion.27, f32[16,256]{1,0:T(8,128)S(1)} %get-tuple-element.282, f32[64,16,256]{2,0,1:T(8,128)} %get-tuple-element.271, bf16[16,80,256]{2,1,0:T(8,128)(2,1)S(1)} %broadcast_select_fusion.7, ...), kind=kOutput, calls=%fused_computation.15.clone.1 | convolution fusion | flops 173539328 | bytes 2916353 | tf_op jit(solution)/shard_map/while/body/eval_jaxpr/bts,brs->rbt/dot_general | solution.py:97
  157.6 3.9 %fusion.273 = f32[64,16,256]{2,0,1:T(8,128)} fusion(bf16[16,16,256]{2,1,0:T(8,128)(2,1)S(1)} %get-tuple-element.283, f32[16,256]{1,0:T(8,128)S(1)} %multiply_reduce_fusion.27, f32[16,256]{1,0:T(8,128)S(1)} %get-tuple-element.282, f32[64,16,256]{2,0,1:T(8,128)} %get-tuple-element.271, bf16[16,80,256]{2,1,0:T(8,128)(2,1)S(1)} %broadcast_select_fusion.7, ...), kind=kOutput, calls=%fused_computation.15.clone.1 | convolution fusion | flops 173539328 | bytes 2916353 | tf_op jit(solution)/shard_map/while/body/eval_jaxpr/bts,brs->rbt/dot_general | solution.py:97
  162.3 3.9 %fusion.273 = f32[64,16,256]{2,0,1:T(8,128)} fusion(bf16[16,16,256]{2,1,0:T(8,128)(2,1)S(1)} %get-tuple-element.283, f32[16,256]{1,0:T(8,128)S(1)} %multiply_reduce_fusion.27, f32[16,256]{1,0:T(8,128)S(1)} %get-tuple-element.282, f32[64,16,256]{2,0,1:T(8,128)} %get-tuple-element.271, bf16[16,80,256]{2,1,0:T(8,128)(2,1)S(1)} %broadcast_select_fusion.7, ...), kind=kOutput, calls=%fused_computation.15.clone.1 | convolution fusion | flops 173539328 | bytes 2916353 | tf_op jit(solution)/shard_map/while/body/eval_jaxpr/bts,brs->rbt/dot_general | solution.py:97
  167.0 3.9 %fusion.273 = f32[64,16,256]{2,0,1:T(8,128)} fusion(bf16[16,16,256]{2,1,0:T(8,128)(2,1)S(1)} %get-tuple-element.283, f32[16,256]{1,0:T(8,128)S(1)} %multiply_reduce_fusion.27, f32[16,256]{1,0:T(8,128)S(1)} %get-tuple-element.282, f32[64,16,256]{2,0,1:T(8,128)} %get-tuple-element.271, bf16[16,80,256]{2,1,0:T(8,128)(2,1)S(1)} %broadcast_select_fusion.7, ...), kind=kOutput, calls=%fused_computation.15.clone.1 | convolution fusion | flops 173539328 | bytes 2916353 | tf_op jit(solution)/shard_map/while/body/eval_jaxpr/bts,brs->rbt/dot_general | solution.py:97
  171.7 3.9 %fusion.273 = f32[64,16,256]{2,0,1:T(8,128)} fusion(bf16[16,16,256]{2,1,0:T(8,128)(2,1)S(1)} %get-tuple-element.283, f32[16,256]{1,0:T(8,128)S(1)} %multiply_reduce_fusion.27, f32[16,256]{1,0:T(8,128)S(1)} %get-tuple-element.282, f32[64,16,256]{2,0,1:T(8,128)} %get-tuple-element.271, bf16[16,80,256]{2,1,0:T(8,128)(2,1)S(1)} %broadcast_select_fusion.7, ...), kind=kOutput, calls=%fused_computation.15.clone.1 | convolution fusion | flops 173539328 | bytes 2916353 | tf_op jit(solution)/shard_map/while/body/eval_jaxpr/bts,brs->rbt/dot_general | solution.py:97
  176.4 3.9 %fusion.273 = f32[64,16,256]{2,0,1:T(8,128)} fusion(bf16[16,16,256]{2,1,0:T(8,128)(2,1)S(1)} %get-tuple-element.283, f32[16,256]{1,0:T(8,128)S(1)} %multiply_reduce_fusion.27, f32[16,256]{1,0:T(8,128)S(1)} %get-tuple-element.282, f32[64,16,256]{2,0,1:T(8,128)} %get-tuple-element.271, bf16[16,80,256]{2,1,0:T(8,128)(2,1)S(1)} %broadcast_select_fusion.7, ...), kind=kOutput, calls=%fused_computation.15.clone.1 | convolution fusion | flops 173539328 | bytes 2916353 | tf_op jit(solution)/shard_map/while/body/eval_jaxpr/bts,brs->rbt/dot_general | solution.py:97
  190.9 4.1 %fusion.14 = f32[64,4096]{1,0:T(8,128)} fusion(f32[64,4096]{1,0:T(8,128)S(1)} %bitcast.145, bf16[64,512]{1,0:T(8,128)(2,1)S(1)} %fusion.96, bf16[512,4096]{1,0:T(8,128)(2,1)} %get-tuple-element.158, f32[4096]{0:T(1024)S(1)} %get-tuple-element.157), kind=kOutput, calls=%fused_computation.33 | convolution fusion | flops 268959744 | bytes 6373376 | tf_op jit(solution)/shard_map/dot_general | solution.py:55
  (262 shorter events, 91.7 us)
Async XLA Ops:
  0.0 13.8 %copy-start = (bf16[16,4096]{1,0:T(8,128)(2,1)S(1)}, bf16[16,4096]{1,0:T(8,128)(2,1)}, u32[]{:S(2)}) copy-start(bf16[16,4096]{1,0:T(8,128)(2,1)} %param.9) | copy-start | bytes 393220
  0.0 13.9 %copy-start.2 = (s32[1,7,512]{2,0,1:T(1,128)S(1)}, s32[1,7,512]{2,0,1:T(1,128)}, u32[]{:S(2)}) copy-start(s32[1,7,512]{2,0,1:T(1,128)} %param.13) | copy-start | bytes 43012
  0.0 13.9 %copy-start.3 = (s32[1,512]{1,0:T(1,128)S(1)}, s32[1,512]{1,0:T(1,128)}, u32[]{:S(2)}) copy-start(s32[1,512]{1,0:T(1,128)} %param.12) | copy-start | bytes 6148
  2.1 112.6 %collective-permute-start.1 = (bf16[80,4096]{1,0:T(8,128)(2,1)S(1)}, bf16[80,4096]{1,0:T(8,128)(2,1)S(1)}, u32[]{:S(2)}, u32[]{:S(2)}) collective-permute-start(bf16[80,4096]{1,0:T(8,128)(2,1)S(1)} %constant_dynamic-update-slice_fusion), channel_id=1, source_target_pairs={{1,0},{2,1},{3,2},{4,3},{5,4},{6,5},{7,6},{8,7},{9,8},{10,9},{11,1... | collective-permute-start | bytes 1966088 | tf_op jit(solution)/shard_map/ppermute | solution.py:31
  10.5 104.2 %collective-permute-start = (bf16[80,4096]{1,0:T(8,128)(2,1)S(1)}, bf16[80,4096]{1,0:T(8,128)(2,1)S(1)}, u32[]{:S(2)}, u32[]{:S(2)}) collective-permute-start(bf16[80,4096]{1,0:T(8,128)(2,1)S(1)} %constant_dynamic-update-slice_fusion), channel_id=1, source_target_pairs={{0,1},{1,2},{2,3},{3,4},{4,5},{5,6},{6,7},{7,8},{8,9},{9,10},{10,1... | collective-permute-start | bytes 1966088 | tf_op jit(solution)/shard_map/ppermute | solution.py:30
  15.4 4.6 %copy-start.1 = (bf16[64,4096]{1,0:T(8,128)(2,1)S(1)}, bf16[64,4096]{1,0:T(8,128)(2,1)}, u32[]{:S(2)}) copy-start(bf16[64,4096]{1,0:T(8,128)(2,1)} %param.10) | copy-start | bytes 1572868
  20.0 1.7 copy-start.4
  21.4 6.4 %collective-permute-start.2 = (bf16[80,512]{1,0:T(8,128)(2,1)S(1)}, bf16[80,512]{1,0:T(8,128)(2,1)S(1)}, u32[]{:S(2)}, u32[]{:S(2)}) collective-permute-start(bf16[80,512]{1,0:T(8,128)(2,1)S(1)} %pad_maximum_fusion.1), channel_id=1, source_target_pairs={{0,1},{1,0},{2,3},{3,2},{4,5},{5,4},{6,7},{7,6},{8,9},{9,8},{10,11... | collective-permute-start | bytes 245768 | tf_op jit(solution)/shard_map/ppermute | solution.py:20
  32.6 4.9 %collective-permute-start.3 = (bf16[80,512]{1,0:T(8,128)(2,1)S(1)}, bf16[80,512]{1,0:T(8,128)(2,1)S(1)}, u32[]{:S(2)}, u32[]{:S(2)}) collective-permute-start(bf16[80,512]{1,0:T(8,128)(2,1)S(1)} %pad_maximum_fusion.2), channel_id=1, source_target_pairs={{0,2},{2,0},{1,3},{3,1},{4,6},{6,4},{5,7},{7,5},{8,10},{10,8},{9,1... | collective-permute-start | bytes 245768 | tf_op jit(solution)/shard_map/ppermute | solution.py:20
  42.3 6.2 %collective-permute-start.4 = (bf16[80,512]{1,0:T(8,128)(2,1)S(1)}, bf16[80,512]{1,0:T(8,128)(2,1)S(1)}, u32[]{:S(2)}, u32[]{:S(2)}) collective-permute-start(bf16[80,512]{1,0:T(8,128)(2,1)S(1)} %pad_maximum_fusion.3), channel_id=1, source_target_pairs={{0,4},{4,0},{1,5},{5,1},{2,6},{6,2},{3,7},{7,3},{8,12},{12,8},{9,1... | collective-permute-start | bytes 245768 | tf_op jit(solution)/shard_map/ppermute | solution.py:20
  53.3 4.5 %collective-permute-start.5 = (bf16[80,512]{1,0:T(8,128)(2,1)S(1)}, bf16[80,512]{1,0:T(8,128)(2,1)S(1)}, u32[]{:S(2)}, u32[]{:S(2)}) collective-permute-start(bf16[80,512]{1,0:T(8,128)(2,1)S(1)} %pad_maximum_fusion.4), channel_id=1, source_target_pairs={{0,8},{8,0},{1,9},{9,1},{2,10},{10,2},{3,11},{11,3},{4,12},{12,4},... | collective-permute-start | bytes 245768 | tf_op jit(solution)/shard_map/ppermute | solution.py:20
  62.6 6.3 %collective-permute-start.6 = (bf16[80,512]{1,0:T(8,128)(2,1)S(1)}, bf16[80,512]{1,0:T(8,128)(2,1)S(1)}, u32[]{:S(2)}, u32[]{:S(2)}) collective-permute-start(bf16[80,512]{1,0:T(8,128)(2,1)S(1)} %pad_maximum_fusion.5), channel_id=1, source_target_pairs={{0,16},{16,0},{1,17},{17,1},{2,18},{18,2},{3,19},{19,3},{4,20},{20... | collective-permute-start | bytes 245768 | tf_op jit(solution)/shard_map/ppermute | solution.py:20
  73.6 4.5 %collective-permute-start.7 = (bf16[80,512]{1,0:T(8,128)(2,1)S(1)}, bf16[80,512]{1,0:T(8,128)(2,1)S(1)}, u32[]{:S(2)}, u32[]{:S(2)}) collective-permute-start(bf16[80,512]{1,0:T(8,128)(2,1)S(1)} %pad_maximum_fusion.6), channel_id=1, source_target_pairs={{0,32},{32,0},{64,96},{96,64},{128,160},{160,128},{192,224},{224,1... | collective-permute-start | bytes 245768 | tf_op jit(solution)/shard_map/ppermute | solution.py:20
  82.3 6.0 %collective-permute-start.8 = (bf16[80,512]{1,0:T(8,128)(2,1)S(1)}, bf16[80,512]{1,0:T(8,128)(2,1)S(1)}, u32[]{:S(2)}, u32[]{:S(2)}) collective-permute-start(bf16[80,512]{1,0:T(8,128)(2,1)S(1)} %pad_maximum_fusion.7), channel_id=1, source_target_pairs={{0,64},{64,0},{32,96},{96,32},{128,192},{192,128},{160,224},{224,1... | collective-permute-start | bytes 245768 | tf_op jit(solution)/shard_map/ppermute | solution.py:20
  92.5 8.7 %collective-permute-start.9 = (bf16[80,512]{1,0:T(8,128)(2,1)S(1)}, bf16[80,512]{1,0:T(8,128)(2,1)S(1)}, u32[]{:S(2)}, u32[]{:S(2)}) collective-permute-start(bf16[80,512]{1,0:T(8,128)(2,1)S(1)} %pad_maximum_fusion.8), channel_id=1, source_target_pairs={{0,128},{128,0},{32,160},{160,32},{64,192},{192,64},{96,224},{224,... | collective-permute-start | bytes 245768 | tf_op jit(solution)/shard_map/ppermute | solution.py:20
  103.6 4.9 %copy-start.7 = (bf16[512,512]{1,0:T(8,128)(2,1)S(1)}, bf16[512,512]{1,0:T(8,128)(2,1)}, u32[]{:S(2)}) copy-start(bf16[512,512]{1,0:T(8,128)(2,1)} %get-tuple-element.204) | copy-start | bytes 1572868
  103.6 4.9 %copy-start.12 = (f32[512]{0:T(512)S(1)}, f32[512]{0:T(512)}, u32[]{:S(2)}) copy-start(f32[512]{0:T(512)} %get-tuple-element.203) | copy-start | bytes 6148
  107.1 2.3 %copy-start.11 = (f32[512]{0:T(512)S(1)}, f32[512]{0:T(512)}, u32[]{:S(2)}) copy-start(f32[512]{0:T(512)} %get-tuple-element.205) | copy-start | bytes 6148
  108.8 2.4 %copy-start.6 = (bf16[512,512]{1,0:T(8,128)(2,1)S(1)}, bf16[512,512]{1,0:T(8,128)(2,1)}, u32[]{:S(2)}) copy-start(bf16[512,512]{1,0:T(8,128)(2,1)} %get-tuple-element.208) | copy-start | bytes 1572868
  108.8 2.4 %copy-start.10 = (f32[512]{0:T(512)S(1)}, f32[512]{0:T(512)}, u32[]{:S(2)}) copy-start(f32[512]{0:T(512)} %get-tuple-element.207) | copy-start | bytes 6148
  110.6 1.4 copy-start.9
  111.4 2.4 %copy-start.5 = (bf16[512,512]{1,0:T(8,128)(2,1)S(1)}, bf16[512,512]{1,0:T(8,128)(2,1)}, u32[]{:S(2)}) copy-start(bf16[512,512]{1,0:T(8,128)(2,1)} %get-tuple-element.212) | copy-start | bytes 1572868
  111.4 2.4 %copy-start.8 = (f32[512]{0:T(512)S(1)}, f32[512]{0:T(512)}, u32[]{:S(2)}) copy-start(f32[512]{0:T(512)} %get-tuple-element.211) | copy-start | bytes 6148
where the time goes:
time: 196 us; the launch traced here: 195 us
  matrix products  104 us (53%)
  waiting for transfers between devices  31.2 us (16%)
  local copies, waits for them, and re-layouts  28 us (14%)
  starting transfers between devices  20.2 us (10%)
  other arithmetic  10.3 us (5%)
    dot_general x16, matrix products, one_turn(): jnp.einsum('bts,brs->rbt', weights, source[:, DIM:], preferred_element_ty...  60.5 us
    ppermute x8, waiting for transfers between devices, partner(): return lax.ppermute(block, axis, route)  31.2 us
    dot_general x15, matrix products, kernel_block(): jnp.einsum('dm,dn->mn', left, right, preferred_element_type=jnp.float32)  21.4 us
    dot_general x8, matrix products, carry_values(): jnp.dot(values, block, preferred_element_type=jnp.float32) / totals[None, :]  10.9 us
    gather x14, local copies, waits for them, and re-layouts, parent_node(): parent_x = jnp.take(joined_x, chosen, axis=1)  9.91 us
    ppermute x8, starting transfers between devices, partner(): return lax.ppermute(block, axis, route)  9.85 us
    gather x16, local copies, waits for them, and re-layouts, one_turn(): source = jnp.take(leaves, leaf_ids[:, turn], axis=0)  9.43 us
    ppermute x1, starting transfers between devices, extended_2(): after = lax.ppermute(leading, axis, down)  8.39 us
  transfers between devices with their start and end apart: 10, of which 7 were waited for; matrix products, arithmetic and copies ran while one was open for 31% of the time, Pallas kernels for 0%

commit v1 on v0

v1 whole, which is shorter than its diff:
```python
import functools
import math

import jax
import jax.numpy as jnp
from jax import lax
from jax.experimental import pallas as pl
from jax.experimental.pallas import tpu as pltpu
from jax.sharding import PartitionSpec as P

DIM = 16
NRHS = 64
LEAF = 256
TILE = 128
DEPTH = 32
ROWS = 96
GAMMA = 0.125
F32 = jnp.float32
BF16 = jnp.bfloat16

LOG2E = 1.0 / math.log(2.0)
VMEM_LIMIT = 24 * 2**20


def split_rows(x):
    wide = x.astype(F32)
    rest = (-GAMMA) * jnp.sum(wide * wide, axis=0, keepdims=True)
    row = lax.broadcasted_iota(jnp.int32, (DIM, x.shape[1]), 0)
    terms = jnp.where((row >= 3) & (row < 6), 1.0, 0.0)
    for i in range(3):
        term = rest.astype(BF16).astype(F32)
        rest = rest - term
        terms = jnp.where(row == i, term, terms)
    return wide, row, terms


def left_rows(x):
    wide, row, terms = split_rows(x)
    return jnp.concatenate([wide, terms], 0).astype(BF16).T


def right_rows(x):
    wide, row, terms = split_rows(x)
    turned = jnp.where(row < 3, 1.0, 0.0)
    for i in range(3):
        turned = jnp.where(row == i + 3, terms[i : i + 1], turned)
    return jnp.concatenate([wide * (2.0 * GAMMA), turned], 0).astype(BF16)


def dot(a, b):
    return jnp.dot(a, b, preferred_element_type=F32)


def dot_nt(a, b):
    return lax.dot_general(a, b, (((1,), (1,)), ((), ())), preferred_element_type=F32)


def entries(left, right):
    return jnp.exp2(dot(left, right) * LOG2E)


def pick(tiles, index):
    out = []
    for at in range(0, index.shape[1], TILE):
        here = jnp.broadcast_to(index[:, at : at + TILE], (DIM, TILE))
        lane = here & (TILE - 1)
        which = here >> 7
        got = jnp.zeros((DIM, TILE), F32)
        for number, tile in enumerate(tiles):
            got = jnp.where(which == number, jnp.take_along_axis(tile, lane, axis=1), got)
        out.append(got)
    return jnp.concatenate(out, 1)


def tiles_of(x):
    x = x.astype(F32)
    return [x[:, at : at + TILE] for at in range(0, x.shape[1], TILE)]


def index_rows(index):
    row = lax.broadcasted_iota(jnp.int32, (16, index.shape[1]), 0)
    high = (index >> 5).astype(F32)
    low = (index & 31).astype(F32)
    return jnp.where(row == 0, high, jnp.where(row == 1, low, 0.0))


def index_of(rows):
    rows = rows.astype(F32)
    return (rows[0:1] * 32.0 + rows[1:2]).astype(jnp.int32)


def base_kernel(points, charges, chosen, tree, node, block, inverse):
    base_x = pick(
        [points[:, at : at + TILE].astype(F32) for at in range(0, points.shape[1], TILE)],
        chosen[...],
    )
    left = left_rows(base_x)
    count = base_x.shape[1]
    up = jnp.zeros((NRHS, count), F32)
    for at in range(0, points.shape[1], LEAF):
        right = right_rows(points[:, at : at + LEAF])
        total = jnp.zeros((1, LEAF), F32)
        for top in range(0, count, LEAF):
            piece = entries(left[top : top + LEAF], right)
            total = total + jnp.sum(piece, axis=0, keepdims=True)
            block[top : top + LEAF, at : at + LEAF] = piece.astype(BF16)
        scale = 1.0 / total
        inverse[:, at : at + LEAF] = scale
        weights = (charges[:, at : at + LEAF].astype(F32) * scale).astype(BF16)
        up = up + dot_nt(weights, block[:, at : at + LEAF])
    node[0:DIM] = base_x.astype(BF16)
    node[DIM : DIM + NRHS] = up.astype(BF16)
    node[DIM + NRHS : ROWS] = index_rows(tree[0:1]).astype(BF16)


def call(kernel, outs, args, name, scratch=(), smem=(), flops=0):
    specs = [
        pl.BlockSpec(memory_space=pltpu.SMEM if i in smem else pltpu.VMEM)
        for i in range(len(args))
    ]
    moved = sum(a.size * a.dtype.itemsize for a in args)
    return pl.pallas_call(
        kernel,
        out_shape=[jax.ShapeDtypeStruct(s, t) for s, t in outs],
        in_specs=specs,
        out_specs=[pl.BlockSpec(memory_space=pltpu.VMEM)] * len(outs),
        scratch_shapes=list(scratch),
        compiler_params=pltpu.CompilerParams(vmem_limit_bytes=VMEM_LIMIT),
        cost_estimate=pl.CostEstimate(flops=flops, bytes_accessed=moved, transcendentals=0),
        name=name,
    )(*args)


def source_kernel(before_x, own_x, after_x, before_q, own_q, after_q, lefts, rights, loads):
    leaves = own_x.shape[1] // LEAF
    for part, (x, q) in enumerate(((before_x, before_q), (own_x, own_q), (after_x, after_q))):
        for leaf in range(leaves):
            at = leaf * LEAF
            here = x[:, at : at + LEAF]
            lefts[part * leaves + leaf] = left_rows(here)
            loads[part * leaves + leaf] = q[:, at : at + LEAF]
            if part == 1:
                rights[leaf] = right_rows(here)


def near_part(start, count, shift, ids, lefts, rights, loads, out, held):
    turns = ids.shape[1]

    def fill(leaf, turn):
        source = ids[start + leaf, turn] - shift
        held[turn] = entries(lefts[source], rights[start + leaf]).astype(BF16)

    def use(leaf, turn, summed):
        source = ids[start + leaf, turn] - shift
        return summed + dot(loads[source], held[turn])

    for turn in range(turns):
        fill(0, turn)

    def step(leaf, carry):
        summed = jnp.zeros((NRHS, LEAF), F32)
        for turn in range(turns):
            summed = use(leaf - 1, turn, summed)
            fill(leaf, turn)
        out[leaf - 1] = summed
        return carry

    lax.fori_loop(1, count, step, 0)
    summed = jnp.zeros((NRHS, LEAF), F32)
    for turn in range(turns):
        summed = use(count - 1, turn, summed)
    out[count - 1] = summed


def beside(source, target_x, held, out):
    left = left_rows(source[0:DIM])
    right = right_rows(target_x)
    count = target_x.shape[1]
    for top in range(0, count, LEAF):
        for at in range(0, count, LEAF):
            held[top : top + LEAF, at : at + LEAF] = entries(
                left[top : top + LEAF], right[:, at : at + LEAF]
            ).astype(BF16)
    out[...] = dot(source[DIM : DIM + NRHS], held[...])


def near_kernel(start, count, with_sides, where, ids, *refs):
    shift = (where[0] - 1) * (ids.shape[0])
    lefts, rights, loads = refs[:3]
    refs = refs[3:]
    if with_sides:
        own, sibling, parent, uncle, out, side_low, side_high, held, square = refs
        beside(sibling, own[0:DIM], square, side_low)
        beside(uncle, parent[0:DIM], square, side_high)
    else:
        out, held = refs
    near_part(start, count, shift, ids, lefts, rights, loads, out, held)


def link(parent_left, child_x, block, inverse):
    right = right_rows(child_x)
    count = child_x.shape[1]
    for at in range(0, count, LEAF):
        total = jnp.zeros((1, LEAF), F32)
        for top in range(0, count, LEAF):
            piece = entries(parent_left[top : top + LEAF], right[:, at : at + LEAF])
            total = total + jnp.sum(piece, axis=0, keepdims=True)
            block[top : top + LEAF, at : at + LEAF] = piece.astype(BF16)
        inverse[:, at : at + LEAF] = 1.0 / total


def lifted(charges, block, inverse):
    weights = (charges.astype(F32) * inverse[...]).astype(BF16)
    return dot_nt(weights, block[...])


def climb_kernel(low, where, tree, own, sibling, cousin, far_cousin, node, parent, uncle,
                 block_low, inverse_low, block_high, inverse_high, square, spare):
    bit_low = ((where[0] >> low) & 1) * 512
    bit_high = ((where[0] >> (low + 1)) & 1) * 512
    parent_x = pick(tiles_of(own[0:DIM]) + tiles_of(sibling[0:DIM]), tree[low : low + 1] ^ bit_low)
    uncle_x = pick(
        tiles_of(cousin[0:DIM]) + tiles_of(far_cousin[0:DIM]),
        index_of(cousin[DIM + NRHS : ROWS]) ^ bit_low,
    )
    next_x = pick(tiles_of(parent_x) + tiles_of(uncle_x), tree[low + 1 : low + 2] ^ bit_high)
    left = left_rows(parent_x)
    link(left, own[0:DIM], block_low, inverse_low)
    link(left, sibling[0:DIM], square, spare)
    up_parent = lifted(own[DIM : DIM + NRHS], block_low, inverse_low) + lifted(
        sibling[DIM : DIM + NRHS], square, spare
    )
    up_parent = up_parent.astype(BF16)
    left = left_rows(uncle_x)
    link(left, cousin[0:DIM], square, spare)
    up_uncle = lifted(cousin[DIM : DIM + NRHS], square, spare)
    link(left, far_cousin[0:DIM], square, spare)
    up_uncle = up_uncle + lifted(far_cousin[DIM : DIM + NRHS], square, spare)
    up_uncle = up_uncle.astype(BF16)
    left = left_rows(next_x)
    link(left, parent_x, block_high, inverse_high)
    link(left, uncle_x, square, spare)
    up_next = lifted(up_parent, block_high, inverse_high) + lifted(up_uncle, square, spare)
    node[0:DIM] = next_x.astype(BF16)
    node[DIM : DIM + NRHS] = up_next.astype(BF16)
    node[DIM + NRHS : ROWS] = index_rows(tree[low + 2 : low + 3]).astype(BF16)
    parent[0:DIM] = parent_x.astype(BF16)
    parent[DIM:] = up_parent
    uncle[0:DIM] = uncle_x.astype(BF16)
    uncle[DIM:] = up_uncle


def down_kernel(low, where, tree, own, sibling, cousin, far_cousin, *refs):
    levels = low
    blocks = refs[0 : 3 * levels]
    base_block, base_inverse = refs[3 * levels : 3 * levels + 2]
    rest = refs[3 * levels + 2 :]
    nears, (out, square, spare, side, top_block, top_inverse, uncle) = rest[:-7], rest[-7:]
    bit_low = ((where[0] >> low) & 1) * 512
    parent_x = pick(tiles_of(own[0:DIM]) + tiles_of(sibling[0:DIM]), tree[low : low + 1] ^ bit_low)
    uncle_x = pick(
        tiles_of(cousin[0:DIM]) + tiles_of(far_cousin[0:DIM]),
        index_of(cousin[DIM + NRHS : ROWS]) ^ bit_low,
    )
    link(left_rows(parent_x), own[0:DIM], top_block, top_inverse)
    left = left_rows(uncle_x)
    link(left, cousin[0:DIM], square, spare)
    up_uncle = lifted(cousin[DIM : DIM + NRHS], square, spare)
    link(left, far_cousin[0:DIM], square, spare)
    up_uncle = up_uncle + lifted(far_cousin[DIM : DIM + NRHS], square, spare)
    uncle[0:DIM] = uncle_x.astype(BF16)
    uncle[DIM:] = up_uncle.astype(BF16)
    beside(uncle, parent_x, square, side)
    downward = side[...].astype(BF16)
    beside(sibling, own[0:DIM], square, side)
    downward = (side[...] + dot(downward, top_block[...]) * top_inverse[...]).astype(BF16)
    for level in range(levels - 1, -1, -1):
        block, inverse, across = blocks[3 * level : 3 * level + 3]
        downward = (across[...] + dot(downward, block[...]) * inverse[...]).astype(BF16)
    at = 0
    for near in nears:
        for leaf in range(near.shape[0]):
            here = slice(at, at + LEAF)
            out[:, here] = near[leaf] + dot(downward, base_block[:, here]) * base_inverse[:, here]
            at += LEAF


def swapped(array, bits, inner_levels):
    inner, outer = lax.axis_size("inner"), lax.axis_size("outer")
    total = inner * outer
    mask = sum(1 << b for b in bits)
    return lax.ppermute(array, ("outer", "inner"), [(i, i ^ mask) for i in range(total)])


def body(points, charges, near_leaves, skel_device, skel_tree):
    inner_levels = lax.axis_size("inner").bit_length() - 1
    outer_levels = lax.axis_size("outer").bit_length() - 1
    levels = inner_levels + outer_levels
    total = 1 << levels
    position = lax.axis_index(("outer", "inner"))
    where = position.astype(jnp.int32).reshape(1)
    width = points.shape[1]
    leaves = near_leaves.shape[0]
    count = skel_device.shape[1]
    tree = skel_tree[0]
    ring = ("outer", "inner")
    ahead = [(i, (i + 1) % total) for i in range(total)]
    back = [((i + 1) % total, i) for i in range(total)]
    before_x = lax.ppermute(points, ring, ahead)
    after_x = lax.ppermute(points, ring, back)
    before_q = lax.ppermute(charges, ring, ahead)
    after_q = lax.ppermute(charges, ring, back)

    square = pltpu.VMEM((count, count), BF16)
    line = pltpu.VMEM((1, count), F32)
    side_out = ((NRHS, count), F32)
    node_out = ((ROWS, count), BF16)
    pair_out = ((DIM + NRHS, count), BF16)
    block_out = [((count, count), BF16), ((1, count), F32)]

    node, base_block, base_inverse = call(
        base_kernel,
        [node_out, ((count, width), BF16), ((1, width), F32)],
        (points, charges, skel_device, tree),
        "base",
        flops=2 * width * count * (DEPTH + NRHS),
    )
    rounds = levels // 2
    chunk = leaves // rounds
    records = {}
    nears = []
    pending = None
    sources = None
    for turn in range(rounds):
        low = 2 * turn
        sibling = swapped(node, (low,), inner_levels)
        cousin = swapped(node, (low + 1,), inner_levels)
        far_cousin = swapped(node, (low, low + 1), inner_levels)
        if sources is None:
            sources = call(
                source_kernel,
                [
                    ((3 * leaves, LEAF, DEPTH), BF16),
                    ((leaves, DEPTH, LEAF), BF16),
                    ((3 * leaves, NRHS, LEAF), BF16),
                ],
                (before_x, points, after_x, before_q, charges, after_q),
                "sources",
                flops=10**9,
            )
        sources, node = lax.optimization_barrier((sources, node))
        args = (where, near_leaves, *sources)
        outs = [((chunk, NRHS, LEAF), F32)]
        scratch = [pltpu.VMEM((near_leaves.shape[1], LEAF, LEAF), BF16)]
        if pending is not None:
            args += pending
            outs += [side_out, side_out]
            scratch.append(square)
        made = call(
            functools.partial(near_kernel, turn * chunk, chunk, pending is not None),
            outs,
            args,
            "near",
            scratch,
            smem=(0, 1),
            flops=2 * chunk * LEAF * near_leaves.shape[1] * LEAF * (DEPTH + NRHS),
        )
        part, sibling, cousin, far_cousin = lax.optimization_barrier((made[0], sibling, cousin, far_cousin))
        nears.append(part)
        if pending is not None:
            records[low - 2].append(made[1])
            records[low - 1].append(made[2])
        if turn < rounds - 1:
            following, parent, uncle, block_low, inverse_low, block_high, inverse_high = call(
                functools.partial(climb_kernel, low),
                [node_out, pair_out, pair_out, *block_out, *block_out],
                (where, tree, node, sibling, cousin, far_cousin),
                "climb",
                [square, line],
                smem=(0,),
                flops=6 * 2 * count * count * (DEPTH + NRHS),
            )
            records[low] = [block_low, inverse_low]
            records[low + 1] = [block_high, inverse_high]
            pending = (node, sibling, parent, uncle)
            node = following
    low = levels - 2
    kept = [array for level in range(low) for array in records[level]]
    [potential] = call(
        functools.partial(down_kernel, low),
        [((NRHS, width), F32)],
        (where, tree, node, sibling, cousin, far_cousin, *kept, base_block, base_inverse, *nears),
        "down",
        [square, line, pltpu.VMEM(*side_out), square, line, pltpu.VMEM(*pair_out)],
        smem=(0,),
        flops=2 * width * count * NRHS,
    )
    return potential


def solution(mesh):
    return jax.shard_map(
        body,
        mesh=mesh,
        in_specs=(
            P(None, ("outer", "inner")),
            P(None, ("outer", "inner")),
            P(("outer", "inner"), None),
            P(("outer", "inner"), None),
            P(("outer", "inner"), None, None),
        ),
        out_specs=P(None, ("outer", "inner")),
        check_vma=False,
    )
```

time: 196 us -> 88 us (0.45)
  matrix products: 104 us -> 0 us
  Pallas kernels: 0 us -> 38.6 us
  waiting for transfers between devices: 31.2 us -> 5.47 us
  local copies, waits for them, and re-layouts: 28 us -> 7.25 us
  starting transfers between devices: 20.2 us -> 36.3 us
  other arithmetic: 10.3 us -> 0 us
    dot_general x55 -> x0, matrix products: 104 us -> none  [the longest x16 60.5 us: one_turn(): jnp.einsum('bts,brs->rbt', weights, source[:, DIM:], preferred_element_ty...]
    pallas_call x0 -> x10, Pallas kernels: none -> 38.6 us  [call(): pl.pallas_call(kernel, out_shape=[jax.ShapeDtypeStruct(s, t) for s, t in...]
    ppermute x10 -> x16, waiting for transfers between devices: 31.2 us -> 5.47 us  [the longest x12 5.46 us: swapped(): lax.ppermute(array, ('outer', 'inner'), [(i, i ^ mask) for i in range(tot...]
    gather x32 -> x0, local copies, waits for them, and re-layouts: 20.8 us -> none  [the longest x14 9.91 us: parent_node(): parent_x = jnp.take(joined_x, chosen, axis=1)]
    ppermute x10 -> x16, starting transfers between devices: 20.2 us -> 36.3 us  [the longest x12 23.2 us: swapped(): lax.ppermute(array, ('outer', 'inner'), [(i, i ^ mask) for i in range(tot...]
    reduce_sum x42 -> x0, other arithmetic: 7.44 us -> none  [the longest x1 5.87 us: carry_values(): totals = jnp.sum(block.astype(jnp.float32), 0)]
    unnamed x33 -> x17, local copies, waits for them, and re-layouts: 3.63 us -> 7.25 us
    select_n x31 -> x0, other arithmetic: 2.3 us -> none  [the longest x16 2 us: one_turn(): source = jnp.take(leaves, leaf_ids[:, turn], axis=0)]
  transfers between devices with their start and end apart: 10 -> 16, of which waited for: 7 -> 2; matrix products, arithmetic and copies ran while one was open for 31% -> 1% of each run, Pallas kernels for 0% -> 30%
where the time goes in v1:
time: 88 us; the launch traced here: 87.8 us
  Pallas kernels  38.6 us (44%)
  starting transfers between devices  36.3 us (41%)
  local copies, waits for them, and re-layouts  7.25 us (8%)
  waiting for transfers between devices  5.47 us (6%)
    pallas_call x10, Pallas kernels, call(): pl.pallas_call(kernel, out_shape=[jax.ShapeDtypeStruct(s, t) for s, t in...  38.6 us
    ppermute x12, starting transfers between devices, swapped(): lax.ppermute(array, ('outer', 'inner'), [(i, i ^ mask) for i in range(tot...  23.2 us
    unnamed x17, local copies, waits for them, and re-layouts  7.25 us
    ppermute x1, starting transfers between devices, body(): after_q = lax.ppermute(charges, ring, back)  6.56 us
    ppermute x1, starting transfers between devices, body(): after_x = lax.ppermute(points, ring, back)  6.55 us
    ppermute x12, waiting for transfers between devices, swapped(): lax.ppermute(array, ('outer', 'inner'), [(i, i ^ mask) for i in range(tot...  5.46 us
  transfers between devices with their start and end apart: 16, of which 2 were waited for; matrix products, arithmetic and copies ran while one was open for 1% of the time, Pallas kernels for 30%

profile of v1, /device:TPU:2, one launch (start us, length us, event | category | flops | bytes accessed | tf_op | source)
XLA Modules:
  0.0 87.8 jit_solution(4599617797805092128)
XLA Ops:
  0.0 6.6 %collective-permute-start.3 = (bf16[64,4096]{1,0:T(8,128)(2,1)}, bf16[64,4096]{1,0:T(8,128)(2,1)S(1)}, u32[]{:S(2)}, u32[]{:S(2)}) collective-permute-start(bf16[64,4096]{1,0:T(8,128)(2,1)} %charges.1), channel_id=1, source_target_pairs={{1,0},{2,1},{3,2},{4,3},{5,4},{6,5},{7,6},{8,7},{9,8},{10,9},{11,1... | collective-permute-start | bytes 1572872 | tf_op jit(solution)/shard_map/ppermute | solution.py:312
  6.6 6.5 %collective-permute-start.1 = (bf16[16,4096]{1,0:T(8,128)(2,1)}, bf16[16,4096]{1,0:T(8,128)(2,1)S(1)}, u32[]{:S(2)}, u32[]{:S(2)}) collective-permute-start(bf16[16,4096]{1,0:T(8,128)(2,1)} %points.1), channel_id=1, source_target_pairs={{1,0},{2,1},{3,2},{4,3},{5,4},{6,5},{7,6},{8,7},{9,8},{10,9},{11,1... | collective-permute-start | bytes 393224 | tf_op jit(solution)/shard_map/ppermute | solution.py:310
  13.8 1.0 %copy-done.3 = bf16[64,4096]{1,0:T(8,128)(2,1)S(1)} copy-done((bf16[64,4096]{1,0:T(8,128)(2,1)S(1)}, bf16[64,4096]{1,0:T(8,128)(2,1)}, u32[]{:S(2)}) %copy-start.3) | copy-done | bytes 524312
  14.9 0.9 %copy-done.5 = bf16[16,4096]{1,0:T(8,128)(2,1)S(1)} copy-done((bf16[16,4096]{1,0:T(8,128)(2,1)S(1)}, bf16[16,4096]{1,0:T(8,128)(2,1)}, u32[]{:S(2)}) %copy-start.5) | copy-done | bytes 131096
  16.5 4.1 %base.1 = (bf16[96,512]{1,0:T(8,128)(2,1)S(1)}, bf16[512,4096]{1,0:T(8,128)(2,1)S(1)}, f32[1,4096]{1,0:T(1,128)S(1)}) custom-call(bf16[16,4096]{1,0:T(8,128)(2,1)S(1)} %copy-done.5, bf16[64,4096]{1,0:T(8,128)(2,1)S(1)} %copy-done.3, s32[1,512]{1,0:T(1,128)S(1)} %copy-done.7, s32[7,512]{1,0:T(8,128)S(1)} %bitcast.4), custom_call_target="tpu_custom_call" | custom-call | flops 402653184 | bytes 671744 | tf_op jit(solution)/shard_map/base/pallas_call | solution.py:122
  20.6 2.0 %copy-done = bf16[512,4096]{1,0:T(8,128)(2,1)} copy-done((bf16[512,4096]{1,0:T(8,128)(2,1)}, bf16[512,4096]{1,0:T(8,128)(2,1)S(1)}, u32[]{:S(2)}) %copy-start) | copy-done | bytes 4194328
  22.6 1.9 %collective-permute-start.6 = (bf16[96,512]{1,0:T(8,128)(2,1)S(1)}, bf16[96,512]{1,0:T(8,128)(2,1)S(1)}, u32[]{:S(2)}, u32[]{:S(2)}) collective-permute-start(bf16[96,512]{1,0:T(8,128)(2,1)S(1)} %get-tuple-element.80.own.refs_3_), channel_id=1, source_target_pairs={{0,3},{1,2},{2,1},{3,0},{4,7},{5,6},{6,5},{7,4},{8,11},{9,10},{10,... | collective-permute-start | bytes 294920 | tf_op jit(solution)/shard_map/ppermute | solution.py:292
  24.5 1.0 %copy-done.4 = bf16[64,4096]{1,0:T(8,128)(2,1)S(1)} copy-done((bf16[64,4096]{1,0:T(8,128)(2,1)S(1)}, bf16[64,4096]{1,0:T(8,128)(2,1)}, u32[]{:S(2)}) %copy-start.4) | copy-done | bytes 524312
  26.4 1.0 %sources.1 = (bf16[48,256,32]{2,1,0:T(8,128)(2,1)S(1)}, bf16[16,32,256]{2,1,0:T(8,128)(2,1)S(1)}, bf16[48,64,256]{2,1,0:T(8,128)(2,1)S(1)}) custom-call(bf16[16,4096]{1,0:T(8,128)(2,1)S(1)} %collective-permute-done.before_x, bf16[16,4096]{1,0:T(8,128)(2,1)S(1)} %copy-done.6, bf16[16,4096]{1,0:T(8,128)(2,1)S(1)} %collective-permute-done.1.after_x, ...), custom_call_target="tpu_custom_call" | custom-call | flops 1000000000 | bytes 1966080 | tf_op jit(solution)/shard_map/sources/pallas_call | solution.py:122
  27.4 4.8 %near.4.refs_20_ = f32[4,64,256]{2,1,0:T(8,128)S(1)} custom-call(s32[1]{0:T(128)} %bitcast.where, s32[16,16]{1,0:T(8,128)S(1)} %copy-done.2, bf16[48,256,32]{2,1,0:T(8,128)(2,1)S(1)} %get-tuple-element.108.refs_0_, bf16[16,32,256]{2,1,0:T(8,128)(2,1)S(1)} %get-tuple-element.109.refs_1_, bf16[48,64,256]{2,1,0:T(8,128)(2,1)S(1)} %get-tuple-element.110.refs_2_), custom_call_target="tpu_custom_call" | custom-call | flops 805306368 | bytes 2622468 | tf_op jit(solution)/shard_map/near/pallas_call | solution.py:122
  32.3 2.5 %climb.3 = (bf16[96,512]{1,0:T(8,128)(2,1)S(1)}, bf16[80,512]{1,0:T(8,128)(2,1)S(1)}, bf16[80,512]{1,0:T(8,128)(2,1)S(1)}, bf16[512,512]{1,0:T(8,128)(2,1)S(1)},...) custom-call(s32[1]{0:T(128)} %bitcast.where, s32[7,512]{1,0:T(8,128)S(1)} %bitcast.5, ...), custom_call_target="tpu_custom_call" | custom-call | flops 301989888 | bytes 407556 | tf_op jit(solution)/shard_map/climb/pallas_call | solution.py:122
  35.1 4.9 %collective-permute-start.9 = (bf16[96,512]{1,0:T(8,128)(2,1)S(1)}, bf16[96,512]{1,0:T(8,128)(2,1)S(1)}, u32[]{:S(2)}, u32[]{:S(2)}) collective-permute-start(bf16[96,512]{1,0:T(8,128)(2,1)S(1)} %get-tuple-element.88.own.refs_3_), channel_id=1, source_target_pairs={{0,12},{1,13},{2,14},{3,15},{4,8},{5,9},{6,10},{7,11},{8,4},{9,5},... | collective-permute-start | bytes 294920 | tf_op jit(solution)/shard_map/ppermute | solution.py:292
  40.0 5.5 %near.5 = (f32[4,64,256]{2,1,0:T(8,128)S(1)}, f32[64,512]{1,0:T(8,128)S(1)}, f32[64,512]{1,0:T(8,128)S(1)}) custom-call(s32[1]{0:T(128)} %bitcast.where, s32[16,16]{1,0:T(8,128)S(1)} %copy-done.2, bf16[48,256,32]{2,1,0:T(8,128)(2,1)S(1)} %get-tuple-element.108.refs_0_, bf16[16,32,256]{2,1,0:T(8,128)(2,1)S(1)} %get-tuple-element.109.refs_1_, ...), custom_call_target="tpu_custom_call" | custom-call | flops 805306368 | bytes 2982916 | tf_op jit(solution)/shard_map/near/pallas_call | solution.py:122
  45.6 2.5 %climb.4 = (bf16[96,512]{1,0:T(8,128)(2,1)S(1)}, bf16[80,512]{1,0:T(8,128)(2,1)S(1)}, bf16[80,512]{1,0:T(8,128)(2,1)S(1)}, bf16[512,512]{1,0:T(8,128)(2,1)S(1)},...) custom-call(s32[1]{0:T(128)} %bitcast.where, s32[7,512]{1,0:T(8,128)S(1)} %bitcast.6, ...), custom_call_target="tpu_custom_call" | custom-call | flops 301989888 | bytes 407556 | tf_op jit(solution)/shard_map/climb/pallas_call | solution.py:122
  48.2 4.7 %collective-permute-start.11 = (bf16[96,512]{1,0:T(8,128)(2,1)S(1)}, bf16[96,512]{1,0:T(8,128)(2,1)S(1)}, u32[]{:S(2)}, u32[]{:S(2)}) collective-permute-start(bf16[96,512]{1,0:T(8,128)(2,1)S(1)} %get-tuple-element.99.own.refs_3_), channel_id=1, source_target_pairs={{0,32},{1,33},{2,34},{3,35},{4,36},{5,37},{6,38},{7,39},{8,40},{9,... | collective-permute-start | bytes 294920 | tf_op jit(solution)/shard_map/ppermute | solution.py:292
  52.9 2.3 %collective-permute-start.12 = (bf16[96,512]{1,0:T(8,128)(2,1)S(1)}, bf16[96,512]{1,0:T(8,128)(2,1)S(1)}, u32[]{:S(2)}, u32[]{:S(2)}) collective-permute-start(bf16[96,512]{1,0:T(8,128)(2,1)S(1)} %get-tuple-element.99.own.refs_3_), channel_id=1, source_target_pairs={{0,48},{1,49},{2,50},{3,51},{4,52},{5,53},{6,54},{7,55},{8,56},{9,... | collective-permute-start | bytes 294920 | tf_op jit(solution)/shard_map/ppermute | solution.py:292
  55.1 5.5 %near.6 = (f32[4,64,256]{2,1,0:T(8,128)S(1)}, f32[64,512]{1,0:T(8,128)S(1)}, f32[64,512]{1,0:T(8,128)S(1)}) custom-call(s32[1]{0:T(128)} %bitcast.where, s32[16,16]{1,0:T(8,128)S(1)} %copy-done.2, bf16[48,256,32]{2,1,0:T(8,128)(2,1)S(1)} %get-tuple-element.108.refs_0_, bf16[16,32,256]{2,1,0:T(8,128)(2,1)S(1)} %get-tuple-element.109.refs_1_, ...), custom_call_target="tpu_custom_call" | custom-call | flops 805306368 | bytes 2982916 | tf_op jit(solution)/shard_map/near/pallas_call | solution.py:122
  60.6 2.6 %collective-permute-done.12.far_cousin = bf16[96,512]{1,0:T(8,128)(2,1)S(1)} collective-permute-done((bf16[96,512]{1,0:T(8,128)(2,1)S(1)}, bf16[96,512]{1,0:T(8,128)(2,1)S(1)}, u32[]{:S(2)}, u32[]{:S(2)}) %collective-permute-start.12) | collective-permute-done | bytes 98336 | tf_op jit(solution)/shard_map/ppermute | solution.py:292
  63.3 2.5 %climb.5 = (bf16[96,512]{1,0:T(8,128)(2,1)S(1)}, bf16[80,512]{1,0:T(8,128)(2,1)S(1)}, bf16[80,512]{1,0:T(8,128)(2,1)S(1)}, bf16[512,512]{1,0:T(8,128)(2,1)S(1)},...) custom-call(s32[1]{0:T(128)} %bitcast.where, s32[7,512]{1,0:T(8,128)S(1)} %bitcast.7, ...), custom_call_target="tpu_custom_call" | custom-call | flops 301989888 | bytes 407556 | tf_op jit(solution)/shard_map/climb/pallas_call | solution.py:122
  65.8 5.5 %collective-permute-start.14 = (bf16[96,512]{1,0:T(8,128)(2,1)S(1)}, bf16[96,512]{1,0:T(8,128)(2,1)S(1)}, u32[]{:S(2)}, u32[]{:S(2)}) collective-permute-start(bf16[96,512]{1,0:T(8,128)(2,1)S(1)} %get-tuple-element.107.own), channel_id=1, source_target_pairs={{0,128},{1,129},{2,130},{3,131},{4,132},{5,133},{6,134},{7,135},{8... | collective-permute-start | bytes 294920 | tf_op jit(solution)/shard_map/ppermute | solution.py:292
  71.3 3.4 %collective-permute-start.15 = (bf16[96,512]{1,0:T(8,128)(2,1)S(1)}, bf16[96,512]{1,0:T(8,128)(2,1)S(1)}, u32[]{:S(2)}, u32[]{:S(2)}) collective-permute-start(bf16[96,512]{1,0:T(8,128)(2,1)S(1)} %get-tuple-element.107.own), channel_id=1, source_target_pairs={{0,192},{1,193},{2,194},{3,195},{4,196},{5,197},{6,198},{7,199},{8... | collective-permute-start | bytes 294920 | tf_op jit(solution)/shard_map/ppermute | solution.py:292
  74.7 5.5 %near.7 = (f32[4,64,256]{2,1,0:T(8,128)S(1)}, f32[64,512]{1,0:T(8,128)S(1)}, f32[64,512]{1,0:T(8,128)S(1)}) custom-call(s32[1]{0:T(128)} %bitcast.where, s32[16,16]{1,0:T(8,128)S(1)} %copy-done.2, bf16[48,256,32]{2,1,0:T(8,128)(2,1)S(1)} %get-tuple-element.108.refs_0_, bf16[16,32,256]{2,1,0:T(8,128)(2,1)S(1)} %get-tuple-element.109.refs_1_, ...), custom_call_target="tpu_custom_call" | custom-call | flops 805306368 | bytes 2982916 | tf_op jit(solution)/shard_map/near/pallas_call | solution.py:122
  80.3 2.8 %collective-permute-done.15.far_cousin = bf16[96,512]{1,0:T(8,128)(2,1)S(1)} collective-permute-done((bf16[96,512]{1,0:T(8,128)(2,1)S(1)}, bf16[96,512]{1,0:T(8,128)(2,1)S(1)}, u32[]{:S(2)}, u32[]{:S(2)}) %collective-permute-start.15) | collective-permute-done | bytes 98336 | tf_op jit(solution)/shard_map/ppermute | solution.py:292
  83.1 4.7 %down.1 = f32[64,4096]{1,0:T(8,128)} custom-call(s32[1]{0:T(128)} %bitcast.where, s32[7,512]{1,0:T(8,128)S(1)} %bitcast.8, bf16[96,512]{1,0:T(8,128)(2,1)S(1)} %get-tuple-element.107.own, bf16[96,512]{1,0:T(8,128)(2,1)S(1)} %collective-permute-done.13.sibling, bf16[96,512]{1,0:T(8,128)(2,1)S(1)} %collective-permute-done.14.cousin, ...), custom_call_target="tpu_custom_call" | custom-call | flops 268435456 | bytes 9611268 | tf_op jit(solution)/shard_map/down/pallas_call | solution.py:122
  (35 shorter events, 2.9 us)
Async XLA Ops:
  0.0 27.4 %copy-start.2 = (s32[16,16]{1,0:T(8,128)S(1)}, s32[16,16]{1,0:T(8,128)}, u32[]{:S(2)}) copy-start(s32[16,16]{1,0:T(8,128)} %ids.7) | copy-start | bytes 3076
  0.0 24.5 %collective-permute-start.2 = (bf16[64,4096]{1,0:T(8,128)(2,1)}, bf16[64,4096]{1,0:T(8,128)(2,1)S(1)}, u32[]{:S(2)}, u32[]{:S(2)}) collective-permute-start(bf16[64,4096]{1,0:T(8,128)(2,1)} %charges.1), channel_id=1, source_target_pairs={{0,1},{1,2},{2,3},{3,4},{4,5},{5,6},{6,7},{7,8},{8,9},{9,10},{10,1... | collective-permute-start | bytes 1572872 | tf_op jit(solution)/shard_map/ppermute | solution.py:311
  0.0 24.5 %collective-permute-start.3 = (bf16[64,4096]{1,0:T(8,128)(2,1)}, bf16[64,4096]{1,0:T(8,128)(2,1)S(1)}, u32[]{:S(2)}, u32[]{:S(2)}) collective-permute-start(bf16[64,4096]{1,0:T(8,128)(2,1)} %charges.1), channel_id=1, source_target_pairs={{1,0},{2,1},{3,2},{4,3},{5,4},{6,5},{7,6},{8,7},{9,8},{10,9},{11,1... | collective-permute-start | bytes 1572872 | tf_op jit(solution)/shard_map/ppermute | solution.py:312
  6.6 16.0 %collective-permute-start = (bf16[16,4096]{1,0:T(8,128)(2,1)}, bf16[16,4096]{1,0:T(8,128)(2,1)S(1)}, u32[]{:S(2)}, u32[]{:S(2)}) collective-permute-start(bf16[16,4096]{1,0:T(8,128)(2,1)} %points.1), channel_id=1, source_target_pairs={{0,1},{1,2},{2,3},{3,4},{4,5},{5,6},{6,7},{7,8},{8,9},{9,10},{10,1... | collective-permute-start | bytes 393224 | tf_op jit(solution)/shard_map/ppermute | solution.py:309
  6.6 16.0 %collective-permute-start.1 = (bf16[16,4096]{1,0:T(8,128)(2,1)}, bf16[16,4096]{1,0:T(8,128)(2,1)S(1)}, u32[]{:S(2)}, u32[]{:S(2)}) collective-permute-start(bf16[16,4096]{1,0:T(8,128)(2,1)} %points.1), channel_id=1, source_target_pairs={{1,0},{2,1},{3,2},{4,3},{5,4},{6,5},{7,6},{8,7},{9,8},{10,9},{11,1... | collective-permute-start | bytes 393224 | tf_op jit(solution)/shard_map/ppermute | solution.py:310
  13.8 1.0 %copy-start.3 = (bf16[64,4096]{1,0:T(8,128)(2,1)S(1)}, bf16[64,4096]{1,0:T(8,128)(2,1)}, u32[]{:S(2)}) copy-start(bf16[64,4096]{1,0:T(8,128)(2,1)} %charges.1) | copy-start | bytes 1572868
  14.9 0.9 %copy-start.5 = (bf16[16,4096]{1,0:T(8,128)(2,1)S(1)}, bf16[16,4096]{1,0:T(8,128)(2,1)}, u32[]{:S(2)}) copy-start(bf16[16,4096]{1,0:T(8,128)(2,1)} %points.1) | copy-start | bytes 393220
  15.8 0.7 copy-start.7
  20.6 2.0 %copy-start = (bf16[512,4096]{1,0:T(8,128)(2,1)}, bf16[512,4096]{1,0:T(8,128)(2,1)S(1)}, u32[]{:S(2)}) copy-start(bf16[512,4096]{1,0:T(8,128)(2,1)S(1)} %get-tuple-element.135.refs_18_) | copy-start | bytes 12582916
  22.6 9.7 %collective-permute-start.4 = (bf16[96,512]{1,0:T(8,128)(2,1)S(1)}, bf16[96,512]{1,0:T(8,128)(2,1)S(1)}, u32[]{:S(2)}, u32[]{:S(2)}) collective-permute-start(bf16[96,512]{1,0:T(8,128)(2,1)S(1)} %get-tuple-element.80.own.refs_3_), channel_id=1, source_target_pairs={{0,1},{1,0},{2,3},{3,2},{4,5},{5,4},{6,7},{7,6},{8,9},{9,8},{10,11... | collective-permute-start | bytes 294920 | tf_op jit(solution)/shard_map/ppermute | solution.py:292
  22.6 9.7 %collective-permute-start.5 = (bf16[96,512]{1,0:T(8,128)(2,1)S(1)}, bf16[96,512]{1,0:T(8,128)(2,1)S(1)}, u32[]{:S(2)}, u32[]{:S(2)}) collective-permute-start(bf16[96,512]{1,0:T(8,128)(2,1)S(1)} %get-tuple-element.80.own.refs_3_), channel_id=1, source_target_pairs={{0,2},{1,3},{2,0},{3,1},{4,6},{5,7},{6,4},{7,5},{8,10},{9,11},{10,... | collective-permute-start | bytes 294920 | tf_op jit(solution)/shard_map/ppermute | solution.py:292
  22.6 9.7 %collective-permute-start.6 = (bf16[96,512]{1,0:T(8,128)(2,1)S(1)}, bf16[96,512]{1,0:T(8,128)(2,1)S(1)}, u32[]{:S(2)}, u32[]{:S(2)}) collective-permute-start(bf16[96,512]{1,0:T(8,128)(2,1)S(1)} %get-tuple-element.80.own.refs_3_), channel_id=1, source_target_pairs={{0,3},{1,2},{2,1},{3,0},{4,7},{5,6},{6,5},{7,4},{8,11},{9,10},{10,... | collective-permute-start | bytes 294920 | tf_op jit(solution)/shard_map/ppermute | solution.py:292
  24.5 1.0 %copy-start.4 = (bf16[64,4096]{1,0:T(8,128)(2,1)S(1)}, bf16[64,4096]{1,0:T(8,128)(2,1)}, u32[]{:S(2)}) copy-start(bf16[64,4096]{1,0:T(8,128)(2,1)} %charges.1) | copy-start | bytes 1572868
  25.5 0.9 %copy-start.6 = (bf16[16,4096]{1,0:T(8,128)(2,1)S(1)}, bf16[16,4096]{1,0:T(8,128)(2,1)}, u32[]{:S(2)}) copy-start(bf16[16,4096]{1,0:T(8,128)(2,1)} %points.1) | copy-start | bytes 393220
  34.8 10.8 %collective-permute-start.7 = (bf16[96,512]{1,0:T(8,128)(2,1)S(1)}, bf16[96,512]{1,0:T(8,128)(2,1)S(1)}, u32[]{:S(2)}, u32[]{:S(2)}) collective-permute-start(bf16[96,512]{1,0:T(8,128)(2,1)S(1)} %get-tuple-element.88.own.refs_3_), channel_id=1, source_target_pairs={{0,4},{1,5},{2,6},{3,7},{4,0},{5,1},{6,2},{7,3},{8,12},{9,13},{10,... | collective-permute-start | bytes 294920 | tf_op jit(solution)/shard_map/ppermute | solution.py:292
  35.0 10.5 %collective-permute-start.8 = (bf16[96,512]{1,0:T(8,128)(2,1)S(1)}, bf16[96,512]{1,0:T(8,128)(2,1)S(1)}, u32[]{:S(2)}, u32[]{:S(2)}) collective-permute-start(bf16[96,512]{1,0:T(8,128)(2,1)S(1)} %get-tuple-element.88.own.refs_3_), channel_id=1, source_target_pairs={{0,8},{1,9},{2,10},{3,11},{4,12},{5,13},{6,14},{7,15},{8,0},{9,1},... | collective-permute-start | bytes 294920 | tf_op jit(solution)/shard_map/ppermute | solution.py:292
  35.1 10.4 %collective-permute-start.9 = (bf16[96,512]{1,0:T(8,128)(2,1)S(1)}, bf16[96,512]{1,0:T(8,128)(2,1)S(1)}, u32[]{:S(2)}, u32[]{:S(2)}) collective-permute-start(bf16[96,512]{1,0:T(8,128)(2,1)S(1)} %get-tuple-element.88.own.refs_3_), channel_id=1, source_target_pairs={{0,12},{1,13},{2,14},{3,15},{4,8},{5,9},{6,10},{7,11},{8,4},{9,5},... | collective-permute-start | bytes 294920 | tf_op jit(solution)/shard_map/ppermute | solution.py:292
  48.1 12.6 %collective-permute-start.10 = (bf16[96,512]{1,0:T(8,128)(2,1)S(1)}, bf16[96,512]{1,0:T(8,128)(2,1)S(1)}, u32[]{:S(2)}, u32[]{:S(2)}) collective-permute-start(bf16[96,512]{1,0:T(8,128)(2,1)S(1)} %get-tuple-element.99.own.refs_3_), channel_id=1, source_target_pairs={{0,16},{1,17},{2,18},{3,19},{4,20},{5,21},{6,22},{7,23},{8,24},{9,... | collective-permute-start | bytes 294920 | tf_op jit(solution)/shard_map/ppermute | solution.py:292
  48.2 12.5 %collective-permute-start.11 = (bf16[96,512]{1,0:T(8,128)(2,1)S(1)}, bf16[96,512]{1,0:T(8,128)(2,1)S(1)}, u32[]{:S(2)}, u32[]{:S(2)}) collective-permute-start(bf16[96,512]{1,0:T(8,128)(2,1)S(1)} %get-tuple-element.99.own.refs_3_), channel_id=1, source_target_pairs={{0,32},{1,33},{2,34},{3,35},{4,36},{5,37},{6,38},{7,39},{8,40},{9,... | collective-permute-start | bytes 294920 | tf_op jit(solution)/shard_map/ppermute | solution.py:292
  52.9 10.4 %collective-permute-start.12 = (bf16[96,512]{1,0:T(8,128)(2,1)S(1)}, bf16[96,512]{1,0:T(8,128)(2,1)S(1)}, u32[]{:S(2)}, u32[]{:S(2)}) collective-permute-start(bf16[96,512]{1,0:T(8,128)(2,1)S(1)} %get-tuple-element.99.own.refs_3_), channel_id=1, source_target_pairs={{0,48},{1,49},{2,50},{3,51},{4,52},{5,53},{6,54},{7,55},{8,56},{9,... | collective-permute-start | bytes 294920 | tf_op jit(solution)/shard_map/ppermute | solution.py:292
  63.3 19.8 %copy-start.1 = (bf16[512,4096]{1,0:T(8,128)(2,1)S(1)}, bf16[512,4096]{1,0:T(8,128)(2,1)}, u32[]{:S(2)}) copy-start(bf16[512,4096]{1,0:T(8,128)(2,1)} %copy-done) | copy-start | bytes 12582916
  65.7 14.5 %collective-permute-start.13 = (bf16[96,512]{1,0:T(8,128)(2,1)S(1)}, bf16[96,512]{1,0:T(8,128)(2,1)S(1)}, u32[]{:S(2)}, u32[]{:S(2)}) collective-permute-start(bf16[96,512]{1,0:T(8,128)(2,1)S(1)} %get-tuple-element.107.own), channel_id=1, source_target_pairs={{0,64},{1,65},{2,66},{3,67},{4,68},{5,69},{6,70},{7,71},{8,72},{9,... | collective-permute-start | bytes 294920 | tf_op jit(solution)/shard_map/ppermute | solution.py:292
  65.8 14.4 %collective-permute-start.14 = (bf16[96,512]{1,0:T(8,128)(2,1)S(1)}, bf16[96,512]{1,0:T(8,128)(2,1)S(1)}, u32[]{:S(2)}, u32[]{:S(2)}) collective-permute-start(bf16[96,512]{1,0:T(8,128)(2,1)S(1)} %get-tuple-element.107.own), channel_id=1, source_target_pairs={{0,128},{1,129},{2,130},{3,131},{4,132},{5,133},{6,134},{7,135},{8... | collective-permute-start | bytes 294920 | tf_op jit(solution)/shard_map/ppermute | solution.py:292
  71.3 11.8 %collective-permute-start.15 = (bf16[96,512]{1,0:T(8,128)(2,1)S(1)}, bf16[96,512]{1,0:T(8,128)(2,1)S(1)}, u32[]{:S(2)}, u32[]{:S(2)}) collective-permute-start(bf16[96,512]{1,0:T(8,128)(2,1)S(1)} %get-tuple-element.107.own), channel_id=1, source_target_pairs={{0,192},{1,193},{2,194},{3,195},{4,196},{5,197},{6,198},{7,199},{8... | collective-permute-start | bytes 294920 | tf_op jit(solution)/shard_map/ppermute | solution.py:292

commit v2 on v1

v2 whole, which is shorter than its diff:
```python
import functools
import math

import jax
import jax.numpy as jnp
from jax import lax
from jax.experimental import pallas as pl
from jax.experimental.pallas import tpu as pltpu
from jax.sharding import PartitionSpec as P

DIM = 16
NRHS = 64
LEAF = 256
TILE = 128
DEPTH = 32
GAMMA = 0.125
F32 = jnp.float32
BF16 = jnp.bfloat16

LOG2E = 1.0 / math.log(2.0)
VMEM_LIMIT = 24 * 2**20


def split_rows(x):
    wide = x.astype(F32)
    rest = (-GAMMA) * jnp.sum(wide * wide, axis=0, keepdims=True)
    row = lax.broadcasted_iota(jnp.int32, (DIM, x.shape[1]), 0)
    terms = jnp.where((row >= 3) & (row < 6), 1.0, 0.0)
    for i in range(3):
        term = rest.astype(BF16).astype(F32)
        rest = rest - term
        terms = jnp.where(row == i, term, terms)
    return wide, row, terms


def left_rows(x):
    wide, row, terms = split_rows(x)
    return jnp.concatenate([wide, terms], 0).astype(BF16).T


def right_rows(x):
    wide, row, terms = split_rows(x)
    turned = jnp.where(row < 3, 1.0, 0.0)
    for i in range(3):
        turned = jnp.where(row == i + 3, terms[i : i + 1], turned)
    return jnp.concatenate([wide * (2.0 * GAMMA), turned], 0).astype(BF16)


def dot(a, b):
    return jnp.dot(a, b, preferred_element_type=F32)


def dot_nt(a, b):
    return lax.dot_general(a, b, (((1,), (1,)), ((), ())), preferred_element_type=F32)


def entries(left, right):
    return jnp.exp2(dot(left, right) * LOG2E)


def pick(tiles, index):
    out = []
    for at in range(0, index.shape[1], TILE):
        here = jnp.broadcast_to(index[:, at : at + TILE], (DIM, TILE))
        lane = here & (TILE - 1)
        which = here >> 7
        got = jnp.zeros((DIM, TILE), F32)
        for number, tile in enumerate(tiles):
            got = jnp.where(which == number, jnp.take_along_axis(tile, lane, axis=1), got)
        out.append(got)
    return jnp.concatenate(out, 1)


def tiles_of(x):
    x = x.astype(F32)
    return [x[:, at : at + TILE] for at in range(0, x.shape[1], TILE)]


def base_kernel(
    points_in, charges_in, tree_in, chosen_in, ids_in,
    node, block, inverse, points, charges, rights, tree_out, ids,
    tree, chosen, sems,
):
    position = lax.axis_index(("outer", "inner"))
    copies = [
        pltpu.make_async_copy(source, target, sems.at[i])
        for i, (source, target) in enumerate(
            (
                (points_in, points),
                (chosen_in, chosen),
                (tree_in, tree),
                (charges_in, charges),
                (ids_in, ids),
            )
        )
    ]
    for copy in copies:
        copy.start()
    leaves = rights.shape[0]
    copies[0].wait()
    copies[1].wait()
    base_x = pick(
        [points[:, at : at + TILE].astype(F32) for at in range(0, points.shape[1], TILE)],
        chosen[...],
    )
    node[0:DIM] = base_x.astype(BF16)
    left = left_rows(base_x)
    count = base_x.shape[1]
    copies[2].wait()
    for level in range(tree.shape[0]):
        bit = ((position >> level) & 1) * count
        tree_out[level : level + 1] = tree[level] ^ bit
    copies[3].wait()
    up = jnp.zeros((NRHS, count), F32)
    for leaf in range(leaves):
        here = slice(leaf * LEAF, (leaf + 1) * LEAF)
        right = right_rows(points[:, here])
        rights[leaf] = right
        total = jnp.zeros((1, LEAF), F32)
        for top in range(0, count, LEAF):
            piece = entries(left[top : top + LEAF], right)
            total = total + jnp.sum(piece, axis=0, keepdims=True)
            block[top : top + LEAF, here] = piece.astype(BF16)
        scale = 1.0 / total
        inverse[:, here] = scale
        weights = (charges[:, here].astype(F32) * scale).astype(BF16)
        up = up + dot_nt(weights, block[:, here])
    node[DIM:] = up.astype(BF16)
    copies[4].wait()


def call(kernel, outs, args, name, scratch=(), spaces={}, out_spaces={}, aliases={}, flops=0):
    moved = sum(a.size * a.dtype.itemsize for a in args)
    args = [
        pltpu.with_memory_space_constraint(a, pltpu.HBM) if spaces.get(i) is pltpu.HBM else a
        for i, a in enumerate(args)
    ]
    return pl.pallas_call(
        kernel,
        out_shape=[
            pltpu.SMEM(s, t) if out_spaces.get(i) is pltpu.SMEM else jax.ShapeDtypeStruct(s, t)
            for i, (s, t) in enumerate(outs)
        ],
        in_specs=[pl.BlockSpec(memory_space=spaces.get(i, pltpu.VMEM)) for i in range(len(args))],
        out_specs=[
            pl.BlockSpec(memory_space=out_spaces.get(i, pltpu.VMEM)) for i in range(len(outs))
        ],
        scratch_shapes=list(scratch),
        input_output_aliases=aliases,
        compiler_params=pltpu.CompilerParams(vmem_limit_bytes=VMEM_LIMIT),
        cost_estimate=pl.CostEstimate(flops=flops, bytes_accessed=moved, transcendentals=0),
        name=name,
    )(*args)


def prepare(x, q, first, leaves, lefts, loads):
    for leaf in range(leaves):
        here = slice(leaf * LEAF, (leaf + 1) * LEAF)
        lefts[first + leaf] = left_rows(x[:, here])
        loads[first + leaf] = q[:, here]


def own_kernel(x, q, lefts, loads):
    leaves = lefts.shape[0] // 3
    prepare(x, q, leaves, leaves, lefts, loads)


def halo_kernel(before_x, after_x, before_q, after_q, lefts_in, loads_in, lefts, loads):
    leaves = lefts.shape[0] // 3
    prepare(before_x, before_q, 0, leaves, lefts, loads)
    prepare(after_x, after_q, 2 * leaves, leaves, lefts, loads)


def near_part(start, count, shift, ids, lefts, rights, loads, out, held):
    turns = ids.shape[1]

    def fill(leaf, turn):
        source = ids[start + leaf, turn] - shift
        held[turn] = entries(lefts[source], rights[start + leaf]).astype(BF16)

    def use(leaf, turn, summed):
        source = ids[start + leaf, turn] - shift
        return summed + dot(loads[source], held[turn])

    for turn in range(turns):
        fill(0, turn)

    def step(leaf, carry):
        summed = jnp.zeros((NRHS, LEAF), F32)
        for turn in range(turns):
            summed = use(leaf - 1, turn, summed)
            fill(leaf, turn)
        out[leaf - 1] = summed
        return carry

    lax.fori_loop(1, count, step, 0)
    summed = jnp.zeros((NRHS, LEAF), F32)
    for turn in range(turns):
        summed = use(count - 1, turn, summed)
    out[count - 1] = summed


def beside(source, target_x, held, out):
    left = left_rows(source[0:DIM])
    right = right_rows(target_x)
    count = target_x.shape[1]
    for top in range(0, count, LEAF):
        for at in range(0, count, LEAF):
            held[top : top + LEAF, at : at + LEAF] = entries(
                left[top : top + LEAF], right[:, at : at + LEAF]
            ).astype(BF16)
    out[...] = dot(source[DIM:], held[...])


def near_kernel(start, count, ids, lefts, rights, loads, own, sibling, out, side, held, square):
    beside(sibling, own[0:DIM], square, side)
    shift = (lax.axis_index(("outer", "inner")) - 1) * rights.shape[0]
    near_part(start, count, shift, ids, lefts, rights, loads, out, held)


def link(parent_left, child_x, block, inverse):
    right = right_rows(child_x)
    count = child_x.shape[1]
    for at in range(0, count, LEAF):
        total = jnp.zeros((1, LEAF), F32)
        for top in range(0, count, LEAF):
            piece = entries(parent_left[top : top + LEAF], right[:, at : at + LEAF])
            total = total + jnp.sum(piece, axis=0, keepdims=True)
            block[top : top + LEAF, at : at + LEAF] = piece.astype(BF16)
        inverse[:, at : at + LEAF] = 1.0 / total


def lifted(charges, block, inverse):
    weights = (charges.astype(F32) * inverse[...]).astype(BF16)
    return dot_nt(weights, block[...])


def climb_kernel(level, tree, own, sibling, node, block, inverse, square, spare):
    next_x = pick(tiles_of(own[0:DIM]) + tiles_of(sibling[0:DIM]), tree[level : level + 1])
    left = left_rows(next_x)
    link(left, own[0:DIM], block, inverse)
    link(left, sibling[0:DIM], square, spare)
    up = lifted(own[DIM:], block, inverse) + lifted(sibling[DIM:], square, spare)
    node[0:DIM] = next_x.astype(BF16)
    node[DIM:] = up.astype(BF16)


def down_kernel(levels, own, sibling, *refs):
    blocks = refs[0 : 3 * levels]
    base_block, base_inverse = refs[3 * levels : 3 * levels + 2]
    nears = refs[3 * levels + 2 : -5]
    out, square, side, made, sems = refs[-5:]
    beside(sibling, own[0:DIM], square, side)
    downward = side[...].astype(BF16)
    for level in range(levels - 1, -1, -1):
        block, inverse, across = blocks[3 * level : 3 * level + 3]
        downward = (across[...] + dot(downward, block[...]) * inverse[...]).astype(BF16)
    at = 0
    writes = []
    for near in nears:
        first = at
        for leaf in range(near.shape[0]):
            here = slice(at, at + LEAF)
            made[:, here] = near[leaf] + dot(downward, base_block[:, here]) * base_inverse[:, here]
            at += LEAF
        here = slice(first, at)
        writes.append(
            pltpu.make_async_copy(made.at[:, here], out.at[:, here], sems.at[len(writes)])
        )
        writes[-1].start()
    for write in writes:
        write.wait()


def swapped(node, bit):
    total = lax.axis_size("inner") * lax.axis_size("outer")
    return lax.ppermute(node, ("outer", "inner"), [(i, i ^ (1 << bit)) for i in range(total)])


def body(points, charges, near_leaves, skel_device, skel_tree):
    ring = ("outer", "inner")
    total = lax.axis_size("inner") * lax.axis_size("outer")
    levels = total.bit_length() - 1
    width = points.shape[1]
    leaves, turns = near_leaves.shape
    count = skel_device.shape[1]
    tree = jnp.transpose(skel_tree, (1, 0, 2))
    ahead = [(i, (i + 1) % total) for i in range(total)]
    back = [((i + 1) % total, i) for i in range(total)]
    before_x = lax.ppermute(points, ring, ahead)
    after_x = lax.ppermute(points, ring, back)
    before_q = lax.ppermute(charges, ring, ahead)
    after_q = lax.ppermute(charges, ring, back)

    square = pltpu.VMEM((count, count), BF16)
    line = pltpu.VMEM((1, count), F32)
    side_out = ((NRHS, count), F32)
    node_out = ((DIM + NRHS, count), BF16)
    block_out = [((count, count), BF16), ((1, count), F32)]

    node, base_block, base_inverse, own_x, own_q, rights, tree, ids = call(
        base_kernel,
        [
            node_out,
            ((count, width), BF16),
            ((1, width), F32),
            (points.shape, BF16),
            (charges.shape, BF16),
            ((leaves, DEPTH, LEAF), BF16),
            ((tree.shape[0], count), jnp.int32),
            ((leaves, turns), jnp.int32),
        ],
        (points, charges, tree, skel_device, near_leaves),
        "base",
        [
            pltpu.VMEM(tree.shape, jnp.int32),
            pltpu.VMEM(skel_device.shape, jnp.int32),
            pltpu.SemaphoreType.DMA((5,)),
        ],
        spaces={i: pltpu.HBM for i in range(5)},
        out_spaces={7: pltpu.SMEM},
        flops=2 * width * count * (DEPTH + NRHS),
    )
    chunks = [0] + [leaves * (i + 1) // (levels - 1) - leaves * i // (levels - 1) for i in range(levels - 1)]
    sources_out = [((3 * leaves, LEAF, DEPTH), BF16), ((3 * leaves, NRHS, LEAF), BF16)]
    start = 0
    records = []
    nears = []
    pending = None
    for level in range(levels):
        sibling = swapped(node, level)
        if level == 0:
            own_x, node = lax.optimization_barrier((own_x, node))
            lefts, loads = call(own_kernel, sources_out, (own_x, own_q), "own", flops=10**8)
            lefts, sibling = lax.optimization_barrier((lefts, sibling))
        else:
            chunk = chunks[level]
            lefts, node = lax.optimization_barrier((lefts, node))
            if level == 1:
                lefts, loads = call(
                    halo_kernel,
                    sources_out,
                    (before_x, after_x, before_q, after_q, lefts, loads),
                    "halo",
                    aliases={4: 0, 5: 1},
                    flops=10**9,
                )
            part, side = call(
                functools.partial(near_kernel, start, chunk),
                [((chunk, NRHS, LEAF), F32), side_out],
                (ids, lefts, rights, loads, *pending),
                "near",
                [pltpu.VMEM((turns, LEAF, LEAF), BF16), square],
                spaces={0: pltpu.SMEM},
                flops=2 * chunk * LEAF * turns * LEAF * (DEPTH + NRHS),
            )
            start += chunk
            part, sibling = lax.optimization_barrier((part, sibling))
            nears.append(part)
            records[-1].append(side)
        if level < levels - 1:
            following, block, inverse = call(
                functools.partial(climb_kernel, level),
                [node_out, *block_out],
                (tree, node, sibling),
                "climb",
                [square, line],
                flops=2 * 2 * count * count * (DEPTH + NRHS),
            )
            records.append([block, inverse])
            pending = (node, sibling)
            node = following
    kept = [array for record in records for array in record]
    [potential] = call(
        functools.partial(down_kernel, levels - 1),
        [((NRHS, width), F32)],
        (node, sibling, *kept, base_block, base_inverse, *nears),
        "down",
        [
            square,
            pltpu.VMEM(*side_out),
            pltpu.VMEM((NRHS, width), F32),
            pltpu.SemaphoreType.DMA((len(nears),)),
        ],
        out_spaces={0: pl.ANY},
        flops=2 * width * count * NRHS,
    )
    return potential


def solution(mesh):
    return jax.shard_map(
        body,
        mesh=mesh,
        in_specs=(
            P(None, ("outer", "inner")),
            P(None, ("outer", "inner")),
            P(("outer", "inner"), None),
            P(("outer", "inner"), None),
            P(("outer", "inner"), None, None),
        ),
        out_specs=P(None, ("outer", "inner")),
        check_vma=False,
    )
```

time: 88 us -> 73.5 us (0.84)
  starting transfers between devices: 36.3 us -> 22.6 us
  waiting for transfers between devices: 5.47 us -> 15.7 us
  local copies, waits for them, and re-layouts: 7.25 us -> 0 us
  Pallas kernels: 38.6 us -> 34.8 us
    ppermute x12 -> x8, starting transfers between devices: 23.2 us -> 9.54 us  [swapped(): lax.ppermute(node, ('outer', 'inner'), [(i, i ^ 1 << bit) for i in range(...]
    ppermute x12 -> x8, waiting for transfers between devices: 5.46 us -> 15.6 us  [swapped(): lax.ppermute(node, ('outer', 'inner'), [(i, i ^ 1 << bit) for i in range(...]
    unnamed x17 -> x0, local copies, waits for them, and re-layouts: 7.25 us -> none
    pallas_call x10 -> x18, Pallas kernels: 38.6 us -> 34.8 us  [call(): pl.pallas_call(kernel, out_shape=[pltpu.SMEM(s, t) if out_spaces.get(i) i...]
  transfers between devices with their start and end apart: 16 -> 12, of which waited for: 2 -> 8; matrix products, arithmetic and copies ran while one was open for 1% -> 0% of each run, Pallas kernels for 30% -> 35%
where the time goes in v2:
time: 73.5 us; the launch traced here: 73.4 us
  Pallas kernels  34.8 us (47%)
  starting transfers between devices  22.6 us (31%)
  waiting for transfers between devices  15.7 us (21%)
    pallas_call x18, Pallas kernels, call(): pl.pallas_call(kernel, out_shape=[pltpu.SMEM(s, t) if out_spaces.get(i) i...  34.8 us
    ppermute x8, waiting for transfers between devices, swapped(): lax.ppermute(node, ('outer', 'inner'), [(i, i ^ 1 << bit) for i in range(...  15.6 us
    ppermute x8, starting transfers between devices, swapped(): lax.ppermute(node, ('outer', 'inner'), [(i, i ^ 1 << bit) for i in range(...  9.54 us
    ppermute x1, starting transfers between devices, body(): after_q = lax.ppermute(charges, ring, back)  6.55 us
    ppermute x1, starting transfers between devices, body(): after_x = lax.ppermute(points, ring, back)  6.55 us
  transfers between devices with their start and end apart: 12, of which 8 were waited for; matrix products, arithmetic and copies ran while one was open for 0% of the time, Pallas kernels for 35%

profile of v2, /device:TPU:2, one launch (start us, length us, event | category | flops | bytes accessed | tf_op | source)
XLA Modules:
  0.0 73.4 jit_solution(5296690218025518192)
XLA Ops:
  0.0 6.5 %collective-permute-start.3 = (bf16[64,4096]{1,0:T(8,128)(2,1)}, bf16[64,4096]{1,0:T(8,128)(2,1)S(1)}, u32[]{:S(2)}, u32[]{:S(2)}) collective-permute-start(bf16[64,4096]{1,0:T(8,128)(2,1)} %charges_in.1), channel_id=1, source_target_pairs={{1,0},{2,1},{3,2},{4,3},{5,4},{6,5},{7,6},{8,7},{9,8},{10,9},{11,1... | collective-permute-start | bytes 1572872 | tf_op jit(solution)/shard_map/ppermute | solution.py:293
  6.6 6.5 %collective-permute-start.1 = (bf16[16,4096]{1,0:T(8,128)(2,1)}, bf16[16,4096]{1,0:T(8,128)(2,1)S(1)}, u32[]{:S(2)}, u32[]{:S(2)}) collective-permute-start(bf16[16,4096]{1,0:T(8,128)(2,1)} %points_in.1), channel_id=1, source_target_pairs={{1,0},{2,1},{3,2},{4,3},{5,4},{6,5},{7,6},{8,7},{9,8},{10,9},{11,1... | collective-permute-start | bytes 393224 | tf_op jit(solution)/shard_map/ppermute | solution.py:291
  13.1 5.1 %base.1 = (bf16[80,512]{1,0:T(8,128)(2,1)S(1)}, bf16[512,4096]{1,0:T(8,128)(2,1)S(1)}, f32[1,4096]{1,0:T(1,128)S(1)}, bf16[16,4096]{1,0:T(8,128)(2,1)S(1)}, bf16...) custom-call(bf16[16,4096]{1,0:T(8,128)(2,1)} %points_in.1, ...), custom_call_target="tpu_custom_call" | custom-call | flops 402653184 | bytes 672768 | tf_op jit(solution)/shard_map/base/pallas_call | solution.py:138
  19.6 1.0 %climb.7 = (bf16[80,512]{1,0:T(8,128)(2,1)S(1)}, bf16[512,512]{1,0:T(8,128)(2,1)S(1)}, f32[1,512]{1,0:T(1,128)S(1)}) custom-call(s32[7,512]{1,0:T(8,128)S(1)} %get-tuple-element.90.tree, bf16[80,512]{1,0:T(8,128)(2,1)S(1)} %get-tuple-element.91.own, bf16[80,512]{1,0:T(8,128)(2,1)S(1)} %collective-permute-done.4.sibling), custom_call_target="tpu_custom_call" | custom-call | flops 100663296 | bytes 178176 | tf_op jit(solution)/shard_map/climb/pallas_call | solution.py:138
  21.4 2.3 %near.7 = (f32[2,64,256]{2,1,0:T(8,128)S(1)}, f32[64,512]{1,0:T(8,128)S(1)}) custom-call(s32[16,16]{1,0:T(8,128)S(4)} %get-tuple-element.98.ids, bf16[48,256,32]{2,1,0:T(8,128)(2,1)S(1)} %get-tuple-element.130.lefts, bf16[16,32,256]{2,1,0:T(8,128)(2,1)S(1)} %get-tuple-element.99.rights, bf16[48,64,256]{2,1,0:T(8,128)(2,1)S(1)} %get-tuple-element.100.loads, ...), custom_call_target="tpu_custom_call" | custom-call | flops 402653184 | bytes 2786304 | tf_op jit(solution)/shard_map/near/pallas_call | solution.py:138
  23.7 1.5 %collective-permute-done.5.sibling = bf16[80,512]{1,0:T(8,128)(2,1)S(1)} collective-permute-done((bf16[80,512]{1,0:T(8,128)(2,1)S(1)}, bf16[80,512]{1,0:T(8,128)(2,1)S(1)}, u32[]{:S(2)}, u32[]{:S(2)}) %collective-permute-start.5) | collective-permute-done | bytes 81952 | tf_op jit(solution)/shard_map/ppermute | solution.py:277
  25.2 1.0 %climb.8 = (bf16[80,512]{1,0:T(8,128)(2,1)S(1)}, bf16[512,512]{1,0:T(8,128)(2,1)S(1)}, f32[1,512]{1,0:T(1,128)S(1)}) custom-call(s32[7,512]{1,0:T(8,128)S(1)} %get-tuple-element.90.tree, bf16[80,512]{1,0:T(8,128)(2,1)S(1)} %get-tuple-element.97.own, bf16[80,512]{1,0:T(8,128)(2,1)S(1)} %collective-permute-done.5.sibling), custom_call_target="tpu_custom_call" | custom-call | flops 100663296 | bytes 178176 | tf_op jit(solution)/shard_map/climb/pallas_call | solution.py:138
  26.4 2.3 %near.8 = (f32[2,64,256]{2,1,0:T(8,128)S(1)}, f32[64,512]{1,0:T(8,128)S(1)}) custom-call(s32[16,16]{1,0:T(8,128)S(4)} %get-tuple-element.98.ids, bf16[48,256,32]{2,1,0:T(8,128)(2,1)S(1)} %get-tuple-element.130.lefts, bf16[16,32,256]{2,1,0:T(8,128)(2,1)S(1)} %get-tuple-element.99.rights, bf16[48,64,256]{2,1,0:T(8,128)(2,1)S(1)} %get-tuple-element.100.loads, ...), custom_call_target="tpu_custom_call" | custom-call | flops 402653184 | bytes 2786304 | tf_op jit(solution)/shard_map/near/pallas_call | solution.py:138
  28.7 3.6 %collective-permute-done.6.sibling = bf16[80,512]{1,0:T(8,128)(2,1)S(1)} collective-permute-done((bf16[80,512]{1,0:T(8,128)(2,1)S(1)}, bf16[80,512]{1,0:T(8,128)(2,1)S(1)}, u32[]{:S(2)}, u32[]{:S(2)}) %collective-permute-start.6) | collective-permute-done | bytes 81952 | tf_op jit(solution)/shard_map/ppermute | solution.py:277
  32.4 1.0 %climb.9 = (bf16[80,512]{1,0:T(8,128)(2,1)S(1)}, bf16[512,512]{1,0:T(8,128)(2,1)S(1)}, f32[1,512]{1,0:T(1,128)S(1)}) custom-call(s32[7,512]{1,0:T(8,128)S(1)} %get-tuple-element.90.tree, bf16[80,512]{1,0:T(8,128)(2,1)S(1)} %get-tuple-element.105.own, bf16[80,512]{1,0:T(8,128)(2,1)S(1)} %collective-permute-done.6.sibling), custom_call_target="tpu_custom_call" | custom-call | flops 100663296 | bytes 178176 | tf_op jit(solution)/shard_map/climb/pallas_call | solution.py:138
  33.4 2.3 %near.9 = (f32[2,64,256]{2,1,0:T(8,128)S(1)}, f32[64,512]{1,0:T(8,128)S(1)}) custom-call(s32[16,16]{1,0:T(8,128)S(4)} %get-tuple-element.98.ids, bf16[48,256,32]{2,1,0:T(8,128)(2,1)S(1)} %get-tuple-element.130.lefts, bf16[16,32,256]{2,1,0:T(8,128)(2,1)S(1)} %get-tuple-element.99.rights, bf16[48,64,256]{2,1,0:T(8,128)(2,1)S(1)} %get-tuple-element.100.loads, ...), custom_call_target="tpu_custom_call" | custom-call | flops 402653184 | bytes 2786304 | tf_op jit(solution)/shard_map/near/pallas_call | solution.py:138
  35.8 2.1 %collective-permute-done.7.sibling = bf16[80,512]{1,0:T(8,128)(2,1)S(1)} collective-permute-done((bf16[80,512]{1,0:T(8,128)(2,1)S(1)}, bf16[80,512]{1,0:T(8,128)(2,1)S(1)}, u32[]{:S(2)}, u32[]{:S(2)}) %collective-permute-start.7) | collective-permute-done | bytes 81952 | tf_op jit(solution)/shard_map/ppermute | solution.py:277
  37.9 1.0 %climb.10 = (bf16[80,512]{1,0:T(8,128)(2,1)S(1)}, bf16[512,512]{1,0:T(8,128)(2,1)S(1)}, f32[1,512]{1,0:T(1,128)S(1)}) custom-call(s32[7,512]{1,0:T(8,128)S(1)} %get-tuple-element.90.tree, bf16[80,512]{1,0:T(8,128)(2,1)S(1)} %get-tuple-element.110.own, bf16[80,512]{1,0:T(8,128)(2,1)S(1)} %collective-permute-done.7.sibling), custom_call_target="tpu_custom_call" | custom-call | flops 100663296 | bytes 178176 | tf_op jit(solution)/shard_map/climb/pallas_call | solution.py:138
  38.9 3.5 %near.10 = (f32[3,64,256]{2,1,0:T(8,128)S(1)}, f32[64,512]{1,0:T(8,128)S(1)}) custom-call(s32[16,16]{1,0:T(8,128)S(4)} %get-tuple-element.98.ids, bf16[48,256,32]{2,1,0:T(8,128)(2,1)S(1)} %get-tuple-element.130.lefts, bf16[16,32,256]{2,1,0:T(8,128)(2,1)S(1)} %get-tuple-element.99.rights, bf16[48,64,256]{2,1,0:T(8,128)(2,1)S(1)} %get-tuple-element.100.loads, ...), custom_call_target="tpu_custom_call" | custom-call | flops 603979776 | bytes 2786304 | tf_op jit(solution)/shard_map/near/pallas_call | solution.py:138
  42.5 2.1 %collective-permute-done.8.sibling = bf16[80,512]{1,0:T(8,128)(2,1)S(1)} collective-permute-done((bf16[80,512]{1,0:T(8,128)(2,1)S(1)}, bf16[80,512]{1,0:T(8,128)(2,1)S(1)}, u32[]{:S(2)}, u32[]{:S(2)}) %collective-permute-start.8) | collective-permute-done | bytes 81952 | tf_op jit(solution)/shard_map/ppermute | solution.py:277
  44.6 1.0 %climb.11 = (bf16[80,512]{1,0:T(8,128)(2,1)S(1)}, bf16[512,512]{1,0:T(8,128)(2,1)S(1)}, f32[1,512]{1,0:T(1,128)S(1)}) custom-call(s32[7,512]{1,0:T(8,128)S(1)} %get-tuple-element.90.tree, bf16[80,512]{1,0:T(8,128)(2,1)S(1)} %get-tuple-element.115.own, bf16[80,512]{1,0:T(8,128)(2,1)S(1)} %collective-permute-done.8.sibling), custom_call_target="tpu_custom_call" | custom-call | flops 100663296 | bytes 178176 | tf_op jit(solution)/shard_map/climb/pallas_call | solution.py:138
  45.6 4.9 %collective-permute-start.9 = (bf16[80,512]{1,0:T(8,128)(2,1)S(1)}, bf16[80,512]{1,0:T(8,128)(2,1)S(1)}, u32[]{:S(2)}, u32[]{:S(2)}) collective-permute-start(bf16[80,512]{1,0:T(8,128)(2,1)S(1)} %get-tuple-element.120.own), channel_id=1, source_target_pairs={{0,32},{1,33},{2,34},{3,35},{4,36},{5,37},{6,38},{7,39},{8,40},{9,... | collective-permute-start | bytes 245768 | tf_op jit(solution)/shard_map/ppermute | solution.py:277
  50.4 2.3 %near.11 = (f32[2,64,256]{2,1,0:T(8,128)S(1)}, f32[64,512]{1,0:T(8,128)S(1)}) custom-call(s32[16,16]{1,0:T(8,128)S(4)} %get-tuple-element.98.ids, bf16[48,256,32]{2,1,0:T(8,128)(2,1)S(1)} %get-tuple-element.130.lefts, bf16[16,32,256]{2,1,0:T(8,128)(2,1)S(1)} %get-tuple-element.99.rights, bf16[48,64,256]{2,1,0:T(8,128)(2,1)S(1)} %get-tuple-element.100.loads, ...), custom_call_target="tpu_custom_call" | custom-call | flops 402653184 | bytes 2786304 | tf_op jit(solution)/shard_map/near/pallas_call | solution.py:138
  53.6 1.0 %climb.12 = (bf16[80,512]{1,0:T(8,128)(2,1)S(1)}, bf16[512,512]{1,0:T(8,128)(2,1)S(1)}, f32[1,512]{1,0:T(1,128)S(1)}) custom-call(s32[7,512]{1,0:T(8,128)S(1)} %get-tuple-element.90.tree, bf16[80,512]{1,0:T(8,128)(2,1)S(1)} %get-tuple-element.120.own, bf16[80,512]{1,0:T(8,128)(2,1)S(1)} %collective-permute-done.9.sibling), custom_call_target="tpu_custom_call" | custom-call | flops 100663296 | bytes 178176 | tf_op jit(solution)/shard_map/climb/pallas_call | solution.py:138
  54.7 2.3 %near.12 = (f32[2,64,256]{2,1,0:T(8,128)S(1)}, f32[64,512]{1,0:T(8,128)S(1)}) custom-call(s32[16,16]{1,0:T(8,128)S(4)} %get-tuple-element.98.ids, bf16[48,256,32]{2,1,0:T(8,128)(2,1)S(1)} %get-tuple-element.130.lefts, bf16[16,32,256]{2,1,0:T(8,128)(2,1)S(1)} %get-tuple-element.99.rights, bf16[48,64,256]{2,1,0:T(8,128)(2,1)S(1)} %get-tuple-element.100.loads, ...), custom_call_target="tpu_custom_call" | custom-call | flops 402653184 | bytes 2786304 | tf_op jit(solution)/shard_map/near/pallas_call | solution.py:138
  57.0 3.6 %collective-permute-done.10.sibling = bf16[80,512]{1,0:T(8,128)(2,1)S(1)} collective-permute-done((bf16[80,512]{1,0:T(8,128)(2,1)S(1)}, bf16[80,512]{1,0:T(8,128)(2,1)S(1)}, u32[]{:S(2)}, u32[]{:S(2)}) %collective-permute-start.10) | collective-permute-done | bytes 81952 | tf_op jit(solution)/shard_map/ppermute | solution.py:277
  61.6 4.0 %collective-permute-start.11 = (bf16[80,512]{1,0:T(8,128)(2,1)S(1)}, bf16[80,512]{1,0:T(8,128)(2,1)S(1)}, u32[]{:S(2)}, u32[]{:S(2)}) collective-permute-start(bf16[80,512]{1,0:T(8,128)(2,1)S(1)} %get-tuple-element.129.own), channel_id=1, source_target_pairs={{0,128},{1,129},{2,130},{3,131},{4,132},{5,133},{6,134},{7,135},{8... | collective-permute-start | bytes 245768 | tf_op jit(solution)/shard_map/ppermute | solution.py:277
  65.6 3.5 %near.13 = (f32[3,64,256]{2,1,0:T(8,128)S(1)}, f32[64,512]{1,0:T(8,128)S(1)}) custom-call(s32[16,16]{1,0:T(8,128)S(4)} %get-tuple-element.98.ids, bf16[48,256,32]{2,1,0:T(8,128)(2,1)S(1)} %get-tuple-element.130.lefts, bf16[16,32,256]{2,1,0:T(8,128)(2,1)S(1)} %get-tuple-element.99.rights, bf16[48,64,256]{2,1,0:T(8,128)(2,1)S(1)} %get-tuple-element.100.loads, ...), custom_call_target="tpu_custom_call" | custom-call | flops 603979776 | bytes 2786304 | tf_op jit(solution)/shard_map/near/pallas_call | solution.py:138
  70.1 3.2 %down.1 = f32[64,4096]{1,0:T(8,128)} custom-call(bf16[80,512]{1,0:T(8,128)(2,1)S(1)} %get-tuple-element.129.own, bf16[80,512]{1,0:T(8,128)(2,1)S(1)} %collective-permute-done.11.sibling, bf16[512,512]{1,0:T(8,128)(2,1)S(1)} %get-tuple-element.133.refs_0_, f32[1,512]{1,0:T(1,128)S(1)} %get-tuple-element.134.refs_1_, ...), custom_call_target="tpu_custom_call" | custom-call | flops 268435456 | bytes 10024960 | tf_op jit(solution)/shard_map/down/pallas_call | solution.py:138
  (18 shorter events, 5.5 us)
Async XLA Ops:
  0.0 20.7 %collective-permute-start.2 = (bf16[64,4096]{1,0:T(8,128)(2,1)}, bf16[64,4096]{1,0:T(8,128)(2,1)S(1)}, u32[]{:S(2)}, u32[]{:S(2)}) collective-permute-start(bf16[64,4096]{1,0:T(8,128)(2,1)} %charges_in.1), channel_id=1, source_target_pairs={{0,1},{1,2},{2,3},{3,4},{4,5},{5,6},{6,7},{7,8},{8,9},{9,10},{10,1... | collective-permute-start | bytes 1572872 | tf_op jit(solution)/shard_map/ppermute | solution.py:292
  0.0 20.7 %collective-permute-start.3 = (bf16[64,4096]{1,0:T(8,128)(2,1)}, bf16[64,4096]{1,0:T(8,128)(2,1)S(1)}, u32[]{:S(2)}, u32[]{:S(2)}) collective-permute-start(bf16[64,4096]{1,0:T(8,128)(2,1)} %charges_in.1), channel_id=1, source_target_pairs={{1,0},{2,1},{3,2},{4,3},{5,4},{6,5},{7,6},{8,7},{9,8},{10,9},{11,1... | collective-permute-start | bytes 1572872 | tf_op jit(solution)/shard_map/ppermute | solution.py:293
  6.6 14.1 %collective-permute-start = (bf16[16,4096]{1,0:T(8,128)(2,1)}, bf16[16,4096]{1,0:T(8,128)(2,1)S(1)}, u32[]{:S(2)}, u32[]{:S(2)}) collective-permute-start(bf16[16,4096]{1,0:T(8,128)(2,1)} %points_in.1), channel_id=1, source_target_pairs={{0,1},{1,2},{2,3},{3,4},{4,5},{5,6},{6,7},{7,8},{8,9},{9,10},{10,1... | collective-permute-start | bytes 393224 | tf_op jit(solution)/shard_map/ppermute | solution.py:290
  6.6 14.1 %collective-permute-start.1 = (bf16[16,4096]{1,0:T(8,128)(2,1)}, bf16[16,4096]{1,0:T(8,128)(2,1)S(1)}, u32[]{:S(2)}, u32[]{:S(2)}) collective-permute-start(bf16[16,4096]{1,0:T(8,128)(2,1)} %points_in.1), channel_id=1, source_target_pairs={{1,0},{2,1},{3,2},{4,3},{5,4},{6,5},{7,6},{8,7},{9,8},{10,9},{11,1... | collective-permute-start | bytes 393224 | tf_op jit(solution)/shard_map/ppermute | solution.py:291
  18.2 1.4 %collective-permute-start.4 = (bf16[80,512]{1,0:T(8,128)(2,1)S(1)}, bf16[80,512]{1,0:T(8,128)(2,1)S(1)}, u32[]{:S(2)}, u32[]{:S(2)}) collective-permute-start(bf16[80,512]{1,0:T(8,128)(2,1)S(1)} %get-tuple-element.91.own), channel_id=1, source_target_pairs={{0,1},{1,0},{2,3},{3,2},{4,5},{5,4},{6,7},{7,6},{8,9},{9,8},{10,11... | collective-permute-start | bytes 245768 | tf_op jit(solution)/shard_map/ppermute | solution.py:277
  20.6 4.6 %collective-permute-start.5 = (bf16[80,512]{1,0:T(8,128)(2,1)S(1)}, bf16[80,512]{1,0:T(8,128)(2,1)S(1)}, u32[]{:S(2)}, u32[]{:S(2)}) collective-permute-start(bf16[80,512]{1,0:T(8,128)(2,1)S(1)} %get-tuple-element.97.own), channel_id=1, source_target_pairs={{0,2},{1,3},{2,0},{3,1},{4,6},{5,7},{6,4},{7,5},{8,10},{9,11},{10,... | collective-permute-start | bytes 245768 | tf_op jit(solution)/shard_map/ppermute | solution.py:277
  26.1 6.2 %collective-permute-start.6 = (bf16[80,512]{1,0:T(8,128)(2,1)S(1)}, bf16[80,512]{1,0:T(8,128)(2,1)S(1)}, u32[]{:S(2)}, u32[]{:S(2)}) collective-permute-start(bf16[80,512]{1,0:T(8,128)(2,1)S(1)} %get-tuple-element.105.own), channel_id=1, source_target_pairs={{0,4},{1,5},{2,6},{3,7},{4,0},{5,1},{6,2},{7,3},{8,12},{9,13},{10,... | collective-permute-start | bytes 245768 | tf_op jit(solution)/shard_map/ppermute | solution.py:277
  33.3 4.5 %collective-permute-start.7 = (bf16[80,512]{1,0:T(8,128)(2,1)S(1)}, bf16[80,512]{1,0:T(8,128)(2,1)S(1)}, u32[]{:S(2)}, u32[]{:S(2)}) collective-permute-start(bf16[80,512]{1,0:T(8,128)(2,1)S(1)} %get-tuple-element.110.own), channel_id=1, source_target_pairs={{0,8},{1,9},{2,10},{3,11},{4,12},{5,13},{6,14},{7,15},{8,0},{9,1},... | collective-permute-start | bytes 245768 | tf_op jit(solution)/shard_map/ppermute | solution.py:277
  38.8 5.7 %collective-permute-start.8 = (bf16[80,512]{1,0:T(8,128)(2,1)S(1)}, bf16[80,512]{1,0:T(8,128)(2,1)S(1)}, u32[]{:S(2)}, u32[]{:S(2)}) collective-permute-start(bf16[80,512]{1,0:T(8,128)(2,1)S(1)} %get-tuple-element.115.own), channel_id=1, source_target_pairs={{0,16},{1,17},{2,18},{3,19},{4,20},{5,21},{6,22},{7,23},{8,24},{9,... | collective-permute-start | bytes 245768 | tf_op jit(solution)/shard_map/ppermute | solution.py:277
  45.6 8.1 %collective-permute-start.9 = (bf16[80,512]{1,0:T(8,128)(2,1)S(1)}, bf16[80,512]{1,0:T(8,128)(2,1)S(1)}, u32[]{:S(2)}, u32[]{:S(2)}) collective-permute-start(bf16[80,512]{1,0:T(8,128)(2,1)S(1)} %get-tuple-element.120.own), channel_id=1, source_target_pairs={{0,32},{1,33},{2,34},{3,35},{4,36},{5,37},{6,38},{7,39},{8,40},{9,... | collective-permute-start | bytes 245768 | tf_op jit(solution)/shard_map/ppermute | solution.py:277
  54.6 6.0 %collective-permute-start.10 = (bf16[80,512]{1,0:T(8,128)(2,1)S(1)}, bf16[80,512]{1,0:T(8,128)(2,1)S(1)}, u32[]{:S(2)}, u32[]{:S(2)}) collective-permute-start(bf16[80,512]{1,0:T(8,128)(2,1)S(1)} %get-tuple-element.125.own), channel_id=1, source_target_pairs={{0,64},{1,65},{2,66},{3,67},{4,68},{5,69},{6,70},{7,71},{8,72},{9,... | collective-permute-start | bytes 245768 | tf_op jit(solution)/shard_map/ppermute | solution.py:277
  61.6 8.4 %collective-permute-start.11 = (bf16[80,512]{1,0:T(8,128)(2,1)S(1)}, bf16[80,512]{1,0:T(8,128)(2,1)S(1)}, u32[]{:S(2)}, u32[]{:S(2)}) collective-permute-start(bf16[80,512]{1,0:T(8,128)(2,1)S(1)} %get-tuple-element.129.own), channel_id=1, source_target_pairs={{0,128},{1,129},{2,130},{3,131},{4,132},{5,133},{6,134},{7,135},{8... | collective-permute-start | bytes 245768 | tf_op jit(solution)/shard_map/ppermute | solution.py:277

commit v3 on v2

--- a/solution.py
+++ b/solution.py
@@ -19,6 +19,7 @@
 
 LOG2E = 1.0 / math.log(2.0)
 VMEM_LIMIT = 24 * 2**20
+REACH = (0, 0, 2, 0, 0, 0, 32, 16)
 
 
 def split_rows(x):
@@ -274,7 +275,8 @@
 
 def swapped(node, bit):
     total = lax.axis_size("inner") * lax.axis_size("outer")
-    return lax.ppermute(node, ("outer", "inner"), [(i, i ^ (1 << bit)) for i in range(total)])
+    mask = (1 << bit) | (REACH[bit] if bit < len(REACH) else 0)
+    return lax.ppermute(node, ("outer", "inner"), [(i, i ^ mask) for i in range(total)])
 
 
 def body(points, charges, near_leaves, skel_device, skel_tree):

time: 73.5 us -> 70.6 us (0.961); the launches traced: 73.4 us -> 69.2 us
  waiting for transfers between devices: 15.7 us -> 12.1 us
    ppermute x8, waiting for transfers between devices: 15.6 us -> 12.1 us  [swapped(): lax.ppermute(node, ('outer', 'inner'), [(i, i ^ mask) for i in range(tota...]
    ppermute x8, starting transfers between devices: 9.54 us -> 8.78 us  [swapped(): lax.ppermute(node, ('outer', 'inner'), [(i, i ^ mask) for i in range(tota...]
  transfers between devices with their start and end apart: 12 -> 12, of which waited for: 8 -> 7; matrix products, arithmetic and copies ran while one was open for 0% -> 0% of each run, Pallas kernels for 35% -> 37%
where the time goes in v3:
time: 70.6 us; the launch traced here: 69.2 us
  Pallas kernels  34.8 us (49%)
  starting transfers between devices  21.9 us (31%)
  waiting for transfers between devices  12.1 us (17%)
    pallas_call x18, Pallas kernels, call(): pl.pallas_call(kernel, out_shape=[pltpu.SMEM(s, t) if out_spaces.get(i) i...  34.8 us
    ppermute x8, waiting for transfers between devices, swapped(): lax.ppermute(node, ('outer', 'inner'), [(i, i ^ mask) for i in range(tota...  12.1 us
    ppermute x8, starting transfers between devices, swapped(): lax.ppermute(node, ('outer', 'inner'), [(i, i ^ mask) for i in range(tota...  8.78 us
    ppermute x1, starting transfers between devices, body(): after_q = lax.ppermute(charges, ring, back)  6.55 us
    ppermute x1, starting transfers between devices, body(): after_x = lax.ppermute(points, ring, back)  6.55 us
  transfers between devices with their start and end apart: 12, of which 7 were waited for; matrix products, arithmetic and copies ran while one was open for 0% of the time, Pallas kernels for 37%

profile of v3, /device:TPU:2, one launch (start us, length us, event | category | flops | bytes accessed | tf_op | source)
XLA Modules:
  0.0 69.2 jit_solution(15434597521448793005)
XLA Ops:
  0.0 6.5 %collective-permute-start.3 = (bf16[64,4096]{1,0:T(8,128)(2,1)}, bf16[64,4096]{1,0:T(8,128)(2,1)S(1)}, u32[]{:S(2)}, u32[]{:S(2)}) collective-permute-start(bf16[64,4096]{1,0:T(8,128)(2,1)} %charges_in.1), channel_id=1, source_target_pairs={{1,0},{2,1},{3,2},{4,3},{5,4},{6,5},{7,6},{8,7},{9,8},{10,9},{11,1... | collective-permute-start | bytes 1572872 | tf_op jit(solution)/shard_map/ppermute | solution.py:295
  6.6 6.5 %collective-permute-start.1 = (bf16[16,4096]{1,0:T(8,128)(2,1)}, bf16[16,4096]{1,0:T(8,128)(2,1)S(1)}, u32[]{:S(2)}, u32[]{:S(2)}) collective-permute-start(bf16[16,4096]{1,0:T(8,128)(2,1)} %points_in.1), channel_id=1, source_target_pairs={{1,0},{2,1},{3,2},{4,3},{5,4},{6,5},{7,6},{8,7},{9,8},{10,9},{11,1... | collective-permute-start | bytes 393224 | tf_op jit(solution)/shard_map/ppermute | solution.py:293
  13.1 5.1 %base.1 = (bf16[80,512]{1,0:T(8,128)(2,1)S(1)}, bf16[512,4096]{1,0:T(8,128)(2,1)S(1)}, f32[1,4096]{1,0:T(1,128)S(1)}, bf16[16,4096]{1,0:T(8,128)(2,1)S(1)}, bf16...) custom-call(bf16[16,4096]{1,0:T(8,128)(2,1)} %points_in.1, ...), custom_call_target="tpu_custom_call" | custom-call | flops 402653184 | bytes 672768 | tf_op jit(solution)/shard_map/base/pallas_call | solution.py:139
  19.6 1.0 %climb.7 = (bf16[80,512]{1,0:T(8,128)(2,1)S(1)}, bf16[512,512]{1,0:T(8,128)(2,1)S(1)}, f32[1,512]{1,0:T(1,128)S(1)}) custom-call(s32[7,512]{1,0:T(8,128)S(1)} %get-tuple-element.90.tree, bf16[80,512]{1,0:T(8,128)(2,1)S(1)} %get-tuple-element.91.own, bf16[80,512]{1,0:T(8,128)(2,1)S(1)} %collective-permute-done.4.sibling), custom_call_target="tpu_custom_call" | custom-call | flops 100663296 | bytes 178176 | tf_op jit(solution)/shard_map/climb/pallas_call | solution.py:139
  21.4 2.3 %near.7 = (f32[2,64,256]{2,1,0:T(8,128)S(1)}, f32[64,512]{1,0:T(8,128)S(1)}) custom-call(s32[16,16]{1,0:T(8,128)S(4)} %get-tuple-element.98.ids, bf16[48,256,32]{2,1,0:T(8,128)(2,1)S(1)} %get-tuple-element.130.lefts, bf16[16,32,256]{2,1,0:T(8,128)(2,1)S(1)} %get-tuple-element.99.rights, bf16[48,64,256]{2,1,0:T(8,128)(2,1)S(1)} %get-tuple-element.100.loads, ...), custom_call_target="tpu_custom_call" | custom-call | flops 402653184 | bytes 2786304 | tf_op jit(solution)/shard_map/near/pallas_call | solution.py:139
  23.7 1.5 %collective-permute-done.5.sibling = bf16[80,512]{1,0:T(8,128)(2,1)S(1)} collective-permute-done((bf16[80,512]{1,0:T(8,128)(2,1)S(1)}, bf16[80,512]{1,0:T(8,128)(2,1)S(1)}, u32[]{:S(2)}, u32[]{:S(2)}) %collective-permute-start.5) | collective-permute-done | bytes 81952 | tf_op jit(solution)/shard_map/ppermute | solution.py:279
  25.2 1.0 %climb.8 = (bf16[80,512]{1,0:T(8,128)(2,1)S(1)}, bf16[512,512]{1,0:T(8,128)(2,1)S(1)}, f32[1,512]{1,0:T(1,128)S(1)}) custom-call(s32[7,512]{1,0:T(8,128)S(1)} %get-tuple-element.90.tree, bf16[80,512]{1,0:T(8,128)(2,1)S(1)} %get-tuple-element.97.own, bf16[80,512]{1,0:T(8,128)(2,1)S(1)} %collective-permute-done.5.sibling), custom_call_target="tpu_custom_call" | custom-call | flops 100663296 | bytes 178176 | tf_op jit(solution)/shard_map/climb/pallas_call | solution.py:139
  26.4 2.3 %near.8 = (f32[2,64,256]{2,1,0:T(8,128)S(1)}, f32[64,512]{1,0:T(8,128)S(1)}) custom-call(s32[16,16]{1,0:T(8,128)S(4)} %get-tuple-element.98.ids, bf16[48,256,32]{2,1,0:T(8,128)(2,1)S(1)} %get-tuple-element.130.lefts, bf16[16,32,256]{2,1,0:T(8,128)(2,1)S(1)} %get-tuple-element.99.rights, bf16[48,64,256]{2,1,0:T(8,128)(2,1)S(1)} %get-tuple-element.100.loads, ...), custom_call_target="tpu_custom_call" | custom-call | flops 402653184 | bytes 2786304 | tf_op jit(solution)/shard_map/near/pallas_call | solution.py:139
  28.7 3.3 %collective-permute-done.6.sibling = bf16[80,512]{1,0:T(8,128)(2,1)S(1)} collective-permute-done((bf16[80,512]{1,0:T(8,128)(2,1)S(1)}, bf16[80,512]{1,0:T(8,128)(2,1)S(1)}, u32[]{:S(2)}, u32[]{:S(2)}) %collective-permute-start.6) | collective-permute-done | bytes 81952 | tf_op jit(solution)/shard_map/ppermute | solution.py:279
  32.1 1.0 %climb.9 = (bf16[80,512]{1,0:T(8,128)(2,1)S(1)}, bf16[512,512]{1,0:T(8,128)(2,1)S(1)}, f32[1,512]{1,0:T(1,128)S(1)}) custom-call(s32[7,512]{1,0:T(8,128)S(1)} %get-tuple-element.90.tree, bf16[80,512]{1,0:T(8,128)(2,1)S(1)} %get-tuple-element.105.own, bf16[80,512]{1,0:T(8,128)(2,1)S(1)} %collective-permute-done.6.sibling), custom_call_target="tpu_custom_call" | custom-call | flops 100663296 | bytes 178176 | tf_op jit(solution)/shard_map/climb/pallas_call | solution.py:139
  33.1 2.3 %near.9 = (f32[2,64,256]{2,1,0:T(8,128)S(1)}, f32[64,512]{1,0:T(8,128)S(1)}) custom-call(s32[16,16]{1,0:T(8,128)S(4)} %get-tuple-element.98.ids, bf16[48,256,32]{2,1,0:T(8,128)(2,1)S(1)} %get-tuple-element.130.lefts, bf16[16,32,256]{2,1,0:T(8,128)(2,1)S(1)} %get-tuple-element.99.rights, bf16[48,64,256]{2,1,0:T(8,128)(2,1)S(1)} %get-tuple-element.100.loads, ...), custom_call_target="tpu_custom_call" | custom-call | flops 402653184 | bytes 2786304 | tf_op jit(solution)/shard_map/near/pallas_call | solution.py:139
  35.5 2.1 %collective-permute-done.7.sibling = bf16[80,512]{1,0:T(8,128)(2,1)S(1)} collective-permute-done((bf16[80,512]{1,0:T(8,128)(2,1)S(1)}, bf16[80,512]{1,0:T(8,128)(2,1)S(1)}, u32[]{:S(2)}, u32[]{:S(2)}) %collective-permute-start.7) | collective-permute-done | bytes 81952 | tf_op jit(solution)/shard_map/ppermute | solution.py:279
  37.6 1.0 %climb.10 = (bf16[80,512]{1,0:T(8,128)(2,1)S(1)}, bf16[512,512]{1,0:T(8,128)(2,1)S(1)}, f32[1,512]{1,0:T(1,128)S(1)}) custom-call(s32[7,512]{1,0:T(8,128)S(1)} %get-tuple-element.90.tree, bf16[80,512]{1,0:T(8,128)(2,1)S(1)} %get-tuple-element.110.own, bf16[80,512]{1,0:T(8,128)(2,1)S(1)} %collective-permute-done.7.sibling), custom_call_target="tpu_custom_call" | custom-call | flops 100663296 | bytes 178176 | tf_op jit(solution)/shard_map/climb/pallas_call | solution.py:139
  38.7 3.5 %near.10 = (f32[3,64,256]{2,1,0:T(8,128)S(1)}, f32[64,512]{1,0:T(8,128)S(1)}) custom-call(s32[16,16]{1,0:T(8,128)S(4)} %get-tuple-element.98.ids, bf16[48,256,32]{2,1,0:T(8,128)(2,1)S(1)} %get-tuple-element.130.lefts, bf16[16,32,256]{2,1,0:T(8,128)(2,1)S(1)} %get-tuple-element.99.rights, bf16[48,64,256]{2,1,0:T(8,128)(2,1)S(1)} %get-tuple-element.100.loads, ...), custom_call_target="tpu_custom_call" | custom-call | flops 603979776 | bytes 2786304 | tf_op jit(solution)/shard_map/near/pallas_call | solution.py:139
  42.2 2.1 %collective-permute-done.8.sibling = bf16[80,512]{1,0:T(8,128)(2,1)S(1)} collective-permute-done((bf16[80,512]{1,0:T(8,128)(2,1)S(1)}, bf16[80,512]{1,0:T(8,128)(2,1)S(1)}, u32[]{:S(2)}, u32[]{:S(2)}) %collective-permute-start.8) | collective-permute-done | bytes 81952 | tf_op jit(solution)/shard_map/ppermute | solution.py:279
  45.3 4.9 %collective-permute-start.9 = (bf16[80,512]{1,0:T(8,128)(2,1)S(1)}, bf16[80,512]{1,0:T(8,128)(2,1)S(1)}, u32[]{:S(2)}, u32[]{:S(2)}) collective-permute-start(bf16[80,512]{1,0:T(8,128)(2,1)S(1)} %get-tuple-element.120.own), channel_id=1, source_target_pairs={{0,32},{1,33},{2,34},{3,35},{4,36},{5,37},{6,38},{7,39},{8,40},{9,... | collective-permute-start | bytes 245768 | tf_op jit(solution)/shard_map/ppermute | solution.py:279
  50.1 2.3 %near.11 = (f32[2,64,256]{2,1,0:T(8,128)S(1)}, f32[64,512]{1,0:T(8,128)S(1)}) custom-call(s32[16,16]{1,0:T(8,128)S(4)} %get-tuple-element.98.ids, bf16[48,256,32]{2,1,0:T(8,128)(2,1)S(1)} %get-tuple-element.130.lefts, bf16[16,32,256]{2,1,0:T(8,128)(2,1)S(1)} %get-tuple-element.99.rights, bf16[48,64,256]{2,1,0:T(8,128)(2,1)S(1)} %get-tuple-element.100.loads, ...), custom_call_target="tpu_custom_call" | custom-call | flops 402653184 | bytes 2786304 | tf_op jit(solution)/shard_map/near/pallas_call | solution.py:139
  52.5 1.0 %climb.12 = (bf16[80,512]{1,0:T(8,128)(2,1)S(1)}, bf16[512,512]{1,0:T(8,128)(2,1)S(1)}, f32[1,512]{1,0:T(1,128)S(1)}) custom-call(s32[7,512]{1,0:T(8,128)S(1)} %get-tuple-element.90.tree, bf16[80,512]{1,0:T(8,128)(2,1)S(1)} %get-tuple-element.120.own, bf16[80,512]{1,0:T(8,128)(2,1)S(1)} %collective-permute-done.9.sibling), custom_call_target="tpu_custom_call" | custom-call | flops 100663296 | bytes 178176 | tf_op jit(solution)/shard_map/climb/pallas_call | solution.py:139
  53.6 2.3 %near.12 = (f32[2,64,256]{2,1,0:T(8,128)S(1)}, f32[64,512]{1,0:T(8,128)S(1)}) custom-call(s32[16,16]{1,0:T(8,128)S(4)} %get-tuple-element.98.ids, bf16[48,256,32]{2,1,0:T(8,128)(2,1)S(1)} %get-tuple-element.130.lefts, bf16[16,32,256]{2,1,0:T(8,128)(2,1)S(1)} %get-tuple-element.99.rights, bf16[48,64,256]{2,1,0:T(8,128)(2,1)S(1)} %get-tuple-element.100.loads, ...), custom_call_target="tpu_custom_call" | custom-call | flops 402653184 | bytes 2786304 | tf_op jit(solution)/shard_map/near/pallas_call | solution.py:139
  55.9 2.1 %collective-permute-done.10.sibling = bf16[80,512]{1,0:T(8,128)(2,1)S(1)} collective-permute-done((bf16[80,512]{1,0:T(8,128)(2,1)S(1)}, bf16[80,512]{1,0:T(8,128)(2,1)S(1)}, u32[]{:S(2)}, u32[]{:S(2)}) %collective-permute-start.10) | collective-permute-done | bytes 81952 | tf_op jit(solution)/shard_map/ppermute | solution.py:279
  58.1 1.0 %climb.13 = (bf16[80,512]{1,0:T(8,128)(2,1)S(1)}, bf16[512,512]{1,0:T(8,128)(2,1)S(1)}, f32[1,512]{1,0:T(1,128)S(1)}) custom-call(s32[7,512]{1,0:T(8,128)S(1)} %get-tuple-element.90.tree, bf16[80,512]{1,0:T(8,128)(2,1)S(1)} %get-tuple-element.125.own, bf16[80,512]{1,0:T(8,128)(2,1)S(1)} %collective-permute-done.10.sibling), custom_call_target="tpu_custom_call" | custom-call | flops 100663296 | bytes 178176 | tf_op jit(solution)/shard_map/climb/pallas_call | solution.py:139
  59.0 3.2 %collective-permute-start.11 = (bf16[80,512]{1,0:T(8,128)(2,1)S(1)}, bf16[80,512]{1,0:T(8,128)(2,1)S(1)}, u32[]{:S(2)}, u32[]{:S(2)}) collective-permute-start(bf16[80,512]{1,0:T(8,128)(2,1)S(1)} %get-tuple-element.129.own), channel_id=1, source_target_pairs={{0,144},{1,145},{2,146},{3,147},{4,148},{5,149},{6,150},{7,151},{8... | collective-permute-start | bytes 245768 | tf_op jit(solution)/shard_map/ppermute | solution.py:279
  62.2 3.5 %near.13 = (f32[3,64,256]{2,1,0:T(8,128)S(1)}, f32[64,512]{1,0:T(8,128)S(1)}) custom-call(s32[16,16]{1,0:T(8,128)S(4)} %get-tuple-element.98.ids, bf16[48,256,32]{2,1,0:T(8,128)(2,1)S(1)} %get-tuple-element.130.lefts, bf16[16,32,256]{2,1,0:T(8,128)(2,1)S(1)} %get-tuple-element.99.rights, bf16[48,64,256]{2,1,0:T(8,128)(2,1)S(1)} %get-tuple-element.100.loads, ...), custom_call_target="tpu_custom_call" | custom-call | flops 603979776 | bytes 2786304 | tf_op jit(solution)/shard_map/near/pallas_call | solution.py:139
  65.8 3.2 %down.1 = f32[64,4096]{1,0:T(8,128)} custom-call(bf16[80,512]{1,0:T(8,128)(2,1)S(1)} %get-tuple-element.129.own, bf16[80,512]{1,0:T(8,128)(2,1)S(1)} %collective-permute-done.11.sibling, bf16[512,512]{1,0:T(8,128)(2,1)S(1)} %get-tuple-element.133.refs_0_, f32[1,512]{1,0:T(1,128)S(1)} %get-tuple-element.134.refs_1_, ...), custom_call_target="tpu_custom_call" | custom-call | flops 268435456 | bytes 10024960 | tf_op jit(solution)/shard_map/down/pallas_call | solution.py:139
  (18 shorter events, 3.8 us)
Async XLA Ops:
  0.0 20.7 %collective-permute-start.2 = (bf16[64,4096]{1,0:T(8,128)(2,1)}, bf16[64,4096]{1,0:T(8,128)(2,1)S(1)}, u32[]{:S(2)}, u32[]{:S(2)}) collective-permute-start(bf16[64,4096]{1,0:T(8,128)(2,1)} %charges_in.1), channel_id=1, source_target_pairs={{0,1},{1,2},{2,3},{3,4},{4,5},{5,6},{6,7},{7,8},{8,9},{9,10},{10,1... | collective-permute-start | bytes 1572872 | tf_op jit(solution)/shard_map/ppermute | solution.py:294
  0.0 20.7 %collective-permute-start.3 = (bf16[64,4096]{1,0:T(8,128)(2,1)}, bf16[64,4096]{1,0:T(8,128)(2,1)S(1)}, u32[]{:S(2)}, u32[]{:S(2)}) collective-permute-start(bf16[64,4096]{1,0:T(8,128)(2,1)} %charges_in.1), channel_id=1, source_target_pairs={{1,0},{2,1},{3,2},{4,3},{5,4},{6,5},{7,6},{8,7},{9,8},{10,9},{11,1... | collective-permute-start | bytes 1572872 | tf_op jit(solution)/shard_map/ppermute | solution.py:295
  6.6 14.1 %collective-permute-start = (bf16[16,4096]{1,0:T(8,128)(2,1)}, bf16[16,4096]{1,0:T(8,128)(2,1)S(1)}, u32[]{:S(2)}, u32[]{:S(2)}) collective-permute-start(bf16[16,4096]{1,0:T(8,128)(2,1)} %points_in.1), channel_id=1, source_target_pairs={{0,1},{1,2},{2,3},{3,4},{4,5},{5,6},{6,7},{7,8},{8,9},{9,10},{10,1... | collective-permute-start | bytes 393224 | tf_op jit(solution)/shard_map/ppermute | solution.py:292
  6.6 14.1 %collective-permute-start.1 = (bf16[16,4096]{1,0:T(8,128)(2,1)}, bf16[16,4096]{1,0:T(8,128)(2,1)S(1)}, u32[]{:S(2)}, u32[]{:S(2)}) collective-permute-start(bf16[16,4096]{1,0:T(8,128)(2,1)} %points_in.1), channel_id=1, source_target_pairs={{1,0},{2,1},{3,2},{4,3},{5,4},{6,5},{7,6},{8,7},{9,8},{10,9},{11,1... | collective-permute-start | bytes 393224 | tf_op jit(solution)/shard_map/ppermute | solution.py:293
  18.2 1.4 %collective-permute-start.4 = (bf16[80,512]{1,0:T(8,128)(2,1)S(1)}, bf16[80,512]{1,0:T(8,128)(2,1)S(1)}, u32[]{:S(2)}, u32[]{:S(2)}) collective-permute-start(bf16[80,512]{1,0:T(8,128)(2,1)S(1)} %get-tuple-element.91.own), channel_id=1, source_target_pairs={{0,1},{1,0},{2,3},{3,2},{4,5},{5,4},{6,7},{7,6},{8,9},{9,8},{10,11... | collective-permute-start | bytes 245768 | tf_op jit(solution)/shard_map/ppermute | solution.py:279
  20.6 4.6 %collective-permute-start.5 = (bf16[80,512]{1,0:T(8,128)(2,1)S(1)}, bf16[80,512]{1,0:T(8,128)(2,1)S(1)}, u32[]{:S(2)}, u32[]{:S(2)}) collective-permute-start(bf16[80,512]{1,0:T(8,128)(2,1)S(1)} %get-tuple-element.97.own), channel_id=1, source_target_pairs={{0,2},{1,3},{2,0},{3,1},{4,6},{5,7},{6,4},{7,5},{8,10},{9,11},{10,... | collective-permute-start | bytes 245768 | tf_op jit(solution)/shard_map/ppermute | solution.py:279
  26.1 5.9 %collective-permute-start.6 = (bf16[80,512]{1,0:T(8,128)(2,1)S(1)}, bf16[80,512]{1,0:T(8,128)(2,1)S(1)}, u32[]{:S(2)}, u32[]{:S(2)}) collective-permute-start(bf16[80,512]{1,0:T(8,128)(2,1)S(1)} %get-tuple-element.105.own), channel_id=1, source_target_pairs={{0,6},{1,7},{2,4},{3,5},{4,2},{5,3},{6,0},{7,1},{8,14},{9,15},{10,... | collective-permute-start | bytes 245768 | tf_op jit(solution)/shard_map/ppermute | solution.py:279
  33.0 4.5 %collective-permute-start.7 = (bf16[80,512]{1,0:T(8,128)(2,1)S(1)}, bf16[80,512]{1,0:T(8,128)(2,1)S(1)}, u32[]{:S(2)}, u32[]{:S(2)}) collective-permute-start(bf16[80,512]{1,0:T(8,128)(2,1)S(1)} %get-tuple-element.110.own), channel_id=1, source_target_pairs={{0,8},{1,9},{2,10},{3,11},{4,12},{5,13},{6,14},{7,15},{8,0},{9,1},... | collective-permute-start | bytes 245768 | tf_op jit(solution)/shard_map/ppermute | solution.py:279
  38.6 5.7 %collective-permute-start.8 = (bf16[80,512]{1,0:T(8,128)(2,1)S(1)}, bf16[80,512]{1,0:T(8,128)(2,1)S(1)}, u32[]{:S(2)}, u32[]{:S(2)}) collective-permute-start(bf16[80,512]{1,0:T(8,128)(2,1)S(1)} %get-tuple-element.115.own), channel_id=1, source_target_pairs={{0,16},{1,17},{2,18},{3,19},{4,20},{5,21},{6,22},{7,23},{8,24},{9,... | collective-permute-start | bytes 245768 | tf_op jit(solution)/shard_map/ppermute | solution.py:279
  45.3 7.3 %collective-permute-start.9 = (bf16[80,512]{1,0:T(8,128)(2,1)S(1)}, bf16[80,512]{1,0:T(8,128)(2,1)S(1)}, u32[]{:S(2)}, u32[]{:S(2)}) collective-permute-start(bf16[80,512]{1,0:T(8,128)(2,1)S(1)} %get-tuple-element.120.own), channel_id=1, source_target_pairs={{0,32},{1,33},{2,34},{3,35},{4,36},{5,37},{6,38},{7,39},{8,40},{9,... | collective-permute-start | bytes 245768 | tf_op jit(solution)/shard_map/ppermute | solution.py:279
  53.5 4.5 %collective-permute-start.10 = (bf16[80,512]{1,0:T(8,128)(2,1)S(1)}, bf16[80,512]{1,0:T(8,128)(2,1)S(1)}, u32[]{:S(2)}, u32[]{:S(2)}) collective-permute-start(bf16[80,512]{1,0:T(8,128)(2,1)S(1)} %get-tuple-element.125.own), channel_id=1, source_target_pairs={{0,96},{1,97},{2,98},{3,99},{4,100},{5,101},{6,102},{7,103},{8,104... | collective-permute-start | bytes 245768 | tf_op jit(solution)/shard_map/ppermute | solution.py:279
  59.0 6.8 %collective-permute-start.11 = (bf16[80,512]{1,0:T(8,128)(2,1)S(1)}, bf16[80,512]{1,0:T(8,128)(2,1)S(1)}, u32[]{:S(2)}, u32[]{:S(2)}) collective-permute-start(bf16[80,512]{1,0:T(8,128)(2,1)S(1)} %get-tuple-element.129.own), channel_id=1, source_target_pairs={{0,144},{1,145},{2,146},{3,147},{4,148},{5,149},{6,150},{7,151},{8... | collective-permute-start | bytes 245768 | tf_op jit(solution)/shard_map/ppermute | solution.py:279

commit v4 on v3

--- a/solution.py
+++ b/solution.py
@@ -166,10 +166,11 @@
     prepare(x, q, leaves, leaves, lefts, loads)
 
 
-def halo_kernel(before_x, after_x, before_q, after_q, lefts_in, loads_in, lefts, loads):
+def halo_kernel(near_x, far_x, near_q, far_q, lefts_in, loads_in, lefts, loads):
     leaves = lefts.shape[0] // 3
-    prepare(before_x, before_q, 0, leaves, lefts, loads)
-    prepare(after_x, after_q, 2 * leaves, leaves, lefts, loads)
+    odd = lax.axis_index(("outer", "inner")) & 1
+    prepare(near_x, near_q, 2 * leaves * (1 - odd), leaves, lefts, loads)
+    prepare(far_x, far_q, 2 * leaves * odd, leaves, lefts, loads)
 
 
 def near_part(start, count, shift, ids, lefts, rights, loads, out, held):
@@ -287,12 +288,12 @@
     leaves, turns = near_leaves.shape
     count = skel_device.shape[1]
     tree = jnp.transpose(skel_tree, (1, 0, 2))
-    ahead = [(i, (i + 1) % total) for i in range(total)]
-    back = [((i + 1) % total, i) for i in range(total)]
-    before_x = lax.ppermute(points, ring, ahead)
-    after_x = lax.ppermute(points, ring, back)
-    before_q = lax.ppermute(charges, ring, ahead)
-    after_q = lax.ppermute(charges, ring, back)
+    near_pairs = [(i, i ^ 1) for i in range(total)]
+    far_pairs = [(i, ((i + 1 ^ 1) - 1) % total) for i in range(total)]
+    far_x = lax.ppermute(points, ring, far_pairs)
+    far_q = lax.ppermute(charges, ring, far_pairs)
+    near_x = lax.ppermute(points, ring, near_pairs)
+    near_q = lax.ppermute(charges, ring, near_pairs)
 
     square = pltpu.VMEM((count, count), BF16)
     line = pltpu.VMEM((1, count), F32)
@@ -342,7 +343,7 @@
                 lefts, loads = call(
                     halo_kernel,
                     sources_out,
-                    (before_x, after_x, before_q, after_q, lefts, loads),
+                    (near_x, far_x, near_q, far_q, lefts, loads),
                     "halo",
                     aliases={4: 0, 5: 1},
                     flops=10**9,

time: 70.6 us -> 64.7 us (0.916)
  starting transfers between devices: 21.9 us -> 17.9 us
  waiting for transfers between devices: 12.1 us -> 10.5 us
    ppermute x4, starting transfers between devices: 13.1 us -> 8.02 us  [the longest x1 7.16 us: body(): far_q = lax.ppermute(charges, ring, far_pairs)]
    ppermute x8, waiting for transfers between devices: 12.1 us -> 10.5 us  [swapped(): lax.ppermute(node, ('outer', 'inner'), [(i, i ^ mask) for i in range(tota...]
    ppermute x8, starting transfers between devices: 8.78 us -> 9.89 us  [swapped(): lax.ppermute(node, ('outer', 'inner'), [(i, i ^ mask) for i in range(tota...]
  transfers between devices with their start and end apart: 12 -> 12, of which waited for: 7 -> 8; matrix products, arithmetic and copies ran while one was open for 0% -> 0% of each run, Pallas kernels for 37% -> 41%
where the time goes in v4:
time: 64.7 us; the launch traced here: 63.5 us
  Pallas kernels  34.8 us (54%)
  starting transfers between devices  17.9 us (28%)
  waiting for transfers between devices  10.5 us (16%)
    pallas_call x18, Pallas kernels, call(): pl.pallas_call(kernel, out_shape=[pltpu.SMEM(s, t) if out_spaces.get(i) i...  34.8 us
    ppermute x8, waiting for transfers between devices, swapped(): lax.ppermute(node, ('outer', 'inner'), [(i, i ^ mask) for i in range(tota...  10.5 us
    ppermute x8, starting transfers between devices, swapped(): lax.ppermute(node, ('outer', 'inner'), [(i, i ^ mask) for i in range(tota...  9.89 us
    ppermute x1, starting transfers between devices, body(): far_q = lax.ppermute(charges, ring, far_pairs)  7.16 us
  transfers between devices with their start and end apart: 12, of which 8 were waited for; matrix products, arithmetic and copies ran while one was open for 0% of the time, Pallas kernels for 41%

profile of v4, /device:TPU:2, one launch (start us, length us, event | category | flops | bytes accessed | tf_op | source)
XLA Modules:
  0.0 63.5 jit_solution(1709639791319417840)
XLA Ops:
  0.0 7.2 %collective-permute-start.3 = (bf16[64,4096]{1,0:T(8,128)(2,1)}, bf16[64,4096]{1,0:T(8,128)(2,1)S(1)}, u32[]{:S(2)}, u32[]{:S(2)}) collective-permute-start(bf16[64,4096]{1,0:T(8,128)(2,1)} %charges_in.1), channel_id=1, source_target_pairs={{0,255},{1,2},{2,1},{3,4},{4,3},{5,6},{6,5},{7,8},{8,7},{9,10},{10... | collective-permute-start | bytes 1572872 | tf_op jit(solution)/shard_map/ppermute | solution.py:294
  8.0 5.1 %base.1 = (bf16[80,512]{1,0:T(8,128)(2,1)S(1)}, bf16[512,4096]{1,0:T(8,128)(2,1)S(1)}, f32[1,4096]{1,0:T(1,128)S(1)}, bf16[16,4096]{1,0:T(8,128)(2,1)S(1)}, bf16...) custom-call(bf16[16,4096]{1,0:T(8,128)(2,1)} %points_in.1, ...), custom_call_target="tpu_custom_call" | custom-call | flops 402653184 | bytes 672768 | tf_op jit(solution)/shard_map/base/pallas_call | solution.py:139
  14.5 1.0 %climb.7 = (bf16[80,512]{1,0:T(8,128)(2,1)S(1)}, bf16[512,512]{1,0:T(8,128)(2,1)S(1)}, f32[1,512]{1,0:T(1,128)S(1)}) custom-call(s32[7,512]{1,0:T(8,128)S(1)} %get-tuple-element.90.tree, bf16[80,512]{1,0:T(8,128)(2,1)S(1)} %get-tuple-element.91.own, bf16[80,512]{1,0:T(8,128)(2,1)S(1)} %collective-permute-done.4.sibling), custom_call_target="tpu_custom_call" | custom-call | flops 100663296 | bytes 178176 | tf_op jit(solution)/shard_map/climb/pallas_call | solution.py:139
  15.5 1.4 %collective-permute-start.5 = (bf16[80,512]{1,0:T(8,128)(2,1)S(1)}, bf16[80,512]{1,0:T(8,128)(2,1)S(1)}, u32[]{:S(2)}, u32[]{:S(2)}) collective-permute-start(bf16[80,512]{1,0:T(8,128)(2,1)S(1)} %get-tuple-element.97.own), channel_id=1, source_target_pairs={{0,2},{1,3},{2,0},{3,1},{4,6},{5,7},{6,4},{7,5},{8,10},{9,11},{10,... | collective-permute-start | bytes 245768 | tf_op jit(solution)/shard_map/ppermute | solution.py:280
  17.6 2.3 %near.7 = (f32[2,64,256]{2,1,0:T(8,128)S(1)}, f32[64,512]{1,0:T(8,128)S(1)}) custom-call(s32[16,16]{1,0:T(8,128)S(4)} %get-tuple-element.98.ids, bf16[48,256,32]{2,1,0:T(8,128)(2,1)S(1)} %get-tuple-element.130.lefts, bf16[16,32,256]{2,1,0:T(8,128)(2,1)S(1)} %get-tuple-element.99.rights, bf16[48,64,256]{2,1,0:T(8,128)(2,1)S(1)} %get-tuple-element.100.loads, ...), custom_call_target="tpu_custom_call" | custom-call | flops 402653184 | bytes 2786304 | tf_op jit(solution)/shard_map/near/pallas_call | solution.py:139
  20.1 1.0 %climb.8 = (bf16[80,512]{1,0:T(8,128)(2,1)S(1)}, bf16[512,512]{1,0:T(8,128)(2,1)S(1)}, f32[1,512]{1,0:T(1,128)S(1)}) custom-call(s32[7,512]{1,0:T(8,128)S(1)} %get-tuple-element.90.tree, bf16[80,512]{1,0:T(8,128)(2,1)S(1)} %get-tuple-element.97.own, bf16[80,512]{1,0:T(8,128)(2,1)S(1)} %collective-permute-done.5.sibling), custom_call_target="tpu_custom_call" | custom-call | flops 100663296 | bytes 178176 | tf_op jit(solution)/shard_map/climb/pallas_call | solution.py:139
  21.3 2.3 %near.8 = (f32[2,64,256]{2,1,0:T(8,128)S(1)}, f32[64,512]{1,0:T(8,128)S(1)}) custom-call(s32[16,16]{1,0:T(8,128)S(4)} %get-tuple-element.98.ids, bf16[48,256,32]{2,1,0:T(8,128)(2,1)S(1)} %get-tuple-element.130.lefts, bf16[16,32,256]{2,1,0:T(8,128)(2,1)S(1)} %get-tuple-element.99.rights, bf16[48,64,256]{2,1,0:T(8,128)(2,1)S(1)} %get-tuple-element.100.loads, ...), custom_call_target="tpu_custom_call" | custom-call | flops 402653184 | bytes 2786304 | tf_op jit(solution)/shard_map/near/pallas_call | solution.py:139
  23.6 3.3 %collective-permute-done.6.sibling = bf16[80,512]{1,0:T(8,128)(2,1)S(1)} collective-permute-done((bf16[80,512]{1,0:T(8,128)(2,1)S(1)}, bf16[80,512]{1,0:T(8,128)(2,1)S(1)}, u32[]{:S(2)}, u32[]{:S(2)}) %collective-permute-start.6) | collective-permute-done | bytes 81952 | tf_op jit(solution)/shard_map/ppermute | solution.py:280
  27.0 1.0 %climb.9 = (bf16[80,512]{1,0:T(8,128)(2,1)S(1)}, bf16[512,512]{1,0:T(8,128)(2,1)S(1)}, f32[1,512]{1,0:T(1,128)S(1)}) custom-call(s32[7,512]{1,0:T(8,128)S(1)} %get-tuple-element.90.tree, bf16[80,512]{1,0:T(8,128)(2,1)S(1)} %get-tuple-element.105.own, bf16[80,512]{1,0:T(8,128)(2,1)S(1)} %collective-permute-done.6.sibling), custom_call_target="tpu_custom_call" | custom-call | flops 100663296 | bytes 178176 | tf_op jit(solution)/shard_map/climb/pallas_call | solution.py:139
  28.0 2.3 %near.9 = (f32[2,64,256]{2,1,0:T(8,128)S(1)}, f32[64,512]{1,0:T(8,128)S(1)}) custom-call(s32[16,16]{1,0:T(8,128)S(4)} %get-tuple-element.98.ids, bf16[48,256,32]{2,1,0:T(8,128)(2,1)S(1)} %get-tuple-element.130.lefts, bf16[16,32,256]{2,1,0:T(8,128)(2,1)S(1)} %get-tuple-element.99.rights, bf16[48,64,256]{2,1,0:T(8,128)(2,1)S(1)} %get-tuple-element.100.loads, ...), custom_call_target="tpu_custom_call" | custom-call | flops 402653184 | bytes 2786304 | tf_op jit(solution)/shard_map/near/pallas_call | solution.py:139
  30.4 2.1 %collective-permute-done.7.sibling = bf16[80,512]{1,0:T(8,128)(2,1)S(1)} collective-permute-done((bf16[80,512]{1,0:T(8,128)(2,1)S(1)}, bf16[80,512]{1,0:T(8,128)(2,1)S(1)}, u32[]{:S(2)}, u32[]{:S(2)}) %collective-permute-start.7) | collective-permute-done | bytes 81952 | tf_op jit(solution)/shard_map/ppermute | solution.py:280
  32.5 1.0 %climb.10 = (bf16[80,512]{1,0:T(8,128)(2,1)S(1)}, bf16[512,512]{1,0:T(8,128)(2,1)S(1)}, f32[1,512]{1,0:T(1,128)S(1)}) custom-call(s32[7,512]{1,0:T(8,128)S(1)} %get-tuple-element.90.tree, bf16[80,512]{1,0:T(8,128)(2,1)S(1)} %get-tuple-element.110.own, bf16[80,512]{1,0:T(8,128)(2,1)S(1)} %collective-permute-done.7.sibling), custom_call_target="tpu_custom_call" | custom-call | flops 100663296 | bytes 178176 | tf_op jit(solution)/shard_map/climb/pallas_call | solution.py:139
  33.4 1.9 %collective-permute-start.8 = (bf16[80,512]{1,0:T(8,128)(2,1)S(1)}, bf16[80,512]{1,0:T(8,128)(2,1)S(1)}, u32[]{:S(2)}, u32[]{:S(2)}) collective-permute-start(bf16[80,512]{1,0:T(8,128)(2,1)S(1)} %get-tuple-element.115.own), channel_id=1, source_target_pairs={{0,16},{1,17},{2,18},{3,19},{4,20},{5,21},{6,22},{7,23},{8,24},{9,... | collective-permute-start | bytes 245768 | tf_op jit(solution)/shard_map/ppermute | solution.py:280
  35.4 3.5 %near.10 = (f32[3,64,256]{2,1,0:T(8,128)S(1)}, f32[64,512]{1,0:T(8,128)S(1)}) custom-call(s32[16,16]{1,0:T(8,128)S(4)} %get-tuple-element.98.ids, bf16[48,256,32]{2,1,0:T(8,128)(2,1)S(1)} %get-tuple-element.130.lefts, bf16[16,32,256]{2,1,0:T(8,128)(2,1)S(1)} %get-tuple-element.99.rights, bf16[48,64,256]{2,1,0:T(8,128)(2,1)S(1)} %get-tuple-element.100.loads, ...), custom_call_target="tpu_custom_call" | custom-call | flops 603979776 | bytes 2786304 | tf_op jit(solution)/shard_map/near/pallas_call | solution.py:139
  39.8 1.0 %climb.11 = (bf16[80,512]{1,0:T(8,128)(2,1)S(1)}, bf16[512,512]{1,0:T(8,128)(2,1)S(1)}, f32[1,512]{1,0:T(1,128)S(1)}) custom-call(s32[7,512]{1,0:T(8,128)S(1)} %get-tuple-element.90.tree, bf16[80,512]{1,0:T(8,128)(2,1)S(1)} %get-tuple-element.115.own, bf16[80,512]{1,0:T(8,128)(2,1)S(1)} %collective-permute-done.8.sibling), custom_call_target="tpu_custom_call" | custom-call | flops 100663296 | bytes 178176 | tf_op jit(solution)/shard_map/climb/pallas_call | solution.py:139
  40.7 3.9 %collective-permute-start.9 = (bf16[80,512]{1,0:T(8,128)(2,1)S(1)}, bf16[80,512]{1,0:T(8,128)(2,1)S(1)}, u32[]{:S(2)}, u32[]{:S(2)}) collective-permute-start(bf16[80,512]{1,0:T(8,128)(2,1)S(1)} %get-tuple-element.120.own), channel_id=1, source_target_pairs={{0,32},{1,33},{2,34},{3,35},{4,36},{5,37},{6,38},{7,39},{8,40},{9,... | collective-permute-start | bytes 245768 | tf_op jit(solution)/shard_map/ppermute | solution.py:280
  44.6 2.3 %near.11 = (f32[2,64,256]{2,1,0:T(8,128)S(1)}, f32[64,512]{1,0:T(8,128)S(1)}) custom-call(s32[16,16]{1,0:T(8,128)S(4)} %get-tuple-element.98.ids, bf16[48,256,32]{2,1,0:T(8,128)(2,1)S(1)} %get-tuple-element.130.lefts, bf16[16,32,256]{2,1,0:T(8,128)(2,1)S(1)} %get-tuple-element.99.rights, bf16[48,64,256]{2,1,0:T(8,128)(2,1)S(1)} %get-tuple-element.100.loads, ...), custom_call_target="tpu_custom_call" | custom-call | flops 402653184 | bytes 2786304 | tf_op jit(solution)/shard_map/near/pallas_call | solution.py:139
  47.0 1.0 %climb.12 = (bf16[80,512]{1,0:T(8,128)(2,1)S(1)}, bf16[512,512]{1,0:T(8,128)(2,1)S(1)}, f32[1,512]{1,0:T(1,128)S(1)}) custom-call(s32[7,512]{1,0:T(8,128)S(1)} %get-tuple-element.90.tree, bf16[80,512]{1,0:T(8,128)(2,1)S(1)} %get-tuple-element.120.own, bf16[80,512]{1,0:T(8,128)(2,1)S(1)} %collective-permute-done.9.sibling), custom_call_target="tpu_custom_call" | custom-call | flops 100663296 | bytes 178176 | tf_op jit(solution)/shard_map/climb/pallas_call | solution.py:139
  48.1 2.3 %near.12 = (f32[2,64,256]{2,1,0:T(8,128)S(1)}, f32[64,512]{1,0:T(8,128)S(1)}) custom-call(s32[16,16]{1,0:T(8,128)S(4)} %get-tuple-element.98.ids, bf16[48,256,32]{2,1,0:T(8,128)(2,1)S(1)} %get-tuple-element.130.lefts, bf16[16,32,256]{2,1,0:T(8,128)(2,1)S(1)} %get-tuple-element.99.rights, bf16[48,64,256]{2,1,0:T(8,128)(2,1)S(1)} %get-tuple-element.100.loads, ...), custom_call_target="tpu_custom_call" | custom-call | flops 402653184 | bytes 2786304 | tf_op jit(solution)/shard_map/near/pallas_call | solution.py:139
  50.4 2.1 %collective-permute-done.10.sibling = bf16[80,512]{1,0:T(8,128)(2,1)S(1)} collective-permute-done((bf16[80,512]{1,0:T(8,128)(2,1)S(1)}, bf16[80,512]{1,0:T(8,128)(2,1)S(1)}, u32[]{:S(2)}, u32[]{:S(2)}) %collective-permute-start.10) | collective-permute-done | bytes 81952 | tf_op jit(solution)/shard_map/ppermute | solution.py:280
  52.5 1.0 %climb.13 = (bf16[80,512]{1,0:T(8,128)(2,1)S(1)}, bf16[512,512]{1,0:T(8,128)(2,1)S(1)}, f32[1,512]{1,0:T(1,128)S(1)}) custom-call(s32[7,512]{1,0:T(8,128)S(1)} %get-tuple-element.90.tree, bf16[80,512]{1,0:T(8,128)(2,1)S(1)} %get-tuple-element.125.own, bf16[80,512]{1,0:T(8,128)(2,1)S(1)} %collective-permute-done.10.sibling), custom_call_target="tpu_custom_call" | custom-call | flops 100663296 | bytes 178176 | tf_op jit(solution)/shard_map/climb/pallas_call | solution.py:139
  53.5 2.2 %collective-permute-start.11 = (bf16[80,512]{1,0:T(8,128)(2,1)S(1)}, bf16[80,512]{1,0:T(8,128)(2,1)S(1)}, u32[]{:S(2)}, u32[]{:S(2)}) collective-permute-start(bf16[80,512]{1,0:T(8,128)(2,1)S(1)} %get-tuple-element.129.own), channel_id=1, source_target_pairs={{0,144},{1,145},{2,146},{3,147},{4,148},{5,149},{6,150},{7,151},{8... | collective-permute-start | bytes 245768 | tf_op jit(solution)/shard_map/ppermute | solution.py:280
  55.7 3.5 %near.13 = (f32[3,64,256]{2,1,0:T(8,128)S(1)}, f32[64,512]{1,0:T(8,128)S(1)}) custom-call(s32[16,16]{1,0:T(8,128)S(4)} %get-tuple-element.98.ids, bf16[48,256,32]{2,1,0:T(8,128)(2,1)S(1)} %get-tuple-element.130.lefts, bf16[16,32,256]{2,1,0:T(8,128)(2,1)S(1)} %get-tuple-element.99.rights, bf16[48,64,256]{2,1,0:T(8,128)(2,1)S(1)} %get-tuple-element.100.loads, ...), custom_call_target="tpu_custom_call" | custom-call | flops 603979776 | bytes 2786304 | tf_op jit(solution)/shard_map/near/pallas_call | solution.py:139
  60.2 3.2 %down.1 = f32[64,4096]{1,0:T(8,128)} custom-call(bf16[80,512]{1,0:T(8,128)(2,1)S(1)} %get-tuple-element.129.own, bf16[80,512]{1,0:T(8,128)(2,1)S(1)} %collective-permute-done.11.sibling, bf16[512,512]{1,0:T(8,128)(2,1)S(1)} %get-tuple-element.133.refs_0_, f32[1,512]{1,0:T(1,128)S(1)} %get-tuple-element.134.refs_1_, ...), custom_call_target="tpu_custom_call" | custom-call | flops 268435456 | bytes 10024960 | tf_op jit(solution)/shard_map/down/pallas_call | solution.py:139
  (18 shorter events, 5.4 us)
Async XLA Ops:
  0.0 16.9 %collective-permute-start.2 = (bf16[64,4096]{1,0:T(8,128)(2,1)}, bf16[64,4096]{1,0:T(8,128)(2,1)S(1)}, u32[]{:S(2)}, u32[]{:S(2)}) collective-permute-start(bf16[64,4096]{1,0:T(8,128)(2,1)} %charges_in.1), channel_id=1, source_target_pairs={{0,1},{1,0},{2,3},{3,2},{4,5},{5,4},{6,7},{7,6},{8,9},{9,8},{10,11... | collective-permute-start | bytes 1572872 | tf_op jit(solution)/shard_map/ppermute | solution.py:296
  0.0 16.9 %collective-permute-start.3 = (bf16[64,4096]{1,0:T(8,128)(2,1)}, bf16[64,4096]{1,0:T(8,128)(2,1)S(1)}, u32[]{:S(2)}, u32[]{:S(2)}) collective-permute-start(bf16[64,4096]{1,0:T(8,128)(2,1)} %charges_in.1), channel_id=1, source_target_pairs={{0,255},{1,2},{2,1},{3,4},{4,3},{5,6},{6,5},{7,8},{8,7},{9,10},{10... | collective-permute-start | bytes 1572872 | tf_op jit(solution)/shard_map/ppermute | solution.py:294
  7.2 9.7 %collective-permute-start = (bf16[16,4096]{1,0:T(8,128)(2,1)}, bf16[16,4096]{1,0:T(8,128)(2,1)S(1)}, u32[]{:S(2)}, u32[]{:S(2)}) collective-permute-start(bf16[16,4096]{1,0:T(8,128)(2,1)} %points_in.1), channel_id=1, source_target_pairs={{0,1},{1,0},{2,3},{3,2},{4,5},{5,4},{6,7},{7,6},{8,9},{9,8},{10,11... | collective-permute-start | bytes 393224 | tf_op jit(solution)/shard_map/ppermute | solution.py:295
  7.2 9.7 %collective-permute-start.1 = (bf16[16,4096]{1,0:T(8,128)(2,1)}, bf16[16,4096]{1,0:T(8,128)(2,1)S(1)}, u32[]{:S(2)}, u32[]{:S(2)}) collective-permute-start(bf16[16,4096]{1,0:T(8,128)(2,1)} %points_in.1), channel_id=1, source_target_pairs={{0,255},{1,2},{2,1},{3,4},{4,3},{5,6},{6,5},{7,8},{8,7},{9,10},{10... | collective-permute-start | bytes 393224 | tf_op jit(solution)/shard_map/ppermute | solution.py:293
  13.1 1.4 %collective-permute-start.4 = (bf16[80,512]{1,0:T(8,128)(2,1)S(1)}, bf16[80,512]{1,0:T(8,128)(2,1)S(1)}, u32[]{:S(2)}, u32[]{:S(2)}) collective-permute-start(bf16[80,512]{1,0:T(8,128)(2,1)S(1)} %get-tuple-element.91.own), channel_id=1, source_target_pairs={{0,1},{1,0},{2,3},{3,2},{4,5},{5,4},{6,7},{7,6},{8,9},{9,8},{10,11... | collective-permute-start | bytes 245768 | tf_op jit(solution)/shard_map/ppermute | solution.py:280
  15.5 4.6 %collective-permute-start.5 = (bf16[80,512]{1,0:T(8,128)(2,1)S(1)}, bf16[80,512]{1,0:T(8,128)(2,1)S(1)}, u32[]{:S(2)}, u32[]{:S(2)}) collective-permute-start(bf16[80,512]{1,0:T(8,128)(2,1)S(1)} %get-tuple-element.97.own), channel_id=1, source_target_pairs={{0,2},{1,3},{2,0},{3,1},{4,6},{5,7},{6,4},{7,5},{8,10},{9,11},{10,... | collective-permute-start | bytes 245768 | tf_op jit(solution)/shard_map/ppermute | solution.py:280
  21.0 5.9 %collective-permute-start.6 = (bf16[80,512]{1,0:T(8,128)(2,1)S(1)}, bf16[80,512]{1,0:T(8,128)(2,1)S(1)}, u32[]{:S(2)}, u32[]{:S(2)}) collective-permute-start(bf16[80,512]{1,0:T(8,128)(2,1)S(1)} %get-tuple-element.105.own), channel_id=1, source_target_pairs={{0,6},{1,7},{2,4},{3,5},{4,2},{5,3},{6,0},{7,1},{8,14},{9,15},{10,... | collective-permute-start | bytes 245768 | tf_op jit(solution)/shard_map/ppermute | solution.py:280
  27.9 4.5 %collective-permute-start.7 = (bf16[80,512]{1,0:T(8,128)(2,1)S(1)}, bf16[80,512]{1,0:T(8,128)(2,1)S(1)}, u32[]{:S(2)}, u32[]{:S(2)}) collective-permute-start(bf16[80,512]{1,0:T(8,128)(2,1)S(1)} %get-tuple-element.110.own), channel_id=1, source_target_pairs={{0,8},{1,9},{2,10},{3,11},{4,12},{5,13},{6,14},{7,15},{8,0},{9,1},... | collective-permute-start | bytes 245768 | tf_op jit(solution)/shard_map/ppermute | solution.py:280
  33.4 6.3 %collective-permute-start.8 = (bf16[80,512]{1,0:T(8,128)(2,1)S(1)}, bf16[80,512]{1,0:T(8,128)(2,1)S(1)}, u32[]{:S(2)}, u32[]{:S(2)}) collective-permute-start(bf16[80,512]{1,0:T(8,128)(2,1)S(1)} %get-tuple-element.115.own), channel_id=1, source_target_pairs={{0,16},{1,17},{2,18},{3,19},{4,20},{5,21},{6,22},{7,23},{8,24},{9,... | collective-permute-start | bytes 245768 | tf_op jit(solution)/shard_map/ppermute | solution.py:280
  40.7 6.3 %collective-permute-start.9 = (bf16[80,512]{1,0:T(8,128)(2,1)S(1)}, bf16[80,512]{1,0:T(8,128)(2,1)S(1)}, u32[]{:S(2)}, u32[]{:S(2)}) collective-permute-start(bf16[80,512]{1,0:T(8,128)(2,1)S(1)} %get-tuple-element.120.own), channel_id=1, source_target_pairs={{0,32},{1,33},{2,34},{3,35},{4,36},{5,37},{6,38},{7,39},{8,40},{9,... | collective-permute-start | bytes 245768 | tf_op jit(solution)/shard_map/ppermute | solution.py:280
  48.0 4.5 %collective-permute-start.10 = (bf16[80,512]{1,0:T(8,128)(2,1)S(1)}, bf16[80,512]{1,0:T(8,128)(2,1)S(1)}, u32[]{:S(2)}, u32[]{:S(2)}) collective-permute-start(bf16[80,512]{1,0:T(8,128)(2,1)S(1)} %get-tuple-element.125.own), channel_id=1, source_target_pairs={{0,96},{1,97},{2,98},{3,99},{4,100},{5,101},{6,102},{7,103},{8,104... | collective-permute-start | bytes 245768 | tf_op jit(solution)/shard_map/ppermute | solution.py:280
  53.5 6.6 %collective-permute-start.11 = (bf16[80,512]{1,0:T(8,128)(2,1)S(1)}, bf16[80,512]{1,0:T(8,128)(2,1)S(1)}, u32[]{:S(2)}, u32[]{:S(2)}) collective-permute-start(bf16[80,512]{1,0:T(8,128)(2,1)S(1)} %get-tuple-element.129.own), channel_id=1, source_target_pairs={{0,144},{1,145},{2,146},{3,147},{4,148},{5,149},{6,150},{7,151},{8... | collective-permute-start | bytes 245768 | tf_op jit(solution)/shard_map/ppermute | solution.py:280

commit v5 on v4

--- a/solution.py
+++ b/solution.py
@@ -211,7 +211,7 @@
             held[top : top + LEAF, at : at + LEAF] = entries(
                 left[top : top + LEAF], right[:, at : at + LEAF]
             ).astype(BF16)
-    out[...] = dot(source[DIM:], held[...])
+    out[...] = dot(source[DIM : DIM + NRHS], held[...])
 
 
 def near_kernel(start, count, ids, lefts, rights, loads, own, sibling, out, side, held, square):
@@ -242,18 +242,42 @@
     left = left_rows(next_x)
     link(left, own[0:DIM], block, inverse)
     link(left, sibling[0:DIM], square, spare)
-    up = lifted(own[DIM:], block, inverse) + lifted(sibling[DIM:], square, spare)
+    up = lifted(own[DIM : DIM + NRHS], block, inverse) + lifted(
+        sibling[DIM : DIM + NRHS], square, spare
+    )
     node[0:DIM] = next_x.astype(BF16)
-    node[DIM:] = up.astype(BF16)
-
-
-def down_kernel(levels, own, sibling, *refs):
+    node[DIM : DIM + NRHS] = up.astype(BF16)
+    if node.shape[0] > DIM + NRHS:
+        index = tree[level + 1 : level + 2]
+        row = lax.broadcasted_iota(jnp.int32, (16, index.shape[1]), 0)
+        high = (index >> 5).astype(F32)
+        low = (index & 31).astype(F32)
+        node[DIM + NRHS :] = jnp.where(row == 0, high, jnp.where(row == 1, low, 0.0)).astype(BF16)
+
+
+def down_kernel(levels, tree, own, sibling, cousin, far_cousin, *refs):
     blocks = refs[0 : 3 * levels]
     base_block, base_inverse = refs[3 * levels : 3 * levels + 2]
-    nears = refs[3 * levels + 2 : -5]
-    out, square, side, made, sems = refs[-5:]
+    nears = refs[3 * levels + 2 : -9]
+    out, square, side, made, sems, spare, top_block, top_inverse, uncle = refs[-9:]
+    parent_x = pick(tiles_of(own[0:DIM]) + tiles_of(sibling[0:DIM]), tree[levels : levels + 1])
+    digits = cousin[DIM + NRHS :].astype(F32)
+    uncle_x = pick(
+        tiles_of(cousin[0:DIM]) + tiles_of(far_cousin[0:DIM]),
+        (digits[0:1] * 32.0 + digits[1:2]).astype(jnp.int32),
+    )
+    link(left_rows(parent_x), own[0:DIM], top_block, top_inverse)
+    left = left_rows(uncle_x)
+    link(left, cousin[0:DIM], square, spare)
+    up = lifted(cousin[DIM : DIM + NRHS], square, spare)
+    link(left, far_cousin[0:DIM], square, spare)
+    up = up + lifted(far_cousin[DIM : DIM + NRHS], square, spare)
+    uncle[0:DIM] = uncle_x.astype(BF16)
+    uncle[DIM:] = up.astype(BF16)
+    beside(uncle, parent_x, square, side)
+    downward = side[...].astype(BF16)
     beside(sibling, own[0:DIM], square, side)
-    downward = side[...].astype(BF16)
+    downward = (side[...] + dot(downward, top_block[...]) * top_inverse[...]).astype(BF16)
     for level in range(levels - 1, -1, -1):
         block, inverse, across = blocks[3 * level : 3 * level + 3]
         downward = (across[...] + dot(downward, block[...]) * inverse[...]).astype(BF16)
@@ -274,9 +298,11 @@
         write.wait()
 
 
-def swapped(node, bit):
+def swapped(node, *bits):
     total = lax.axis_size("inner") * lax.axis_size("outer")
-    mask = (1 << bit) | (REACH[bit] if bit < len(REACH) else 0)
+    mask = 0
+    for bit in bits:
+        mask |= (1 << bit) | (REACH[bit] if bit < len(REACH) else 0)
     return lax.ppermute(node, ("outer", "inner"), [(i, i ^ mask) for i in range(total)])
 
 
@@ -324,14 +350,20 @@
         out_spaces={7: pltpu.SMEM},
         flops=2 * width * count * (DEPTH + NRHS),
     )
-    chunks = [0] + [leaves * (i + 1) // (levels - 1) - leaves * i // (levels - 1) for i in range(levels - 1)]
+    rest = levels - 3
+    chunks = [0] + [2 + (i == 3) for i in range(rest)]
+    chunks.append(leaves - sum(chunks))
     sources_out = [((3 * leaves, LEAF, DEPTH), BF16), ((3 * leaves, NRHS, LEAF), BF16)]
     start = 0
     records = []
     nears = []
     pending = None
-    for level in range(levels):
+    for level in range(levels - 1):
+        last = level == levels - 2
         sibling = swapped(node, level)
+        if last:
+            cousin = swapped(node, level + 1)
+            far_cousin = swapped(node, level, level + 1)
         if level == 0:
             own_x, node = lax.optimization_barrier((own_x, node))
             lefts, loads = call(own_kernel, sources_out, (own_x, own_q), "own", flops=10**8)
@@ -358,13 +390,16 @@
                 flops=2 * chunk * LEAF * turns * LEAF * (DEPTH + NRHS),
             )
             start += chunk
+            if last:
+                part, cousin, far_cousin = lax.optimization_barrier((part, cousin, far_cousin))
             part, sibling = lax.optimization_barrier((part, sibling))
             nears.append(part)
             records[-1].append(side)
-        if level < levels - 1:
+        if not last:
+            extra = 16 if level == levels - 3 else 0
             following, block, inverse = call(
                 functools.partial(climb_kernel, level),
-                [node_out, *block_out],
+                [((DIM + NRHS + extra, count), BF16), *block_out],
                 (tree, node, sibling),
                 "climb",
                 [square, line],
@@ -375,15 +410,19 @@
             node = following
     kept = [array for record in records for array in record]
     [potential] = call(
-        functools.partial(down_kernel, levels - 1),
+        functools.partial(down_kernel, levels - 2),
         [((NRHS, width), F32)],
-        (node, sibling, *kept, base_block, base_inverse, *nears),
+        (tree, node, sibling, cousin, far_cousin, *kept, base_block, base_inverse, *nears),
         "down",
         [
             square,
             pltpu.VMEM(*side_out),
             pltpu.VMEM((NRHS, width), F32),
             pltpu.SemaphoreType.DMA((len(nears),)),
+            line,
+            square,
+            line,
+            pltpu.VMEM(*node_out),
         ],
         out_spaces={0: pl.ANY},
         flops=2 * width * count * NRHS,

time: 64.7 us -> 64.8 us (level)
  waiting for transfers between devices: 10.5 us -> 7.56 us
  starting transfers between devices: 17.9 us -> 20.8 us
    ppermute x8 -> x9, starting transfers between devices: 9.89 us -> 13.5 us  [swapped(): lax.ppermute(node, ('outer', 'inner'), [(i, i ^ mask) for i in range(tota...]
    ppermute x8 -> x9, waiting for transfers between devices: 10.5 us -> 7.55 us  [swapped(): lax.ppermute(node, ('outer', 'inner'), [(i, i ^ mask) for i in range(tota...]
    ppermute x1, starting transfers between devices: 7.16 us -> 6.49 us  [body(): far_q = lax.ppermute(charges, ring, far_pairs)]
    pallas_call x18 -> x16, Pallas kernels: 34.8 us -> 34.8 us  [call(): pl.pallas_call(kernel, out_shape=[pltpu.SMEM(s, t) if out_spaces.get(i) i...]
  transfers between devices with their start and end apart: 12 -> 13, of which waited for: 8 -> 6; matrix products, arithmetic and copies ran while one was open for 0% -> 0% of each run, Pallas kernels for 41% -> 40%
where the time goes in v5:
time: 64.8 us; the launch traced here: 63.5 us
  Pallas kernels  34.8 us (54%)
  starting transfers between devices  20.8 us (32%)
  waiting for transfers between devices  7.56 us (12%)
    pallas_call x16, Pallas kernels, call(): pl.pallas_call(kernel, out_shape=[pltpu.SMEM(s, t) if out_spaces.get(i) i...  34.8 us
    ppermute x9, starting transfers between devices, swapped(): lax.ppermute(node, ('outer', 'inner'), [(i, i ^ mask) for i in range(tota...  13.5 us
    ppermute x9, waiting for transfers between devices, swapped(): lax.ppermute(node, ('outer', 'inner'), [(i, i ^ mask) for i in range(tota...  7.55 us
    ppermute x1, starting transfers between devices, body(): far_q = lax.ppermute(charges, ring, far_pairs)  6.49 us
  transfers between devices with their start and end apart: 13, of which 6 were waited for; matrix products, arithmetic and copies ran while one was open for 0% of the time, Pallas kernels for 40%

profile of v5, /device:TPU:2, one launch (start us, length us, event | category | flops | bytes accessed | tf_op | source)
XLA Modules:
  0.0 63.5 jit_solution(7677824382520522119)
XLA Ops:
  0.0 6.5 %collective-permute-start.3 = (bf16[64,4096]{1,0:T(8,128)(2,1)}, bf16[64,4096]{1,0:T(8,128)(2,1)S(1)}, u32[]{:S(2)}, u32[]{:S(2)}) collective-permute-start(bf16[64,4096]{1,0:T(8,128)(2,1)} %charges_in.1), channel_id=1, source_target_pairs={{0,255},{1,2},{2,1},{3,4},{4,3},{5,6},{6,5},{7,8},{8,7},{9,10},{10... | collective-permute-start | bytes 1572872 | tf_op jit(solution)/shard_map/ppermute | solution.py:320
  6.5 0.9 %collective-permute-start.1 = (bf16[16,4096]{1,0:T(8,128)(2,1)}, bf16[16,4096]{1,0:T(8,128)(2,1)S(1)}, u32[]{:S(2)}, u32[]{:S(2)}) collective-permute-start(bf16[16,4096]{1,0:T(8,128)(2,1)} %points_in.1), channel_id=1, source_target_pairs={{0,255},{1,2},{2,1},{3,4},{4,3},{5,6},{6,5},{7,8},{8,7},{9,10},{10... | collective-permute-start | bytes 393224 | tf_op jit(solution)/shard_map/ppermute | solution.py:319
  7.3 5.1 %base.1 = (bf16[80,512]{1,0:T(8,128)(2,1)S(1)}, bf16[512,4096]{1,0:T(8,128)(2,1)S(1)}, f32[1,4096]{1,0:T(1,128)S(1)}, bf16[16,4096]{1,0:T(8,128)(2,1)S(1)}, bf16...) custom-call(bf16[16,4096]{1,0:T(8,128)(2,1)} %points_in.1, ...), custom_call_target="tpu_custom_call" | custom-call | flops 402653184 | bytes 672768 | tf_op jit(solution)/shard_map/base/pallas_call | solution.py:139
  14.0 1.0 %climb.6 = (bf16[80,512]{1,0:T(8,128)(2,1)S(1)}, bf16[512,512]{1,0:T(8,128)(2,1)S(1)}, f32[1,512]{1,0:T(1,128)S(1)}) custom-call(s32[7,512]{1,0:T(8,128)S(1)} %get-tuple-element.78.tree, bf16[80,512]{1,0:T(8,128)(2,1)S(1)} %get-tuple-element.85.own, bf16[80,512]{1,0:T(8,128)(2,1)S(1)} %collective-permute-done.4.sibling), custom_call_target="tpu_custom_call" | custom-call | flops 100663296 | bytes 178176 | tf_op jit(solution)/shard_map/climb/pallas_call | solution.py:139
  14.9 1.4 %collective-permute-start.5 = (bf16[80,512]{1,0:T(8,128)(2,1)S(1)}, bf16[80,512]{1,0:T(8,128)(2,1)S(1)}, u32[]{:S(2)}, u32[]{:S(2)}) collective-permute-start(bf16[80,512]{1,0:T(8,128)(2,1)S(1)} %get-tuple-element.91.own), channel_id=1, source_target_pairs={{0,2},{1,3},{2,0},{3,1},{4,6},{5,7},{6,4},{7,5},{8,10},{9,11},{10,... | collective-permute-start | bytes 245768 | tf_op jit(solution)/shard_map/ppermute | solution.py:306
  17.0 2.3 %near.6 = (f32[2,64,256]{2,1,0:T(8,128)S(1)}, f32[64,512]{1,0:T(8,128)S(1)}) custom-call(s32[16,16]{1,0:T(8,128)S(4)} %get-tuple-element.92.ids, bf16[48,256,32]{2,1,0:T(8,128)(2,1)S(1)} %get-tuple-element.119.lefts, bf16[16,32,256]{2,1,0:T(8,128)(2,1)S(1)} %get-tuple-element.93.rights, bf16[48,64,256]{2,1,0:T(8,128)(2,1)S(1)} %get-tuple-element.94.loads, ...), custom_call_target="tpu_custom_call" | custom-call | flops 402653184 | bytes 2786304 | tf_op jit(solution)/shard_map/near/pallas_call | solution.py:139
  19.7 1.0 %climb.7 = (bf16[80,512]{1,0:T(8,128)(2,1)S(1)}, bf16[512,512]{1,0:T(8,128)(2,1)S(1)}, f32[1,512]{1,0:T(1,128)S(1)}) custom-call(s32[7,512]{1,0:T(8,128)S(1)} %get-tuple-element.78.tree, bf16[80,512]{1,0:T(8,128)(2,1)S(1)} %get-tuple-element.91.own, bf16[80,512]{1,0:T(8,128)(2,1)S(1)} %collective-permute-done.5.sibling), custom_call_target="tpu_custom_call" | custom-call | flops 100663296 | bytes 178176 | tf_op jit(solution)/shard_map/climb/pallas_call | solution.py:139
  21.0 2.3 %near.7 = (f32[2,64,256]{2,1,0:T(8,128)S(1)}, f32[64,512]{1,0:T(8,128)S(1)}) custom-call(s32[16,16]{1,0:T(8,128)S(4)} %get-tuple-element.92.ids, bf16[48,256,32]{2,1,0:T(8,128)(2,1)S(1)} %get-tuple-element.119.lefts, bf16[16,32,256]{2,1,0:T(8,128)(2,1)S(1)} %get-tuple-element.93.rights, bf16[48,64,256]{2,1,0:T(8,128)(2,1)S(1)} %get-tuple-element.94.loads, ...), custom_call_target="tpu_custom_call" | custom-call | flops 402653184 | bytes 2786304 | tf_op jit(solution)/shard_map/near/pallas_call | solution.py:139
  23.3 3.3 %collective-permute-done.6.sibling = bf16[80,512]{1,0:T(8,128)(2,1)S(1)} collective-permute-done((bf16[80,512]{1,0:T(8,128)(2,1)S(1)}, bf16[80,512]{1,0:T(8,128)(2,1)S(1)}, u32[]{:S(2)}, u32[]{:S(2)}) %collective-permute-start.6) | collective-permute-done | bytes 81952 | tf_op jit(solution)/shard_map/ppermute | solution.py:306
  26.6 1.0 %climb.8 = (bf16[80,512]{1,0:T(8,128)(2,1)S(1)}, bf16[512,512]{1,0:T(8,128)(2,1)S(1)}, f32[1,512]{1,0:T(1,128)S(1)}) custom-call(s32[7,512]{1,0:T(8,128)S(1)} %get-tuple-element.78.tree, bf16[80,512]{1,0:T(8,128)(2,1)S(1)} %get-tuple-element.99.own, bf16[80,512]{1,0:T(8,128)(2,1)S(1)} %collective-permute-done.6.sibling), custom_call_target="tpu_custom_call" | custom-call | flops 100663296 | bytes 178176 | tf_op jit(solution)/shard_map/climb/pallas_call | solution.py:139
  27.7 2.3 %near.8 = (f32[2,64,256]{2,1,0:T(8,128)S(1)}, f32[64,512]{1,0:T(8,128)S(1)}) custom-call(s32[16,16]{1,0:T(8,128)S(4)} %get-tuple-element.92.ids, bf16[48,256,32]{2,1,0:T(8,128)(2,1)S(1)} %get-tuple-element.119.lefts, bf16[16,32,256]{2,1,0:T(8,128)(2,1)S(1)} %get-tuple-element.93.rights, bf16[48,64,256]{2,1,0:T(8,128)(2,1)S(1)} %get-tuple-element.94.loads, ...), custom_call_target="tpu_custom_call" | custom-call | flops 402653184 | bytes 2786304 | tf_op jit(solution)/shard_map/near/pallas_call | solution.py:139
  30.0 2.1 %collective-permute-done.7.sibling = bf16[80,512]{1,0:T(8,128)(2,1)S(1)} collective-permute-done((bf16[80,512]{1,0:T(8,128)(2,1)S(1)}, bf16[80,512]{1,0:T(8,128)(2,1)S(1)}, u32[]{:S(2)}, u32[]{:S(2)}) %collective-permute-start.7) | collective-permute-done | bytes 81952 | tf_op jit(solution)/shard_map/ppermute | solution.py:306
  32.1 1.0 %climb.9 = (bf16[80,512]{1,0:T(8,128)(2,1)S(1)}, bf16[512,512]{1,0:T(8,128)(2,1)S(1)}, f32[1,512]{1,0:T(1,128)S(1)}) custom-call(s32[7,512]{1,0:T(8,128)S(1)} %get-tuple-element.78.tree, bf16[80,512]{1,0:T(8,128)(2,1)S(1)} %get-tuple-element.104.own, bf16[80,512]{1,0:T(8,128)(2,1)S(1)} %collective-permute-done.7.sibling), custom_call_target="tpu_custom_call" | custom-call | flops 100663296 | bytes 178176 | tf_op jit(solution)/shard_map/climb/pallas_call | solution.py:139
  33.1 1.7 %collective-permute-start.8 = (bf16[80,512]{1,0:T(8,128)(2,1)S(1)}, bf16[80,512]{1,0:T(8,128)(2,1)S(1)}, u32[]{:S(2)}, u32[]{:S(2)}) collective-permute-start(bf16[80,512]{1,0:T(8,128)(2,1)S(1)} %get-tuple-element.109.own), channel_id=1, source_target_pairs={{0,16},{1,17},{2,18},{3,19},{4,20},{5,21},{6,22},{7,23},{8,24},{9,... | collective-permute-start | bytes 245768 | tf_op jit(solution)/shard_map/ppermute | solution.py:306
  34.8 3.5 %near.9 = (f32[3,64,256]{2,1,0:T(8,128)S(1)}, f32[64,512]{1,0:T(8,128)S(1)}) custom-call(s32[16,16]{1,0:T(8,128)S(4)} %get-tuple-element.92.ids, bf16[48,256,32]{2,1,0:T(8,128)(2,1)S(1)} %get-tuple-element.119.lefts, bf16[16,32,256]{2,1,0:T(8,128)(2,1)S(1)} %get-tuple-element.93.rights, bf16[48,64,256]{2,1,0:T(8,128)(2,1)S(1)} %get-tuple-element.94.loads, ...), custom_call_target="tpu_custom_call" | custom-call | flops 603979776 | bytes 2786304 | tf_op jit(solution)/shard_map/near/pallas_call | solution.py:139
  38.4 1.0 %collective-permute-done.8.sibling = bf16[80,512]{1,0:T(8,128)(2,1)S(1)} collective-permute-done((bf16[80,512]{1,0:T(8,128)(2,1)S(1)}, bf16[80,512]{1,0:T(8,128)(2,1)S(1)}, u32[]{:S(2)}, u32[]{:S(2)}) %collective-permute-start.8) | collective-permute-done | bytes 81952 | tf_op jit(solution)/shard_map/ppermute | solution.py:306
  39.4 1.0 %climb.10 = (bf16[80,512]{1,0:T(8,128)(2,1)S(1)}, bf16[512,512]{1,0:T(8,128)(2,1)S(1)}, f32[1,512]{1,0:T(1,128)S(1)}) custom-call(s32[7,512]{1,0:T(8,128)S(1)} %get-tuple-element.78.tree, bf16[80,512]{1,0:T(8,128)(2,1)S(1)} %get-tuple-element.109.own, bf16[80,512]{1,0:T(8,128)(2,1)S(1)} %collective-permute-done.8.sibling), custom_call_target="tpu_custom_call" | custom-call | flops 100663296 | bytes 178176 | tf_op jit(solution)/shard_map/climb/pallas_call | solution.py:139
  40.4 3.7 %collective-permute-start.9 = (bf16[80,512]{1,0:T(8,128)(2,1)S(1)}, bf16[80,512]{1,0:T(8,128)(2,1)S(1)}, u32[]{:S(2)}, u32[]{:S(2)}) collective-permute-start(bf16[80,512]{1,0:T(8,128)(2,1)S(1)} %get-tuple-element.114.own), channel_id=1, source_target_pairs={{0,32},{1,33},{2,34},{3,35},{4,36},{5,37},{6,38},{7,39},{8,40},{9,... | collective-permute-start | bytes 245768 | tf_op jit(solution)/shard_map/ppermute | solution.py:306
  44.1 2.3 %near.10 = (f32[2,64,256]{2,1,0:T(8,128)S(1)}, f32[64,512]{1,0:T(8,128)S(1)}) custom-call(s32[16,16]{1,0:T(8,128)S(4)} %get-tuple-element.92.ids, bf16[48,256,32]{2,1,0:T(8,128)(2,1)S(1)} %get-tuple-element.119.lefts, bf16[16,32,256]{2,1,0:T(8,128)(2,1)S(1)} %get-tuple-element.93.rights, bf16[48,64,256]{2,1,0:T(8,128)(2,1)S(1)} %get-tuple-element.94.loads, ...), custom_call_target="tpu_custom_call" | custom-call | flops 402653184 | bytes 2786304 | tf_op jit(solution)/shard_map/near/pallas_call | solution.py:139
  46.6 1.0 %climb.11 = (bf16[96,512]{1,0:T(8,128)(2,1)S(1)}, bf16[512,512]{1,0:T(8,128)(2,1)S(1)}, f32[1,512]{1,0:T(1,128)S(1)}) custom-call(s32[7,512]{1,0:T(8,128)S(1)} %get-tuple-element.78.tree, bf16[80,512]{1,0:T(8,128)(2,1)S(1)} %get-tuple-element.114.own, bf16[80,512]{1,0:T(8,128)(2,1)S(1)} %collective-permute-done.9.sibling), custom_call_target="tpu_custom_call" | custom-call | flops 100663296 | bytes 178176 | tf_op jit(solution)/shard_map/climb/pallas_call | solution.py:139
  47.5 3.9 %collective-permute-start.11 = (bf16[96,512]{1,0:T(8,128)(2,1)S(1)}, bf16[96,512]{1,0:T(8,128)(2,1)S(1)}, u32[]{:S(2)}, u32[]{:S(2)}) collective-permute-start(bf16[96,512]{1,0:T(8,128)(2,1)S(1)} %get-tuple-element.118.own), channel_id=1, source_target_pairs={{0,240},{1,241},{2,242},{3,243},{4,244},{5,245},{6,246},{7,247},{8... | collective-permute-start | bytes 294920 | tf_op jit(solution)/shard_map/ppermute | solution.py:306
  51.4 1.8 %collective-permute-start.12 = (bf16[96,512]{1,0:T(8,128)(2,1)S(1)}, bf16[96,512]{1,0:T(8,128)(2,1)S(1)}, u32[]{:S(2)}, u32[]{:S(2)}) collective-permute-start(bf16[96,512]{1,0:T(8,128)(2,1)S(1)} %get-tuple-element.118.own), channel_id=1, source_target_pairs={{0,96},{1,97},{2,98},{3,99},{4,100},{5,101},{6,102},{7,103},{8,104... | collective-permute-start | bytes 294920 | tf_op jit(solution)/shard_map/ppermute | solution.py:306
  53.2 5.5 %near.11 = (f32[5,64,256]{2,1,0:T(8,128)S(1)}, f32[64,512]{1,0:T(8,128)S(1)}) custom-call(s32[16,16]{1,0:T(8,128)S(4)} %get-tuple-element.92.ids, bf16[48,256,32]{2,1,0:T(8,128)(2,1)S(1)} %get-tuple-element.119.lefts, bf16[16,32,256]{2,1,0:T(8,128)(2,1)S(1)} %get-tuple-element.93.rights, bf16[48,64,256]{2,1,0:T(8,128)(2,1)S(1)} %get-tuple-element.94.loads, ...), custom_call_target="tpu_custom_call" | custom-call | flops 1006632960 | bytes 2786304 | tf_op jit(solution)/shard_map/near/pallas_call | solution.py:139
  58.8 4.5 %down.1 = f32[64,4096]{1,0:T(8,128)} custom-call(s32[7,512]{1,0:T(8,128)S(1)} %get-tuple-element.78.tree, bf16[96,512]{1,0:T(8,128)(2,1)S(1)} %get-tuple-element.118.own, bf16[96,512]{1,0:T(8,128)(2,1)S(1)} %collective-permute-done.12.sibling, bf16[96,512]{1,0:T(8,128)(2,1)S(1)} %collective-permute-done.10.cousin, ...), custom_call_target="tpu_custom_call" | custom-call | flops 268435456 | bytes 9611264 | tf_op jit(solution)/shard_map/down/pallas_call | solution.py:139
  (18 shorter events, 3.1 us)
Async XLA Ops:
  0.0 16.3 %collective-permute-start.3 = (bf16[64,4096]{1,0:T(8,128)(2,1)}, bf16[64,4096]{1,0:T(8,128)(2,1)S(1)}, u32[]{:S(2)}, u32[]{:S(2)}) collective-permute-start(bf16[64,4096]{1,0:T(8,128)(2,1)} %charges_in.1), channel_id=1, source_target_pairs={{0,255},{1,2},{2,1},{3,4},{4,3},{5,6},{6,5},{7,8},{8,7},{9,10},{10... | collective-permute-start | bytes 1572872 | tf_op jit(solution)/shard_map/ppermute | solution.py:320
  6.5 9.9 %collective-permute-start.2 = (bf16[64,4096]{1,0:T(8,128)(2,1)}, bf16[64,4096]{1,0:T(8,128)(2,1)S(1)}, u32[]{:S(2)}, u32[]{:S(2)}) collective-permute-start(bf16[64,4096]{1,0:T(8,128)(2,1)} %charges_in.1), channel_id=1, source_target_pairs={{0,1},{1,0},{2,3},{3,2},{4,5},{5,4},{6,7},{7,6},{8,9},{9,8},{10,11... | collective-permute-start | bytes 1572872 | tf_op jit(solution)/shard_map/ppermute | solution.py:322
  6.5 9.8 %collective-permute-start.1 = (bf16[16,4096]{1,0:T(8,128)(2,1)}, bf16[16,4096]{1,0:T(8,128)(2,1)S(1)}, u32[]{:S(2)}, u32[]{:S(2)}) collective-permute-start(bf16[16,4096]{1,0:T(8,128)(2,1)} %points_in.1), channel_id=1, source_target_pairs={{0,255},{1,2},{2,1},{3,4},{4,3},{5,6},{6,5},{7,8},{8,7},{9,10},{10... | collective-permute-start | bytes 393224 | tf_op jit(solution)/shard_map/ppermute | solution.py:319
  7.3 9.0 %collective-permute-start = (bf16[16,4096]{1,0:T(8,128)(2,1)}, bf16[16,4096]{1,0:T(8,128)(2,1)S(1)}, u32[]{:S(2)}, u32[]{:S(2)}) collective-permute-start(bf16[16,4096]{1,0:T(8,128)(2,1)} %points_in.1), channel_id=1, source_target_pairs={{0,1},{1,0},{2,3},{3,2},{4,5},{5,4},{6,7},{7,6},{8,9},{9,8},{10,11... | collective-permute-start | bytes 393224 | tf_op jit(solution)/shard_map/ppermute | solution.py:321
  12.5 1.5 %collective-permute-start.4 = (bf16[80,512]{1,0:T(8,128)(2,1)S(1)}, bf16[80,512]{1,0:T(8,128)(2,1)S(1)}, u32[]{:S(2)}, u32[]{:S(2)}) collective-permute-start(bf16[80,512]{1,0:T(8,128)(2,1)S(1)} %get-tuple-element.85.own), channel_id=1, source_target_pairs={{0,1},{1,0},{2,3},{3,2},{4,5},{5,4},{6,7},{7,6},{8,9},{9,8},{10,11... | collective-permute-start | bytes 245768 | tf_op jit(solution)/shard_map/ppermute | solution.py:306
  14.9 4.8 %collective-permute-start.5 = (bf16[80,512]{1,0:T(8,128)(2,1)S(1)}, bf16[80,512]{1,0:T(8,128)(2,1)S(1)}, u32[]{:S(2)}, u32[]{:S(2)}) collective-permute-start(bf16[80,512]{1,0:T(8,128)(2,1)S(1)} %get-tuple-element.91.own), channel_id=1, source_target_pairs={{0,2},{1,3},{2,0},{3,1},{4,6},{5,7},{6,4},{7,5},{8,10},{9,11},{10,... | collective-permute-start | bytes 245768 | tf_op jit(solution)/shard_map/ppermute | solution.py:306
  20.7 5.9 %collective-permute-start.6 = (bf16[80,512]{1,0:T(8,128)(2,1)S(1)}, bf16[80,512]{1,0:T(8,128)(2,1)S(1)}, u32[]{:S(2)}, u32[]{:S(2)}) collective-permute-start(bf16[80,512]{1,0:T(8,128)(2,1)S(1)} %get-tuple-element.99.own), channel_id=1, source_target_pairs={{0,6},{1,7},{2,4},{3,5},{4,2},{5,3},{6,0},{7,1},{8,14},{9,15},{10,... | collective-permute-start | bytes 245768 | tf_op jit(solution)/shard_map/ppermute | solution.py:306
  27.6 4.5 %collective-permute-start.7 = (bf16[80,512]{1,0:T(8,128)(2,1)S(1)}, bf16[80,512]{1,0:T(8,128)(2,1)S(1)}, u32[]{:S(2)}, u32[]{:S(2)}) collective-permute-start(bf16[80,512]{1,0:T(8,128)(2,1)S(1)} %get-tuple-element.104.own), channel_id=1, source_target_pairs={{0,8},{1,9},{2,10},{3,11},{4,12},{5,13},{6,14},{7,15},{8,0},{9,1},... | collective-permute-start | bytes 245768 | tf_op jit(solution)/shard_map/ppermute | solution.py:306
  33.1 6.3 %collective-permute-start.8 = (bf16[80,512]{1,0:T(8,128)(2,1)S(1)}, bf16[80,512]{1,0:T(8,128)(2,1)S(1)}, u32[]{:S(2)}, u32[]{:S(2)}) collective-permute-start(bf16[80,512]{1,0:T(8,128)(2,1)S(1)} %get-tuple-element.109.own), channel_id=1, source_target_pairs={{0,16},{1,17},{2,18},{3,19},{4,20},{5,21},{6,22},{7,23},{8,24},{9,... | collective-permute-start | bytes 245768 | tf_op jit(solution)/shard_map/ppermute | solution.py:306
  40.4 6.2 %collective-permute-start.9 = (bf16[80,512]{1,0:T(8,128)(2,1)S(1)}, bf16[80,512]{1,0:T(8,128)(2,1)S(1)}, u32[]{:S(2)}, u32[]{:S(2)}) collective-permute-start(bf16[80,512]{1,0:T(8,128)(2,1)S(1)} %get-tuple-element.114.own), channel_id=1, source_target_pairs={{0,32},{1,33},{2,34},{3,35},{4,36},{5,37},{6,38},{7,39},{8,40},{9,... | collective-permute-start | bytes 245768 | tf_op jit(solution)/shard_map/ppermute | solution.py:306
  47.5 11.2 %collective-permute-start.11 = (bf16[96,512]{1,0:T(8,128)(2,1)S(1)}, bf16[96,512]{1,0:T(8,128)(2,1)S(1)}, u32[]{:S(2)}, u32[]{:S(2)}) collective-permute-start(bf16[96,512]{1,0:T(8,128)(2,1)S(1)} %get-tuple-element.118.own), channel_id=1, source_target_pairs={{0,240},{1,241},{2,242},{3,243},{4,244},{5,245},{6,246},{7,247},{8... | collective-permute-start | bytes 294920 | tf_op jit(solution)/shard_map/ppermute | solution.py:306
  51.4 7.4 %collective-permute-start.10 = (bf16[96,512]{1,0:T(8,128)(2,1)S(1)}, bf16[96,512]{1,0:T(8,128)(2,1)S(1)}, u32[]{:S(2)}, u32[]{:S(2)}) collective-permute-start(bf16[96,512]{1,0:T(8,128)(2,1)S(1)} %get-tuple-element.118.own), channel_id=1, source_target_pairs={{0,144},{1,145},{2,146},{3,147},{4,148},{5,149},{6,150},{7,151},{8... | collective-permute-start | bytes 294920 | tf_op jit(solution)/shard_map/ppermute | solution.py:306
  51.4 7.4 %collective-permute-start.12 = (bf16[96,512]{1,0:T(8,128)(2,1)S(1)}, bf16[96,512]{1,0:T(8,128)(2,1)S(1)}, u32[]{:S(2)}, u32[]{:S(2)}) collective-permute-start(bf16[96,512]{1,0:T(8,128)(2,1)S(1)} %get-tuple-element.118.own), channel_id=1, source_target_pairs={{0,96},{1,97},{2,98},{3,99},{4,100},{5,101},{6,102},{7,103},{8,104... | collective-permute-start | bytes 294920 | tf_op jit(solution)/shard_map/ppermute | solution.py:306
